TPU v7x, 512 devices: a whole 4x8x8 slice. The times are simulated.
512 devices in a mesh: req: 32 (over z, x), prefix: 16 (over y, core).
Axes of the slice: x: 4, y: 8, z: 8, core: 2. Of those that a mesh axis runs over, the one named last changes fastest.
Arguments:
- queries: bfloat16 [2, 1024, 8192], P(None, ('req', 'prefix')), may hold values from -20 to 20
- prefix_keys: bfloat16 [6144, 1024], P('prefix'), may hold values from -6.25 to 6.25
- prefix_values: bfloat16 [6144, 1024], P('prefix'), may hold values from -6 to 6
- pool_keys: bfloat16 [1024, 128, 1024], P(('req', 'prefix')), may hold values from -8 to 8
- pool_values: bfloat16 [1024, 128, 1024], P(('req', 'prefix')), may hold values from -6 to 6
- new_keys: bfloat16 [2, 1024, 1024], P(None, ('req', 'prefix')), may hold values from -10 to 10
- new_values: bfloat16 [2, 1024, 1024], P(None, ('req', 'prefix')), may hold values from -6 to 6
- block_table: int32 [1024, 16], replicated, may hold values from 0 to 63, as said below
- suffix_lengths: int32 [1024], replicated, may hold values from 0 to 2048, as said below
Outputs:
- attended: bfloat16 [2, 1024, 8192], P(None, ('req', 'prefix'))
Inputs may be any that keep to these rules, and one draw needn't show every extreme that they name: `block_table`: requests 2 g * 32 to (2 g + 2) * 32 - 1 form pair g, whose pool is pool rows 2 g * 16 * 2 onward, 64 of them. Entry j of request i, for j * 128 < suffix_lengths[i], is the slot in the pair's pool that holds that block; every slot of a pair's pool holds exactly one live block; other entries are arbitrary slot numbers. `suffix_lengths`: in each pair one request has 2048 suffix positions, 48 requests have 1 to 128, and the rest none.
All inputs are finite; a program needn't handle non-finite values.
Results may differ from a plain program's by a relative error of at most 0.0023.
Values may be sent and summed in bfloat16 or wider, within the bound.
No kernel may reach another device: no remote copies, remote signals or barrier semaphores. Data moves between devices by JAX's collectives and lax.ppermute only.
A program may use at most 128 MiB of HBM per device.

v0:
```python
import math

import jax
import jax.numpy as jnp
from jax import lax
from jax.sharding import PartitionSpec as P

H = 64
KVH = 8
DH = 128
BLK = 128


NEG = -1e30


def from_partner(array, axis, apart):
    return lax.ppermute(array, axis, [(i, i ^ 1 << apart) for i in range(lax.axis_size(axis))])


def joined(part, axis, combine):
    gathered = jax.tree.map(lambda a: lax.all_gather(a, axis), part)

    def take(source):
        return jax.tree.map(lambda a: lax.dynamic_index_in_dim(a, source, 0, False), gathered)

    return lax.fori_loop(
        1, lax.axis_size(axis), lambda source, state: combine(state, take(source)), take(0)
    )


def block_terms(scores, live):
    masked = jnp.where(live, scores, NEG)
    block_peak = jnp.max(masked, axis=-1)
    weights = jnp.where(live, jnp.exp(masked - block_peak[..., None]), 0.0).astype(jnp.bfloat16)
    block_total = jnp.sum(weights.astype(jnp.float32), axis=-1)
    return (block_peak, weights, block_total)


def fold_blocks(block_peak, block_out, block_total):
    row_top = jnp.max(block_peak, axis=-1)
    factor = jnp.exp(block_peak - row_top[..., None])
    return (
        row_top,
        jnp.sum(factor[..., None] * block_out, axis=-2),
        jnp.sum(factor * block_total, axis=-1),
    )


def join(earlier, later):
    row_top = jnp.maximum(earlier[0], later[0])
    factor_a = jnp.exp(earlier[0] - row_top)
    factor_b = jnp.exp(later[0] - row_top)
    merged_out = earlier[1] * factor_a[..., None] + later[1] * factor_b[..., None]
    return (row_top, merged_out, earlier[2] * factor_a + later[2] * factor_b)


def slot_owner(slot_ids, first_row, query_count, pair_table, lengths, block_width):
    blocks = pair_table.shape[1]
    pair_rows = pair_table.shape[0]
    live_entry = jnp.arange(blocks, dtype=jnp.int32)[None, :] * block_width < lengths[:, None]
    match = (pair_table[None] == slot_ids[:, None, None]) & live_entry[None]
    row_ids = jnp.arange(pair_rows, dtype=jnp.int32)
    owner_row = jnp.sum(jnp.where(match, row_ids[None, :, None], 0), axis=(1, 2)) - first_row
    position = jnp.sum(
        jnp.where(match, jnp.arange(blocks, dtype=jnp.int32)[None, None, :], 0), axis=(1, 2)
    )
    slot_length = jnp.sum(jnp.where(match, lengths[None, :, None], 0), axis=(1, 2))
    is_taken = jnp.any(match, axis=(1, 2)) & (owner_row >= 0) & (owner_row < query_count)
    safe_owner = jnp.clip(owner_row, 0, query_count - 1)
    offsets = jnp.arange(block_width, dtype=jnp.int32)[None, :]
    token_live = is_taken[:, None] & (
        position[:, None] * block_width + offsets < slot_length[:, None]
    )
    return (is_taken, safe_owner, token_live)


def slot_attend(picked_rows, key_rows, value_rows, token_live):
    group_size = H // KVH
    scaling = 1.0 / math.sqrt(DH)
    slot_count = key_rows.shape[0]
    block_width = key_rows.shape[1]
    picked = picked_rows.reshape(2, slot_count, KVH, group_size, DH)
    slot_keys = key_rows.reshape(slot_count, block_width, KVH, DH)
    slot_values = value_rows.reshape(slot_count, block_width, KVH, DH)
    scores = (
        jnp.einsum("snkgd,nbkd->snkgb", picked, slot_keys, preferred_element_type=jnp.float32)
        * scaling
    )
    block_peak, weights, block_total = block_terms(scores, token_live[None, :, None, None, :])
    block_out = jnp.einsum(
        "snkgb,nbkd->snkgd", weights, slot_values, preferred_element_type=jnp.float32
    )
    return (block_peak, block_out, block_total)


def spread_rows(block_peak, block_out, block_total, is_taken, safe_owner, query_count):
    onehot = is_taken[None, :] & (
        safe_owner[None, :] == jnp.arange(query_count, dtype=jnp.int32)[:, None]
    )
    spread = onehot[None, :, :, None, None]
    row_peak = jnp.max(jnp.where(spread, block_peak[:, None], NEG), axis=2)
    factor = jnp.where(spread, jnp.exp(block_peak[:, None] - row_peak[:, :, None]), 0.0)
    row_out = jnp.einsum("srnkg,snkgd->srkgd", factor, block_out, precision=lax.Precision.HIGHEST)
    row_total = jnp.einsum("srnkg,snkg->srkg", factor, block_total, precision=lax.Precision.HIGHEST)
    return (row_peak, row_out, row_total)


def suffix_terms(key_rows, value_rows, slot_ids, query_rows, first_row, pair_table, lengths):
    query_count = query_rows.shape[1]
    is_taken, safe_owner, token_live = slot_owner(
        slot_ids, first_row, query_count, pair_table, lengths, key_rows.shape[1]
    )
    picked = jnp.take(query_rows, safe_owner, axis=1)
    block_peak, block_out, block_total = slot_attend(picked, key_rows, value_rows, token_live)
    return spread_rows(block_peak, block_out, block_total, is_taken, safe_owner, query_count)


def per_device(
    queries,
    prefix_keys,
    prefix_values,
    pool_keys,
    pool_values,
    new_keys,
    new_values,
    block_table,
    suffix_lengths,
):
    group_size = H // KVH
    scaling = 1.0 / math.sqrt(DH)
    n_prefix = lax.axis_size("prefix")
    share_rows = queries.shape[1]
    group_rows = share_rows * n_prefix
    slot_count = pool_keys.shape[0]
    req_index = lax.axis_index("req")
    pre_index = lax.axis_index("prefix")
    pair_half = req_index % 2
    pair_rows = 2 * group_rows
    pair_start = req_index // 2 * pair_rows
    pair_table = lax.dynamic_slice_in_dim(block_table, pair_start, pair_rows, 0)
    lengths = lax.dynamic_slice_in_dim(suffix_lengths, pair_start, pair_rows, 0)
    slot_range = jnp.arange(slot_count, dtype=jnp.int32)
    own_ids = (pair_half * n_prefix + pre_index) * slot_count + slot_range
    group_queries = lax.all_gather(queries, "prefix", axis=1, tiled=True)
    query_tiles = group_queries.reshape(2, group_rows, KVH, group_size, DH)
    key_rows = prefix_keys.reshape(-1, KVH, DH)
    scores = (
        jnp.einsum("srkgd,tkd->srkgt", query_tiles, key_rows, preferred_element_type=jnp.float32)
        * scaling
    )
    scores = scores.reshape(2, group_rows, KVH, group_size, -1, BLK)
    block_peak, weights, block_total = block_terms(scores, True)
    value_rows = prefix_values.reshape(-1, BLK, KVH, DH)
    block_out = jnp.einsum(
        "srkgnb,nbkd->srkgnd", weights, value_rows, preferred_element_type=jnp.float32
    )
    local = fold_blocks(block_peak, block_out, block_total)
    own_first = pair_half * group_rows
    partner_first = (1 - pair_half) * group_rows
    partner_queries = from_partner(group_queries, "req", 0)
    suffix = suffix_terms(
        pool_keys, pool_values, own_ids, group_queries, own_first, pair_table, lengths
    )
    lent = suffix_terms(
        pool_keys, pool_values, own_ids, partner_queries, partner_first, pair_table, lengths
    )
    returned = from_partner((lent[0], lent[1], lent[2]), "req", 0)
    suffix = join(suffix, returned)
    local = join(local, suffix)
    merged = joined((local[0], local[1], local[2]), "prefix", join)
    mine = tuple(
        (
            lax.dynamic_slice_in_dim(member, pre_index * share_rows, share_rows, 1)
            for member in merged
        )
    )
    own_queries = queries.reshape(2, share_rows, KVH, group_size, DH)
    fresh_keys = new_keys.reshape(2, share_rows, KVH, DH)
    fresh_values = new_values.reshape(2, share_rows, KVH, DH)
    scores = (
        jnp.einsum("srkgd,nrkd->srkgn", own_queries, fresh_keys, preferred_element_type=jnp.float32)
        * scaling
    )
    new_live = (jnp.arange(2)[None, :] <= jnp.arange(2)[:, None])[:, None, None, None, :]
    new_peak, new_weights, new_total = block_terms(scores, new_live)
    new_out = jnp.einsum(
        "srkgn,nrkd->srkgd", new_weights, fresh_values, preferred_element_type=jnp.float32
    )
    final = join(mine, (new_peak, new_out, new_total))
    result = final[1] / final[2][..., None]
    return result.astype(jnp.bfloat16).reshape(2, share_rows, H * DH)


def solution(mesh):
    placed = (
        P(None, ("req", "prefix"), None),
        P("prefix", None),
        P("prefix", None),
        P(("req", "prefix"), None, None),
        P(("req", "prefix"), None, None),
        P(None, ("req", "prefix"), None),
        P(None, ("req", "prefix"), None),
        P(),
        P(),
    )
    return jax.shard_map(
        per_device,
        mesh=mesh,
        in_specs=placed,
        out_specs=P(None, ("req", "prefix"), None),
        check_vma=False,
    )
```

profile of v0, /device:TPU:1, one launch (start us, length us, event | category | flops | bytes accessed | tf_op | source)
XLA Modules:
  0.0 421.2 jit_solution(4469419800522458257)
XLA Ops:
  6.5 1.7 copy.188
  9.8 1.1 copy.262
  10.9 1.1 copy.264
  15.2 41.0 %all-gather.6.cloned.1.call-done = bf16[2,32,8192]{2,0,1:T(2,128)(2,1)} async-done(((bf16[2,2,8192]{2,0,1:T(2,128)(2,1)}), bf16[2,32,8192]{2,0,1:T(2,128)(2,1)}) %all-gather.6.cloned.1.call-update) | async-done | bytes 1048592 | tf_op jit(solution)/shard_map/all_gather | solution.py:145
  56.2 1.9 gather_fusion
  58.9 1.8 reshape.370
  60.8 1.4 fusion.77
  62.3 4.1 bitcast_reduce_fusion
  66.4 3.3 collective-permute-start
  69.7 9.8 %convert_reduce_fusion = (f32[2,32,8,8,3]{3,4,2,1,0:T(4,128)S(1)}, bf16[2,32,8,8,3,128]{5,3,4,2,1,0:T(8,128)(2,1)}) fusion(f32[2,32,8,8,3]{3,4,2,1,0:T(4,128)S(1)} %bitcast_reduce_fusion, f32[2,32,8,8,384]{4,1,3,0,2:T(8,128)S(1)} %get-tuple-element.252), kind=kLoop, calls=%fused_computation.16 | loop fusion | flops 6279168 | bytes 9535488 | tf_op jit(solution)/shard_map/reduce_sum | solution.py:36
  79.5 13.4 %collective-permute-done = bf16[2,32,8192]{2,0,1:T(2,128)(2,1)} collective-permute-done((bf16[2,32,8192]{2,0,1:T(2,128)(2,1)S(1)}, bf16[2,32,8192]{2,0,1:T(2,128)(2,1)}, u32[]{:S(2)}, u32[]{:S(2)}) %collective-permute-start) | collective-permute-done | bytes 1048608 | tf_op jit(solution)/shard_map/ppermute | solution.py:18
  92.9 1.9 gather_fusion.1
  96.5 1.7 fusion.79
  98.3 1.4 convolution_bitcast_fusion.1
  100.6 5.6 %convolution_bitcast_fusion = f32[2,32,8,8,128]{4,1,3,2,0:T(8,128)} fusion(f32[2,2,8,8,128]{4,3,0,2,1:T(8,128)S(1)} %convolution_bitcast_fusion.1, pred[32,2]{0,1:T(4,128)(4,1)} %compare_and_fusion.3, f32[2,32,8,8]{1,3,2,0:T(8,128)S(1)} %select_reduce_fusion, f32[2,2,8,8]{1,3,2,0:T(8,128)S(1)} %copy.197), kind=kOutput, calls=%fused_computation.25 | convolution fusion | flops 12599296 | bytes 2245696 | tf_op jit(solution)/shard_map/srnkg,snkgd->srkgd/dot_general | solution.py:104
  106.2 3.1 collective-permute-start.2
  109.4 1.6 fusion.78
  111.5 0.9 copy.194
  113.0 1.2 copy.204
  114.4 1.0 convolution_bitcast_fusion.2
  115.4 3.5 fusion.3
  119.5 1.7 fusion.36
  121.2 2.1 collective-permute-start.3
  123.5 3.4 collective-permute-start.1
  126.8 1.6 fusion.35
  128.5 27.4 %collective-permute-done.3 = f32[2,32,8,8]{1,3,0,2:T(8,128)S(1)} collective-permute-done((f32[2,32,8,8]{1,3,0,2:T(8,128)S(1)}, f32[2,32,8,8]{1,3,0,2:T(8,128)S(1)}, u32[]{:S(2)}, u32[]{:S(2)}) %collective-permute-start.3) | collective-permute-done | bytes 16416 | tf_op jit(solution)/shard_map/ppermute | solution.py:18
  155.9 1.4 collective-permute-done.1
  157.4 7.3 %fusion.10 = f32[2,32,8,8,128]{4,1,3,2,0:T(8,128)S(1)} fusion(f32[2,32,8,8,128]{4,3,1,0,2:T(8,128)S(1)} %fusion.3, f32[2,32,8,8,128]{4,1,3,2,0:T(8,128)} %collective-permute-done.2, f32[2,2,8,8,128]{4,3,0,2,1:T(8,128)S(1)} %copy-done.16, pred[32,2]{0,1:T(4,128)(4,1)S(1)} %copy-done.24, f32[2,32,8,8]{1,3,2,0:T(8,128)S(1)} %select_reduce_fusion.1, ...), kind=kOutput, calls=%fused_computation.23 | convolution fusion | flops 15745024 | bytes 6505536 | tf_op jit(solution)/shard_map/srnkg,snkgd->srkgd/dot_general | solution.py:104
  164.6 2.5 copy.217
  168.7 23.5 %all-gather = f32[32,32,8,8]{1,3,2,0:T(8,128)} all-gather(f32[2,32,8,8]{1,3,2,0:T(8,128)S(1)} %copy.200), channel_id=2, replica_groups=mesh['req'=32,'prefix'=16] {'prefix'}, dimensions={0}, use_global_device_ids=true | all-gather | bytes 278528 | tf_op jit(solution)/shard_map/all_gather | solution.py:22
  193.1 25.2 %all-gather.2 = f32[32,32,8,8]{1,3,2,0:T(8,128)} all-gather(f32[2,32,8,8]{1,3,2,0:T(8,128)S(1)} %copy.221), channel_id=4, replica_groups=mesh['req'=32,'prefix'=16] {'prefix'}, dimensions={0}, use_global_device_ids=true | all-gather | bytes 278528 | tf_op jit(solution)/shard_map/all_gather | solution.py:22
  219.1 132.5 %all-gather.8.cloned.1.call-done = f32[32,32,8,8,128]{4,3,2,1,0:T(8,128)} async-done(((f32[2,32,8,8,128]{4,3,2,1,0:T(8,128)}), f32[32,32,8,8,128]{4,3,2,1,0:T(8,128)}) %all-gather.8.cloned.1.call-update) | async-done | bytes 33554448 | tf_op jit(solution)/shard_map/all_gather | solution.py:22
  351.7 1.7 slice.11
  353.4 59.5 %while.19 = (s32[]{:T(128)}, f32[2,32,8,8]{1,3,2,0:T(8,128)S(1)}, f32[2,32,8,8,128]{4,3,2,1,0:T(8,128)S(1)}, f32[2,32,8,8]{1,3,2,0:T(8,128)S(1)}, f32[16,2,32,8,...) while((s32[]{:T(128)}, f32[2,32,8,8]{1,3,2,0:T(8,128)S(1)}, ...), condition=%wide.region_16.18_spmd, body=%wide.region_15.17_spmd.sunk | while | flops 1597445 | bytes 6520983 | solution.py:27
  353.4 0.9 fusion.91
  354.7 2.7 fusion.92
  357.4 0.9 fusion.91
  358.7 2.7 fusion.92
  361.4 0.9 fusion.91
  362.6 2.7 fusion.92
  365.3 0.9 fusion.91
  366.6 2.7 fusion.92
  369.3 0.9 fusion.91
  370.6 2.7 fusion.92
  373.3 0.9 fusion.91
  374.5 2.7 fusion.92
  377.2 0.9 fusion.91
  378.5 2.7 fusion.92
  381.2 0.9 fusion.91
  382.5 2.7 fusion.92
  385.2 0.9 fusion.91
  386.4 2.7 fusion.92
  389.1 0.9 fusion.91
  390.4 2.7 fusion.92
  393.1 0.9 fusion.91
  394.4 2.7 fusion.92
  397.1 0.9 fusion.91
  398.3 2.7 fusion.92
  401.0 0.9 fusion.91
  402.3 2.7 fusion.92
  405.0 0.9 fusion.91
  406.3 2.7 fusion.92
  409.0 0.9 fusion.91
  410.2 2.7 fusion.92
  (138 shorter events, 19.1 us)
Async XLA Ops:
  6.5 1.8 copy-start
  6.5 5.5 %copy-start.3 = (bf16[384,1024]{1,0:T(8,128)(2,1)S(1)}, bf16[384,1024]{1,0:T(8,128)(2,1)}, u32[]{:S(2)}) copy-start(bf16[384,1024]{1,0:T(8,128)(2,1)} %param.14) | copy-start | bytes 2359300
  6.5 5.7 %copy-start.4 = (bf16[384,1024]{1,0:T(8,128)(2,1)S(1)}, bf16[384,1024]{1,0:T(8,128)(2,1)}, u32[]{:S(2)}) copy-start(bf16[384,1024]{1,0:T(8,128)(2,1)} %param.15) | copy-start | bytes 2359300
  6.5 49.7 %all-gather.6.cloned.1.call-start = ((), (), s32[]{:S(2)}) async-start(), calls=%async_computation | async-start | bytes 1114112 | tf_op jit(solution)/shard_map/all_gather | solution.py:145
  8.2 343.5 %all-gather.8.cloned.1.call-start = ((), (), s32[]{:S(2)}) async-start(), calls=%async_computation.1 | async-start | bytes 35651584 | tf_op jit(solution)/shard_map/all_gather | solution.py:22
  62.2 4.2 copy-start.2
  66.4 26.5 %collective-permute-start = (bf16[2,32,8192]{2,0,1:T(2,128)(2,1)S(1)}, bf16[2,32,8192]{2,0,1:T(2,128)(2,1)}, u32[]{:S(2)}, u32[]{:S(2)}) collective-permute-start(bf16[2,32,8192]{2,0,1:T(2,128)(2,1)S(1)} %copy-done.2), channel_id=1, source_target_pairs={{0,16},{16,0},{32,48},{48,32},{64,80},{80,64},{96,112},{112,96},{1... | collective-permute-start | bytes 3145736 | tf_op jit(solution)/shard_map/ppermute | solution.py:18
  98.3 12.7 %copy-start.5 = (f32[2,2,8,8]{1,3,2,0:T(8,128)}, f32[2,2,8,8]{1,3,2,0:T(8,128)S(1)}, u32[]{:S(2)}) copy-start(f32[2,2,8,8]{1,3,2,0:T(8,128)S(1)} %copy.197) | copy-start | bytes 3076
  98.3 11.1 %copy-start.12 = (bf16[2,2,8,8,128]{4,3,2,0,1:T(8,128)(2,1)S(1)}, bf16[2,2,8,8,128]{4,3,2,0,1:T(8,128)(2,1)}, u32[]{:S(2)}) copy-start(bf16[2,2,8,8,128]{4,3,2,0,1:T(8,128)(2,1)} %reshape.317) | copy-start | bytes 196612
  98.3 11.1 %copy-start.20 = (pred[2,128]{1,0:T(4,128)(4,1)S(1)}, pred[2,128]{1,0:T(4,128)(4,1)}, u32[]{:S(2)}) copy-start(pred[2,128]{1,0:T(4,128)(4,1)} %get-tuple-element.242) | copy-start | bytes 772
  100.6 8.7 %copy-start.7 = (f32[2,32,8,8]{1,3,2,0:T(8,128)}, f32[2,32,8,8]{1,3,2,0:T(8,128)S(1)}, u32[]{:S(2)}) copy-start(f32[2,32,8,8]{1,3,2,0:T(8,128)S(1)} %select_reduce_fusion) | copy-start | bytes 49156
  106.2 51.1 %collective-permute-start.2 = (f32[2,32,8,8,128]{4,1,3,2,0:T(8,128)}, f32[2,32,8,8,128]{4,1,3,2,0:T(8,128)}, u32[]{:S(2)}, u32[]{:S(2)}) collective-permute-start(f32[2,32,8,8,128]{4,1,3,2,0:T(8,128)} %convolution_bitcast_fusion), channel_id=1, source_target_pairs={{0,16},{16,0},{32,48},{48,32},{64,80},{80,64},{96,112},{112,96},{1... | collective-permute-start | bytes 6291464 | tf_op jit(solution)/shard_map/ppermute | solution.py:18
  111.5 2.7 copy-start.23
  111.5 2.9 copy-start.10
  111.5 2.9 copy-start.11
  111.5 2.9 copy-start.14
  111.5 2.9 copy-start.21
  115.4 3.5 copy-start.8
  115.4 3.6 copy-start.9
  115.4 3.6 copy-start.15
  115.4 3.6 copy-start.19
  115.4 3.6 copy-start.22
  115.4 4.1 copy-start.6
  118.9 38.4 %copy-start.16 = (f32[2,2,8,8,128]{4,3,0,2,1:T(8,128)S(1)}, f32[2,2,8,8,128]{4,3,0,2,1:T(8,128)}, u32[]{:S(2)}) copy-start(f32[2,2,8,8,128]{4,3,0,2,1:T(8,128)} %convolution_bitcast_fusion.2) | copy-start | bytes 393220
  118.9 38.4 %copy-start.24 = (pred[32,2]{0,1:T(4,128)(4,1)S(1)}, pred[32,2]{0,1:T(4,128)(4,1)}, u32[]{:S(2)}) copy-start(pred[32,2]{0,1:T(4,128)(4,1)} %compare_and_fusion.5) | copy-start | bytes 196
  121.2 34.7 %collective-permute-start.3 = (f32[2,32,8,8]{1,3,0,2:T(8,128)S(1)}, f32[2,32,8,8]{1,3,0,2:T(8,128)S(1)}, u32[]{:S(2)}, u32[]{:S(2)}) collective-permute-start(f32[2,32,8,8]{1,3,0,2:T(8,128)S(1)} %bitcast.142), channel_id=1, source_target_pairs={{0,16},{16,0},{32,48},{48,32},{64,80},{80,64},{96,112},{112,96},{1... | collective-permute-start | bytes 49160 | tf_op jit(solution)/shard_map/ppermute | solution.py:18
  123.5 33.8 %collective-permute-start.1 = (f32[2,32,8,8]{1,3,0,2:T(8,128)S(1)}, f32[2,32,8,8]{1,3,0,2:T(8,128)S(1)}, u32[]{:S(2)}, u32[]{:S(2)}) collective-permute-start(f32[2,32,8,8]{1,3,0,2:T(8,128)S(1)} %copy.198), channel_id=1, source_target_pairs={{0,16},{16,0},{32,48},{48,32},{64,80},{80,64},{96,112},{112,96},{1... | collective-permute-start | bytes 49160 | tf_op jit(solution)/shard_map/ppermute | solution.py:18
  167.2 0.8 copy-start.13
  167.2 0.9 copy-start.17
  167.2 0.9 copy-start.18
  412.9 1.4 copy-start.1
Sparse Core Ops, SparseCore 0:
  9.5 46.6 all-gather.5
  167.3 184.3 all-gather.7
where the time goes:
time: 423 us; the launch traced here: 421 us
  waiting for transfers between devices  216 us (51%)
  other arithmetic  73.4 us (17%)
  blocking collectives  48.7 us (12%)
  local copies, waits for them, and re-layouts  29.4 us (7%)
  matrix products  27.5 us (7%)
  between operations  14 us (3%)
  starting transfers between devices  12 us (3%)
    all_gather x1, waiting for transfers between devices, joined(): gathered = jax.tree.map(lambda a: lax.all_gather(a, axis), part)  133 us
    all_gather x2, blocking collectives, joined(): gathered = jax.tree.map(lambda a: lax.all_gather(a, axis), part)  48.7 us
    ppermute x4, waiting for transfers between devices, from_partner(): lax.ppermute(array, axis, [(i, i ^ 1 << apart) for i in range(lax.axis_si...  42.2 us
    all_gather x1, waiting for transfers between devices, per_device(): group_queries = lax.all_gather(queries, 'prefix', axis=1, tiled=True)  41 us
    add x15, other arithmetic, join(): earlier[1] * factor_a[..., None] + later[1] * factor_b[..., None]  40.4 us
    add x17, other arithmetic, join(): return (row_top, merged_out, earlier[2] * factor_a + later[2] * factor_b)  14.2 us
    dot_general x2, matrix products, spread_rows(): jnp.einsum('srnkg,snkgd->srkgd', factor, block_out, precision=lax.Precisi...  12.9 us
    ppermute x4, starting transfers between devices, from_partner(): lax.ppermute(array, axis, [(i, i ^ 1 << apart) for i in range(lax.axis_si...  11.9 us
  transfers between devices with their start and end apart: 6, of which 5 were waited for; matrix products, arithmetic and copies ran while one was open for 8% of the time, Pallas kernels for 0%

commit v1 on v0

v1 whole, which is shorter than its diff:
```python
import functools
import math

import jax
import jax.numpy as jnp
from jax import lax
from jax.experimental import pallas as pl
from jax.experimental.pallas import tpu as pltpu
from jax.sharding import PartitionSpec as P

H = 64
KVH = 8
DH = 128
BLK = 128
GROUP = H // KVH
HALF = KVH // 2
NEG = -1e30
LOG2E = 1.0 / math.log(2.0)
EXPO = LOG2E / math.sqrt(DH)
LIFT = 8192.0

bf16 = jnp.bfloat16
f32 = jnp.float32
NT = (((1,), (1,)), ((), ()))
VM = pl.BlockSpec(memory_space=pltpu.VMEM)
SM = pl.BlockSpec(memory_space=pltpu.SMEM)
ANY = pl.BlockSpec(memory_space=pl.ANY)


def prepare_kernel(q_ref, nk_ref, nv_ref, len_ref, table_ref, qt_ref, nkp_ref, nvp_ref, meta_ref, rows_ref, sem):
    req = lax.axis_index("req")
    pre = lax.axis_index("prefix")
    pair_rows = rows_ref.shape[0]
    n_pre = pair_rows // 4
    pair = req // 2
    side = req % 2
    copy = pltpu.make_async_copy(
        table_ref.at[pl.ds(pl.multiple_of(pair * pair_rows, pair_rows), pair_rows), :], rows_ref, sem
    )
    copy.start()
    pieces = []
    steps = [q_ref[s].astype(f32) for s in range(2)]
    for head in range(H):
        for s in range(2):
            pieces.append(steps[s][:, head * DH : (head + 1) * DH])
    qt_ref[...] = jnp.concatenate(pieces, axis=0).astype(bf16)
    for src, dst in ((nk_ref, nkp_ref), (nv_ref, nvp_ref)):
        top = jnp.concatenate([src[0].astype(f32), src[1].astype(f32), jnp.zeros((12, KVH * DH), f32)], axis=0)
        dst[...] = jnp.zeros(dst.shape, bf16)
        dst[0:16, :] = top.astype(bf16)
    lane = lax.broadcasted_iota(jnp.int32, (pair_rows, 128), 1)
    row = lax.broadcasted_iota(jnp.int32, (pair_rows, 128), 0)
    per_line = 128 // pair_rows
    line = len_ref[pl.ds(pair // per_line, 1), :]
    at = row + (pair % per_line) * pair_rows
    lengths = jnp.sum(jnp.where(lane == at, jnp.broadcast_to(line, (pair_rows, 128)), 0), axis=1, keepdims=True)
    copy.wait()
    blocks = rows_ref.shape[1]
    table = rows_ref[...]
    col = lax.broadcasted_iota(jnp.int32, (pair_rows, blocks), 1)
    trow = lax.broadcasted_iota(jnp.int32, (pair_rows, blocks), 0)
    left = jnp.broadcast_to(lengths, (pair_rows, blocks)) - col * BLK
    for n in range(4):
        holder = side if n < 2 else 1 - side
        slot = (holder * n_pre + pre) * 2 + n % 2
        hit = (table == slot) & (left > 0)
        owner = jnp.sum(jnp.where(hit, trow, 0)) - side * (pair_rows // 2)
        live = jnp.sum(jnp.where(hit, jnp.minimum(left, BLK), 0))
        mine = (owner >= 0) & (owner < pair_rows // 2)
        owner = jnp.where(mine, owner, 0)
        meta_ref[n, 0] = owner // 2
        meta_ref[n, 1] = owner % 2
        meta_ref[n, 2] = jnp.where(mine, live, 0)


def attend_kernel(
    flip, q_ref, pk_ref, pv_ref, ok_ref, ov_ref, xk_ref, xv_ref, nk_ref, nv_ref, meta_ref,
    out_ref, m_s, t_s, a_s, l_s,
):
    pre = lax.axis_index("prefix")
    half = pre % 2
    if flip:
        half = 1 - half
    n_dev = q_ref.shape[0]
    rows = n_dev * 32
    ones = jnp.ones((BLK, DH), bf16)
    lane = lax.broadcasted_iota(jnp.int32, (32, BLK), 1)
    row = lax.broadcasted_iota(jnp.int32, (32, BLK), 0)
    row_req = row % 2
    row_step = row // 2 % 2
    new_live = (lane < 4) & (lane % 2 == row_req) & (lane // 2 <= row_step)
    n_blocks = pk_ref.shape[0] // BLK
    for i in range(HALF):
        kvh = half * HALF + i
        lanes = pl.ds(pl.multiple_of(kvh * DH, DH), DH)
        qrows = pl.ds(pl.multiple_of(kvh * 32, 32), 32)
        q = q_ref[:, qrows, :].reshape(rows, DH)
        peaks, outs = [], []
        for b in range(n_blocks):
            span = slice(b * BLK, (b + 1) * BLK)
            s = lax.dot_general(q, pk_ref[span, lanes], NT, preferred_element_type=f32)
            peak = jnp.max(s, axis=1, keepdims=True)
            w = jnp.exp2((s - peak) * EXPO).astype(bf16)
            v = jnp.concatenate([pv_ref[span, lanes], ones], axis=1)
            peaks.append(peak)
            outs.append(jnp.dot(w, v, preferred_element_type=f32))
        top = functools.reduce(jnp.maximum, peaks)
        both = 0.0
        for peak, o in zip(peaks, outs):
            both = both + jnp.exp2((peak - top) * EXPO) * o
        m_s[...] = jnp.broadcast_to(top, (rows, DH)).reshape(n_dev, 32, DH)
        a_s[...] = both[:, :DH].reshape(n_dev, 32, DH)
        t_s[...] = both[:, DH:].reshape(n_dev, 32, DH)
        extra = []
        for n in range(5):
            if n < 4:
                kr, vr = (ok_ref, ov_ref) if n < 2 else (xk_ref, xv_ref)
                dev = meta_ref[n, 0]
                k, v = kr[n % 2, :, lanes], vr[n % 2, :, lanes]
                live = (row_req == meta_ref[n, 1]) & (lane < meta_ref[n, 2])
            else:
                dev = pre
                k, v = nk_ref[:, lanes], nv_ref[:, lanes]
                live = new_live
            s = lax.dot_general(q_ref[dev, qrows, :], k, NT, preferred_element_type=f32)
            s = jnp.where(live, s, NEG)
            peak = jnp.max(s, axis=1, keepdims=True)
            w = jnp.where(live, jnp.exp2((s - peak) * EXPO), 0.0).astype(bf16)
            o = jnp.dot(w, jnp.concatenate([v, ones], axis=1), preferred_element_type=f32)
            extra.append((dev, peak, o))
        for dev, peak, o in extra:
            old = m_s[dev]
            new = jnp.maximum(old, peak)
            fa = jnp.exp2((old - new) * EXPO)
            fb = jnp.exp2((peak - new) * EXPO)
            m_s[dev] = new
            a_s[dev] = a_s[dev] * fa + o[:, :DH] * fb
            t_s[dev] = t_s[dev] * fa + o[:, DH:] * fb
        total = t_s[...]
        out_ref[:, i * 32 : (i + 1) * 32, :] = a_s[...] / total
        l_s[:, i * 32 : (i + 1) * 32, :] = m_s[...] * EXPO + jnp.log(total) * LOG2E
    eye = lax.broadcasted_iota(jnp.int32, (DH, DH), 0) == lax.broadcasted_iota(jnp.int32, (DH, DH), 1)
    for dev in range(n_dev):
        line = jnp.sum(jnp.where(eye, l_s[dev], 0.0), axis=0, keepdims=True)
        out_ref[dev, 128:136, :] = jnp.broadcast_to(line, (8, DH))


def columns(lines):
    pad = jnp.zeros((DH - lines.shape[0], DH), f32)
    return jnp.concatenate([lines, pad], axis=0).T


def core_merge_kernel(a_ref, b_ref, out_ref):
    n_dev = a_ref.shape[0]
    la = a_ref[:, 128:136, :][:, 0, :]
    lb = b_ref[:, 128:136, :][:, 0, :]
    top = jnp.maximum(la, lb)
    wa = jnp.exp2(la - top)
    wb = jnp.exp2(lb - top)
    total = wa + wb
    lse = top + jnp.log(total) * LOG2E
    hi = lse.astype(bf16).astype(f32)
    mid = (lse - hi).astype(bf16).astype(f32)
    low = lse - hi - mid
    ca = columns(wa * (LIFT / total))
    cb = columns(wb * (LIFT / total))
    for dev in range(n_dev):
        out_ref[dev, 0:128, :] = (
            a_ref[dev, 0:128, :] * ca[:, dev : dev + 1] + b_ref[dev, 0:128, :] * cb[:, dev : dev + 1]
        )
        out_ref[dev, 128:136, :] = jnp.concatenate(
            [hi[dev : dev + 1], mid[dev : dev + 1], low[dev : dev + 1], jnp.zeros((5, DH), f32)], axis=0
        )


def final_kernel(z_ref, out_ref):
    n_dev = z_ref.shape[0]
    for c in range(2):
        lines = []
        for src in range(c, n_dev, 2):
            parts = z_ref[src, 128:136, :]
            lines.append(jnp.sum(parts, axis=0, keepdims=True))
        lse = jnp.concatenate(lines, axis=0)
        w = jnp.exp2(lse - jnp.max(lse, axis=0, keepdims=True))
        w = columns(w / (LIFT * jnp.sum(w, axis=0, keepdims=True)))
        o = 0.0
        for y, src in enumerate(range(c, n_dev, 2)):
            o = o + z_ref[src, 0:128, :] * w[:, y : y + 1]
        for h in range(H // 2):
            head = c * (H // 2) + h
            for s in range(2):
                r = h * 4 + s * 2
                out_ref[s, :, head * DH : (head + 1) * DH] = o[r : r + 2, :].astype(bf16)


def call(kernel, out_shape, ins, out_specs=VM, scratch=(), flops=0, moved=0, name=None):
    return pl.pallas_call(
        kernel,
        out_shape=out_shape,
        in_specs=ins,
        out_specs=out_specs,
        scratch_shapes=list(scratch),
        compiler_params=pltpu.CompilerParams(vmem_limit_bytes=40 * 1024 * 1024),
        cost_estimate=pl.CostEstimate(flops=flops, bytes_accessed=moved, transcendentals=0),
        name=name,
    )


def per_device(
    queries,
    prefix_keys,
    prefix_values,
    pool_keys,
    pool_values,
    new_keys,
    new_values,
    block_table,
    suffix_lengths,
):
    n_req = lax.axis_size("req")
    n_pre = lax.axis_size("prefix")
    pair_rows = 4 * n_pre
    swap = [(i, i ^ 1) for i in range(n_req)]
    core = [(i, i ^ 1) for i in range(n_pre)]
    far_keys = lax.ppermute(pool_keys, "req", swap)
    far_values = lax.ppermute(pool_values, "req", swap)
    sds = jax.ShapeDtypeStruct
    own, nk, nv, meta = call(
        prepare_kernel,
        (sds((4 * H, DH), bf16), sds((BLK, KVH * DH), bf16), sds((BLK, KVH * DH), bf16), sds((4, 3), jnp.int32)),
        [VM, VM, VM, VM, ANY],
        (VM, VM, VM, SM),
        [pltpu.VMEM((pair_rows, block_table.shape[1]), jnp.int32), pltpu.SemaphoreType.DMA],
        name="prepare",
    )(queries, new_keys, new_values, suffix_lengths.reshape(-1, 128), block_table)
    group = lax.all_gather(own, "prefix", axis=0)
    partial = sds((n_pre, 136, DH), f32)
    state = pltpu.VMEM((n_pre, 32, DH), f32)

    def attend(flip):
        return call(
            functools.partial(attend_kernel, flip),
            partial,
            [VM] * 9 + [SM],
            VM,
            [state, state, state, pltpu.VMEM((n_pre, 128, DH), f32)],
            flops=800_000_000,
            moved=6_000_000,
            name="attend_other" if flip else "attend_own",
        )(group, prefix_keys, prefix_values, pool_keys, pool_values, far_keys, far_values, nk, nv, meta)

    theirs = lax.ppermute(attend(True), "prefix", core)
    mine = attend(False)
    merged = call(core_merge_kernel, partial, [VM, VM], moved=4_000_000, name="core_merge")(mine, theirs)
    spread = lax.all_to_all(merged.astype(jnp.float16), "prefix", 0, 0, tiled=True)
    return call(final_kernel, sds((2, 2, H * DH), bf16), [VM], moved=1_000_000, name="final")(
        spread.astype(f32)
    )


def solution(mesh):
    placed = (
        P(None, ("req", "prefix"), None),
        P("prefix", None),
        P("prefix", None),
        P(("req", "prefix"), None, None),
        P(("req", "prefix"), None, None),
        P(None, ("req", "prefix"), None),
        P(None, ("req", "prefix"), None),
        P(),
        P(),
    )
    return jax.shard_map(
        per_device,
        mesh=mesh,
        in_specs=placed,
        out_specs=P(None, ("req", "prefix"), None),
        check_vma=False,
    )
```

time: 423 us -> 109 us (0.26)
  waiting for transfers between devices: 216 us -> 41 us
  other arithmetic: 73.4 us -> 0.15 us
  matrix products: 27.5 us -> 0 us
  blocking collectives: 48.7 us -> 22.9 us
  local copies, waits for them, and re-layouts: 29.4 us -> 8.46 us
  Pallas kernels: 0 us -> 14.6 us
    all_gather x2 -> x1, waiting for transfers between devices: 174 us -> 24.7 us  [per_device(): group = lax.all_gather(own, 'prefix', axis=0)]
    add x33 -> x0, other arithmetic: 54.6 us -> none  [the longest x15 40.4 us: join(): earlier[1] * factor_a[..., None] + later[1] * factor_b[..., None]]
    all_gather x2 -> x0, blocking collectives: 48.7 us -> none  [joined(): gathered = jax.tree.map(lambda a: lax.all_gather(a, axis), part)]
    dot_general x12 -> x0, matrix products: 27.5 us -> none  [the longest x2 12.9 us: spread_rows(): jnp.einsum('srnkg,snkgd->srkgd', factor, block_out, precision=lax.Precisi...]
    ppermute x4 -> x3, waiting for transfers between devices: 42.2 us -> 16.3 us  [the longest x1 11.2 us: per_device(): far_values = lax.ppermute(pool_values, 'req', swap)]
    all_to_all x0 -> x1, blocking collectives: none -> 22.9 us  [per_device(): lax.all_to_all(merged.astype(jnp.float16), 'prefix', 0, 0, tiled=True)]
    pallas_call x0 -> x5, Pallas kernels: none -> 14.6 us  [the longest x2 11.7 us: attend(): call(functools.partial(attend_kernel, flip), partial, [VM] * 9 + [SM], VM...]
    reduce_sum x5 -> x0, other arithmetic: 10.5 us -> none  [the longest x3 10.2 us: block_terms(): block_total = jnp.sum(weights.astype(jnp.float32), axis=-1)]
  transfers between devices with their start and end apart: 6 -> 4, of which waited for: 5 -> 3; matrix products, arithmetic and copies ran while one was open for 8% -> 0% of each run, Pallas kernels for 0% -> 5%
where the time goes in v1:
time: 109 us
  waiting for transfers between devices  41 us (38%)
  blocking collectives  22.9 us (21%)
  Pallas kernels  14.6 us (13%)
  between operations  13.5 us (12%)
  local copies, waits for them, and re-layouts  8.46 us (8%)
  starting transfers between devices  8.08 us (7%)
    all_gather x1, waiting for transfers between devices, per_device(): group = lax.all_gather(own, 'prefix', axis=0)  24.7 us
    all_to_all x1, blocking collectives, per_device(): lax.all_to_all(merged.astype(jnp.float16), 'prefix', 0, 0, tiled=True)  22.9 us
    pallas_call x2, Pallas kernels, attend(): call(functools.partial(attend_kernel, flip), partial, [VM] * 9 + [SM], VM...  11.7 us
    ppermute x1, waiting for transfers between devices, per_device(): far_values = lax.ppermute(pool_values, 'req', swap)  11.2 us
    unnamed x19, local copies, waits for them, and re-layouts  8.46 us
    ppermute x1, waiting for transfers between devices, per_device(): far_keys = lax.ppermute(pool_keys, 'req', swap)  5.03 us
    ppermute x1, starting transfers between devices, per_device(): far_keys = lax.ppermute(pool_keys, 'req', swap)  3.97 us
  transfers between devices with their start and end apart: 4, of which 3 were waited for; matrix products, arithmetic and copies ran while one was open for 0% of the time, Pallas kernels for 5%

profile of v1, /device:TPU:1, one launch (start us, length us, event | category | flops | bytes accessed | tf_op | source)
XLA Modules:
  0.0 108.7 jit_solution(10708943136495353969)
XLA Ops:
  6.5 0.0 copy-start.1
  6.5 0.0 all-gather.3.cloned.1.call-start
  6.5 1.1 %copy.10.table_ref = s32[1024,16]{1,0:T(8,128)S(1)} copy(s32[1024,16]{0,1:T(8,128)} %param.16) | data formatting | bytes 131072 | tf_op args[7]
  7.7 0.0 copy-start.5
  7.7 0.8 copy-done.5
  8.5 0.0 copy-start.6
  8.5 0.7 copy-done.6
  9.2 0.0 copy-start.7
  9.2 0.7 copy-done.7
  9.9 0.0 copy-start.8
  9.9 0.7 copy-done.8
  10.6 1.0 prepare.1
  11.6 0.0 all-gather.3.cloned.1.call-update
  11.6 4.0 %collective-permute-start = (bf16[2,128,1024]{2,1,0:T(8,128)(2,1)}, bf16[2,128,1024]{2,1,0:T(8,128)(2,1)S(1)}, u32[]{:S(2)}, u32[]{:S(2)}) collective-permute-start(bf16[2,128,1024]{2,1,0:T(8,128)(2,1)} %ok_ref.3), channel_id=1, source_target_pairs={{0,16},{16,0},{32,48},{48,32},{64,80},{80,64},{96,112},{112,96},{1... | collective-permute-start | bytes 1572872 | tf_op jit(solution)/shard_map/ppermute | solution.py:225
  15.6 1.9 %collective-permute-start.1 = (bf16[2,128,1024]{2,1,0:T(8,128)(2,1)}, bf16[2,128,1024]{2,1,0:T(8,128)(2,1)S(1)}, u32[]{:S(2)}, u32[]{:S(2)}) collective-permute-start(bf16[2,128,1024]{2,1,0:T(8,128)(2,1)} %ov_ref.3), channel_id=1, source_target_pairs={{0,16},{16,0},{32,48},{48,32},{64,80},{80,64},{96,112},{112,96},{1... | collective-permute-start | bytes 1572872 | tf_op jit(solution)/shard_map/ppermute | solution.py:226
  17.5 5.0 %collective-permute-done.xk_ref = bf16[2,128,1024]{2,1,0:T(8,128)(2,1)S(1)} collective-permute-done((bf16[2,128,1024]{2,1,0:T(8,128)(2,1)}, bf16[2,128,1024]{2,1,0:T(8,128)(2,1)S(1)}, u32[]{:S(2)}, u32[]{:S(2)}) %collective-permute-start) | collective-permute-done | bytes 524320 | tf_op jit(solution)/shard_map/ppermute | solution.py:225
  22.6 11.2 %collective-permute-done.1.xv_ref = bf16[2,128,1024]{2,1,0:T(8,128)(2,1)S(1)} collective-permute-done((bf16[2,128,1024]{2,1,0:T(8,128)(2,1)}, bf16[2,128,1024]{2,1,0:T(8,128)(2,1)S(1)}, u32[]{:S(2)}, u32[]{:S(2)}) %collective-permute-start.1) | collective-permute-done | bytes 524320 | tf_op jit(solution)/shard_map/ppermute | solution.py:226
  33.8 24.7 %all-gather.3.cloned.1.call-done = bf16[4096,128]{1,0:T(8,128)(2,1)} async-done(((bf16[256,128]{1,0:T(8,128)(2,1)}), bf16[4096,128]{1,0:T(8,128)(2,1)}) %all-gather.3.cloned.1.call-update) | async-done | bytes 1048592 | tf_op jit(solution)/shard_map/all_gather | solution.py:236
  58.5 0.0 copy-done.1
  58.5 0.0 copy-start
  58.5 1.2 %copy-done = bf16[4096,128]{1,0:T(8,128)(2,1)S(1)} copy-done((bf16[4096,128]{1,0:T(8,128)(2,1)S(1)}, bf16[4096,128]{1,0:T(8,128)(2,1)}, u32[]{:S(2)}) %copy-start) | copy-done | bytes 1048600
  59.7 0.0 copy-start.2
  59.7 1.1 %copy-done.2 = bf16[384,1024]{1,0:T(8,128)(2,1)S(1)} copy-done((bf16[384,1024]{1,0:T(8,128)(2,1)S(1)}, bf16[384,1024]{1,0:T(8,128)(2,1)}, u32[]{:S(2)}) %copy-start.2) | copy-done | bytes 786456
  60.9 0.0 copy-start.3
  60.9 1.0 copy-done.3
  61.9 0.0 copy-start.4
  61.9 1.0 copy-done.4
  63.0 5.9 %attend_other.1 = f32[16,136,128]{2,1,0:T(8,128)S(1)} custom-call(bf16[16,256,128]{2,1,0:T(8,128)(2,1)S(1)} %bitcast.2, bf16[384,1024]{1,0:T(8,128)(2,1)S(1)} %copy-done.1, bf16[384,1024]{1,0:T(8,128)(2,1)S(1)} %copy-done.2, bf16[2,128,1024]{2,1,0:T(8,128)(2,1)S(1)} %copy-done.3, bf16[2,128,1024]{2,1,0:T(8,128)(2,1)S(1)} %copy-done.4, ...), custom_call_target="tpu_custom_call" | custom-call | flops 800000000 | bytes 6000000 | tf_op jit(solution)/shard_map/attend_other/pallas_call | solution.py:241
  68.8 2.2 %collective-permute-start.2 = (f32[16,136,128]{2,1,0:T(8,128)S(1)}, f32[16,136,128]{2,1,0:T(8,128)S(1)}, u32[]{:S(2)}, u32[]{:S(2)}) collective-permute-start(f32[16,136,128]{2,1,0:T(8,128)S(1)} %attend_other.1), channel_id=1, source_target_pairs={{0,1},{1,0},{2,3},{3,2},{4,5},{5,4},{6,7},{7,6},{8,9},{9,8},{10,11... | collective-permute-start | bytes 3342344 | tf_op jit(solution)/shard_map/ppermute | solution.py:252
  71.0 5.9 %attend_own.1.a_ref = f32[16,136,128]{2,1,0:T(8,128)S(1)} custom-call(bf16[16,256,128]{2,1,0:T(8,128)(2,1)S(1)} %bitcast.3, bf16[384,1024]{1,0:T(8,128)(2,1)S(1)} %copy-done.1, bf16[384,1024]{1,0:T(8,128)(2,1)S(1)} %copy-done.2, bf16[2,128,1024]{2,1,0:T(8,128)(2,1)S(1)} %copy-done.3, bf16[2,128,1024]{2,1,0:T(8,128)(2,1)S(1)} %copy-done.4, ...), custom_call_target="tpu_custom_call" | custom-call | flops 800000000 | bytes 6000000 | tf_op jit(solution)/shard_map/attend_own/pallas_call | solution.py:241
  76.9 0.0 collective-permute-done.2.b_ref
  76.9 0.8 core_merge.1
  77.7 0.1 convert_element_type.6
  77.8 22.9 %all_to_all.5 = f16[16,136,128]{2,1,0:T(8,128)(2,1)S(1)} all-to-all(f16[16,136,128]{2,1,0:T(8,128)(2,1)S(1)} %convert_element_type.6), channel_id=1, replica_groups=mesh['req'=32,'prefix'=16] {'prefix'}, dimensions={0} | all-to-all | bytes 1114112 | tf_op jit(solution)/shard_map/all_to_all | solution.py:255
  100.7 0.1 convert_element_type.7.z_ref
  100.7 1.1 %final.1 = bf16[2,2,8192]{2,1,0:T(2,128)(2,1)} custom-call(f32[16,136,128]{2,1,0:T(8,128)S(1)} %convert_element_type.7.z_ref), custom_call_target="tpu_custom_call" | custom-call | bytes 1000000 | tf_op jit(solution)/shard_map/final/pallas_call | solution.py:256
Async XLA Ops:
  6.5 52.0 %copy-start.1 = (bf16[384,1024]{1,0:T(8,128)(2,1)S(1)}, bf16[384,1024]{1,0:T(8,128)(2,1)}, u32[]{:S(2)}) copy-start(bf16[384,1024]{1,0:T(8,128)(2,1)} %pk_ref.3) | copy-start | bytes 2359300
  6.5 52.0 %all-gather.3.cloned.1.call-start = ((), (), s32[]{:S(2)}) async-start(), calls=%async_computation.1 | async-start | bytes 1114112 | tf_op jit(solution)/shard_map/all_gather | solution.py:236
  7.7 0.8 copy-start.5
  8.5 0.7 copy-start.6
  9.2 0.7 copy-start.7
  9.9 0.7 copy-start.8
  11.6 10.9 %collective-permute-start = (bf16[2,128,1024]{2,1,0:T(8,128)(2,1)}, bf16[2,128,1024]{2,1,0:T(8,128)(2,1)S(1)}, u32[]{:S(2)}, u32[]{:S(2)}) collective-permute-start(bf16[2,128,1024]{2,1,0:T(8,128)(2,1)} %ok_ref.3), channel_id=1, source_target_pairs={{0,16},{16,0},{32,48},{48,32},{64,80},{80,64},{96,112},{112,96},{1... | collective-permute-start | bytes 1572872 | tf_op jit(solution)/shard_map/ppermute | solution.py:225
  15.6 18.2 %collective-permute-start.1 = (bf16[2,128,1024]{2,1,0:T(8,128)(2,1)}, bf16[2,128,1024]{2,1,0:T(8,128)(2,1)S(1)}, u32[]{:S(2)}, u32[]{:S(2)}) collective-permute-start(bf16[2,128,1024]{2,1,0:T(8,128)(2,1)} %ov_ref.3), channel_id=1, source_target_pairs={{0,16},{16,0},{32,48},{48,32},{64,80},{80,64},{96,112},{112,96},{1... | collective-permute-start | bytes 1572872 | tf_op jit(solution)/shard_map/ppermute | solution.py:226
  58.5 1.2 %copy-start = (bf16[4096,128]{1,0:T(8,128)(2,1)S(1)}, bf16[4096,128]{1,0:T(8,128)(2,1)}, u32[]{:S(2)}) copy-start(bf16[4096,128]{1,0:T(8,128)(2,1)} %all-gather.3.cloned.1.call-done) | copy-start | bytes 3145732
  59.7 1.1 %copy-start.2 = (bf16[384,1024]{1,0:T(8,128)(2,1)S(1)}, bf16[384,1024]{1,0:T(8,128)(2,1)}, u32[]{:S(2)}) copy-start(bf16[384,1024]{1,0:T(8,128)(2,1)} %pv_ref.3) | copy-start | bytes 2359300
  60.9 1.0 copy-start.3
  61.9 1.0 copy-start.4
  68.8 8.1 %collective-permute-start.2 = (f32[16,136,128]{2,1,0:T(8,128)S(1)}, f32[16,136,128]{2,1,0:T(8,128)S(1)}, u32[]{:S(2)}, u32[]{:S(2)}) collective-permute-start(f32[16,136,128]{2,1,0:T(8,128)S(1)} %attend_other.1), channel_id=1, source_target_pairs={{0,1},{1,0},{2,3},{3,2},{4,5},{5,4},{6,7},{7,6},{8,9},{9,8},{10,11... | collective-permute-start | bytes 3342344 | tf_op jit(solution)/shard_map/ppermute | solution.py:252
Sparse Core Ops, SparseCore 0:
  11.7 46.7 all-gather.2

commit v2 on v1

--- a/solution.py
+++ b/solution.py
@@ -18,6 +18,7 @@
 LOG2E = 1.0 / math.log(2.0)
 EXPO = LOG2E / math.sqrt(DH)
 LIFT = 8192.0
+QLIFT = 2048.0
 
 bf16 = jnp.bfloat16
 f32 = jnp.float32
@@ -27,44 +28,49 @@
 ANY = pl.BlockSpec(memory_space=pl.ANY)
 
 
-def prepare_kernel(q_ref, nk_ref, nv_ref, len_ref, table_ref, qt_ref, nkp_ref, nvp_ref, meta_ref, rows_ref, sem):
+def prepare_kernel(
+    q_ref, nk_ref, nv_ref, len_ref, table_ref, qt_ref, nkp_ref, nvp_ref, meta_ref,
+    q_s, nk_s, nv_s, len_s, table_s, sems,
+):
     req = lax.axis_index("req")
     pre = lax.axis_index("prefix")
-    pair_rows = rows_ref.shape[0]
-    n_pre = pair_rows // 4
+    n_pre = lax.axis_size("prefix")
+    pair_rows = 4 * n_pre
+    per_line = 128 // pair_rows
     pair = req // 2
     side = req % 2
-    copy = pltpu.make_async_copy(
-        table_ref.at[pl.ds(pl.multiple_of(pair * pair_rows, pair_rows), pair_rows), :], rows_ref, sem
-    )
-    copy.start()
+    line = pair // per_line
+    first = (pair % per_line) * pair_rows
+    lanes = pl.ds(pl.multiple_of(line * 128, 128), 128)
+    sources = (len_ref, table_ref.at[:, lanes], q_ref, nk_ref, nv_ref)
+    copies = [
+        pltpu.make_async_copy(src, dst, sems.at[i])
+        for i, (src, dst) in enumerate(zip(sources, (len_s, table_s, q_s, nk_s, nv_s)))
+    ]
+    for copy in copies:
+        copy.start()
+    for copy in copies:
+        copy.wait()
     pieces = []
-    steps = [q_ref[s].astype(f32) for s in range(2)]
+    steps = [q_s[s].astype(f32) * QLIFT for s in range(2)]
     for head in range(H):
         for s in range(2):
             pieces.append(steps[s][:, head * DH : (head + 1) * DH])
-    qt_ref[...] = jnp.concatenate(pieces, axis=0).astype(bf16)
-    for src, dst in ((nk_ref, nkp_ref), (nv_ref, nvp_ref)):
+    qt_ref[...] = jnp.concatenate(pieces, axis=0)
+    for src, dst in ((nk_s, nkp_ref), (nv_s, nvp_ref)):
         top = jnp.concatenate([src[0].astype(f32), src[1].astype(f32), jnp.zeros((12, KVH * DH), f32)], axis=0)
         dst[...] = jnp.zeros(dst.shape, bf16)
         dst[0:16, :] = top.astype(bf16)
-    lane = lax.broadcasted_iota(jnp.int32, (pair_rows, 128), 1)
-    row = lax.broadcasted_iota(jnp.int32, (pair_rows, 128), 0)
-    per_line = 128 // pair_rows
-    line = len_ref[pl.ds(pair // per_line, 1), :]
-    at = row + (pair % per_line) * pair_rows
-    lengths = jnp.sum(jnp.where(lane == at, jnp.broadcast_to(line, (pair_rows, 128)), 0), axis=1, keepdims=True)
-    copy.wait()
-    blocks = rows_ref.shape[1]
-    table = rows_ref[...]
-    col = lax.broadcasted_iota(jnp.int32, (pair_rows, blocks), 1)
-    trow = lax.broadcasted_iota(jnp.int32, (pair_rows, blocks), 0)
-    left = jnp.broadcast_to(lengths, (pair_rows, blocks)) - col * BLK
+    table = table_s[...]
+    lane = lax.broadcasted_iota(jnp.int32, table.shape, 1) - first
+    block = lax.broadcasted_iota(jnp.int32, table.shape, 0)
+    left = jnp.broadcast_to(len_s[pl.ds(line, 1), :], table.shape) - block * BLK
+    usable = (left > 0) & (lane >= 0) & (lane < pair_rows)
     for n in range(4):
         holder = side if n < 2 else 1 - side
         slot = (holder * n_pre + pre) * 2 + n % 2
-        hit = (table == slot) & (left > 0)
-        owner = jnp.sum(jnp.where(hit, trow, 0)) - side * (pair_rows // 2)
+        hit = (table == slot) & usable
+        owner = jnp.sum(jnp.where(hit, lane, 0)) - side * (pair_rows // 2)
         live = jnp.sum(jnp.where(hit, jnp.minimum(left, BLK), 0))
         mine = (owner >= 0) & (owner < pair_rows // 2)
         owner = jnp.where(mine, owner, 0)
@@ -114,8 +120,8 @@
         extra = []
         for n in range(5):
             if n < 4:
+                dev = meta_ref[n, 0]
                 kr, vr = (ok_ref, ov_ref) if n < 2 else (xk_ref, xv_ref)
-                dev = meta_ref[n, 0]
                 k, v = kr[n % 2, :, lanes], vr[n % 2, :, lanes]
                 live = (row_req == meta_ref[n, 1]) & (lane < meta_ref[n, 2])
             else:
@@ -193,14 +199,14 @@
                 out_ref[s, :, head * DH : (head + 1) * DH] = o[r : r + 2, :].astype(bf16)
 
 
-def call(kernel, out_shape, ins, out_specs=VM, scratch=(), flops=0, moved=0, name=None):
+def call(kernel, out_shape, ins, out_specs=VM, scratch=(), flops=0, moved=0, name=None, room=40):
     return pl.pallas_call(
         kernel,
         out_shape=out_shape,
         in_specs=ins,
         out_specs=out_specs,
         scratch_shapes=list(scratch),
-        compiler_params=pltpu.CompilerParams(vmem_limit_bytes=40 * 1024 * 1024),
+        compiler_params=pltpu.CompilerParams(vmem_limit_bytes=room * 1024 * 1024),
         cost_estimate=pl.CostEstimate(flops=flops, bytes_accessed=moved, transcendentals=0),
         name=name,
     )
@@ -227,13 +233,22 @@
     sds = jax.ShapeDtypeStruct
     own, nk, nv, meta = call(
         prepare_kernel,
-        (sds((4 * H, DH), bf16), sds((BLK, KVH * DH), bf16), sds((BLK, KVH * DH), bf16), sds((4, 3), jnp.int32)),
-        [VM, VM, VM, VM, ANY],
+        (sds((4 * H, DH), f32), sds((BLK, KVH * DH), bf16), sds((BLK, KVH * DH), bf16), sds((4, 3), jnp.int32)),
+        [ANY] * 5,
         (VM, VM, VM, SM),
-        [pltpu.VMEM((pair_rows, block_table.shape[1]), jnp.int32), pltpu.SemaphoreType.DMA],
+        [
+            pltpu.VMEM(queries.shape, bf16),
+            pltpu.VMEM(new_keys.shape, bf16),
+            pltpu.VMEM(new_values.shape, bf16),
+            pltpu.VMEM((suffix_lengths.size // 128, 128), jnp.int32),
+            pltpu.VMEM((block_table.shape[1], 128), jnp.int32),
+            pltpu.SemaphoreType.DMA((5,)),
+        ],
         name="prepare",
-    )(queries, new_keys, new_values, suffix_lengths.reshape(-1, 128), block_table)
-    group = lax.all_gather(own, "prefix", axis=0)
+        room=62,
+    )(queries, new_keys, new_values, suffix_lengths.reshape(-1, 128), block_table.T)
+    group = lax.all_gather(own.astype(jnp.float16), "prefix", axis=0)
+    group = (group.astype(f32) * (1.0 / QLIFT)).astype(bf16)
     partial = sds((n_pre, 136, DH), f32)
     state = pltpu.VMEM((n_pre, 32, DH), f32)
 
@@ -243,7 +258,12 @@
             partial,
             [VM] * 9 + [SM],
             VM,
-            [state, state, state, pltpu.VMEM((n_pre, 128, DH), f32)],
+            [
+                state,
+                state,
+                state,
+                pltpu.VMEM((n_pre, 128, DH), f32),
+            ],
             flops=800_000_000,
             moved=6_000_000,
             name="attend_other" if flip else "attend_own",

time: 109 us -> 72.4 us (0.66)
  waiting for transfers between devices: 41 us -> 0.01 us
  blocking collectives: 22.9 us -> 45.9 us
  between operations: 13.5 us -> 0.15 us
  local copies, waits for them, and re-layouts: 8.46 us -> 1.23 us
  other arithmetic: 0.15 us -> 1.3 us
    all_gather x1 -> x0, waiting for transfers between devices: 24.7 us -> none  [per_device(): group = lax.all_gather(own, 'prefix', axis=0)]
    all_gather x0 -> x1, blocking collectives: none -> 24.7 us  [per_device(): group = lax.all_gather(own.astype(jnp.float16), 'prefix', axis=0)]
    ppermute x1, waiting for transfers between devices: 11.2 us -> 0.01 us  [per_device(): far_values = lax.ppermute(pool_values, 'req', swap)]
    unnamed x19 -> x14, local copies, waits for them, and re-layouts: 8.46 us -> 1.23 us
    ppermute x1, waiting for transfers between devices: 5.03 us -> 0.01 us  [per_device(): far_keys = lax.ppermute(pool_keys, 'req', swap)]
    all_to_all x1, blocking collectives: 22.9 us -> 21.2 us  [per_device(): lax.all_to_all(merged.astype(jnp.float16), 'prefix', 0, 0, tiled=True)]
    convert_element_type x0 -> x2, other arithmetic: none -> 1.15 us  [the longest x1 0.92 us: per_device(): group = lax.all_gather(own.astype(jnp.float16), 'prefix', axis=0)]
  transfers between devices with their start and end apart: 4 -> 3, of which waited for: 3 -> 0; matrix products, arithmetic and copies ran while one was open for 0% -> 2% of each run, Pallas kernels for 5% -> 11%
where the time goes in v2:
time: 72.4 us; the launch traced here: 72.1 us
  blocking collectives  45.9 us (63%)
  Pallas kernels  15.6 us (22%)
  starting transfers between devices  7.93 us (11%)
  other arithmetic  1.3 us (2%)
  local copies, waits for them, and re-layouts  1.23 us (2%)
    all_gather x1, blocking collectives, per_device(): group = lax.all_gather(own.astype(jnp.float16), 'prefix', axis=0)  24.7 us
    all_to_all x1, blocking collectives, per_device(): lax.all_to_all(merged.astype(jnp.float16), 'prefix', 0, 0, tiled=True)  21.2 us
    pallas_call x2, Pallas kernels, attend(): call(functools.partial(attend_kernel, flip), partial, [VM] * 9 + [SM], VM...  11.7 us
    ppermute x1, starting transfers between devices, per_device(): far_keys = lax.ppermute(pool_keys, 'req', swap)  3.94 us
    ppermute x1, starting transfers between devices, per_device(): theirs = lax.ppermute(attend(True), 'prefix', core)  2.07 us
    pallas_call x1, Pallas kernels, per_device(): call(prepare_kernel, (sds((4 * H, DH), f32), sds((BLK, KVH * DH), bf16),...  1.93 us
    ppermute x1, starting transfers between devices, per_device(): far_values = lax.ppermute(pool_values, 'req', swap)  1.92 us
  transfers between devices with their start and end apart: 3, of which 0 were waited for; matrix products, arithmetic and copies ran while one was open for 2% of the time, Pallas kernels for 11%

profile of v2, /device:TPU:1, one launch (start us, length us, event | category | flops | bytes accessed | tf_op | source)
XLA Modules:
  0.0 72.1 jit_solution(12667086847029217856)
XLA Ops:
  0.0 3.9 %collective-permute-start = (bf16[2,128,1024]{2,1,0:T(8,128)(2,1)}, bf16[2,128,1024]{2,1,0:T(8,128)(2,1)S(1)}, u32[]{:S(2)}, u32[]{:S(2)}) collective-permute-start(bf16[2,128,1024]{2,1,0:T(8,128)(2,1)} %ok_ref.3), channel_id=1, source_target_pairs={{0,16},{16,0},{32,48},{48,32},{64,80},{80,64},{96,112},{112,96},{1... | collective-permute-start | bytes 1572872 | tf_op jit(solution)/shard_map/ppermute | solution.py:231
  3.9 1.9 %collective-permute-start.1 = (bf16[2,128,1024]{2,1,0:T(8,128)(2,1)}, bf16[2,128,1024]{2,1,0:T(8,128)(2,1)S(1)}, u32[]{:S(2)}, u32[]{:S(2)}) collective-permute-start(bf16[2,128,1024]{2,1,0:T(8,128)(2,1)} %ov_ref.3), channel_id=1, source_target_pairs={{0,16},{16,0},{32,48},{48,32},{64,80},{80,64},{96,112},{112,96},{1... | collective-permute-start | bytes 1572872 | tf_op jit(solution)/shard_map/ppermute | solution.py:232
  5.9 1.9 %prepare.1 = (f32[256,128]{1,0:T(8,128)}, bf16[128,1024]{1,0:T(8,128)(2,1)}, bf16[128,1024]{1,0:T(8,128)(2,1)}, s32[4,3]{1,0:T(4,128)}) custom-call(bf16[2,2,8192]{2,1,0:T(2,128)(2,1)} %q_ref.1, bf16[2,2,1024]{2,1,0:T(2,128)(2,1)} %nk_ref.1, bf16[2,2,1024]{2,1,0:T(2,128)(2,1)} %nv_ref.1, s32[8,128]{1,0:T(8,128)} %bitcast.6, s32[16,1024]{1,0:T(8,128)} %bitcast.5), custom_call_target="tpu_custom_call" | custom-call | tf_op jit(solution)/shard_map/prepare/pallas_call | solution.py:234
  7.8 0.9 %convert_element_type.15 = f16[256,128]{1,0:T(8,128)(2,1)S(1)} convert(f32[256,128]{1,0:T(8,128)} %get-tuple-element.9) | non-fusion elementwise | flops 32768 | bytes 196608 | tf_op jit(solution)/shard_map/convert_element_type | solution.py:250
  8.7 0.0 copy-start.3
  8.7 0.0 copy-start.4
  8.8 0.0 copy-start.5
  8.8 24.7 %all-gather.2 = f16[4096,128]{1,0:T(8,128)(2,1)S(1)} all-gather(f16[256,128]{1,0:T(8,128)(2,1)S(1)} %convert_element_type.15), channel_id=2, replica_groups=mesh['req'=32,'prefix'=16] {'prefix'}, dimensions={0}, use_global_device_ids=true | all-gather | bytes 1114112 | tf_op jit(solution)/shard_map/all_gather | solution.py:250
  33.4 0.0 copy-start
  33.4 0.0 copy-start.1
  33.4 0.0 copy-start.2
  33.4 0.0 copy-start.6
  33.4 0.2 multiply_convert_fusion
  33.7 0.0 collective-permute-done.xk_ref
  33.7 0.0 collective-permute-done.1.xv_ref
  33.7 0.0 copy-done.3
  33.7 0.0 copy-done.4
  33.7 0.0 copy-done.5
  33.7 0.8 %copy-done = bf16[384,1024]{1,0:T(8,128)(2,1)S(1)} copy-done((bf16[384,1024]{1,0:T(8,128)(2,1)S(1)}, bf16[384,1024]{1,0:T(8,128)(2,1)}, u32[]{:S(2)}) %copy-start) | copy-done | bytes 786456
  34.6 0.2 copy-done.1
  34.8 0.1 copy-done.2
  34.9 0.0 copy-done.6
  34.9 5.9 %attend_other.1 = f32[16,136,128]{2,1,0:T(8,128)S(1)} custom-call(bf16[16,256,128]{2,1,0:T(8,128)(2,1)S(1)} %bitcast.3, bf16[384,1024]{1,0:T(8,128)(2,1)S(1)} %copy-done, bf16[384,1024]{1,0:T(8,128)(2,1)S(1)} %copy-done.1, bf16[2,128,1024]{2,1,0:T(8,128)(2,1)S(1)} %copy-done.2, bf16[2,128,1024]{2,1,0:T(8,128)(2,1)S(1)} %copy-done.3, ...), custom_call_target="tpu_custom_call" | custom-call | flops 800000000 | bytes 6000000 | tf_op jit(solution)/shard_map/attend_other/pallas_call | solution.py:256
  40.8 2.1 %collective-permute-start.2 = (f32[16,136,128]{2,1,0:T(8,128)S(1)}, f32[16,136,128]{2,1,0:T(8,128)S(1)}, u32[]{:S(2)}, u32[]{:S(2)}) collective-permute-start(f32[16,136,128]{2,1,0:T(8,128)S(1)} %attend_other.1), channel_id=1, source_target_pairs={{0,1},{1,0},{2,3},{3,2},{4,5},{5,4},{6,7},{7,6},{8,9},{9,8},{10,11... | collective-permute-start | bytes 3342344 | tf_op jit(solution)/shard_map/ppermute | solution.py:272
  42.9 5.9 %attend_own.1.a_ref = f32[16,136,128]{2,1,0:T(8,128)S(1)} custom-call(bf16[16,256,128]{2,1,0:T(8,128)(2,1)S(1)} %bitcast.4, bf16[384,1024]{1,0:T(8,128)(2,1)S(1)} %copy-done, bf16[384,1024]{1,0:T(8,128)(2,1)S(1)} %copy-done.1, bf16[2,128,1024]{2,1,0:T(8,128)(2,1)S(1)} %copy-done.2, bf16[2,128,1024]{2,1,0:T(8,128)(2,1)S(1)} %copy-done.3, ...), custom_call_target="tpu_custom_call" | custom-call | flops 800000000 | bytes 6000000 | tf_op jit(solution)/shard_map/attend_own/pallas_call | solution.py:256
  48.8 0.0 collective-permute-done.2.b_ref
  48.8 0.8 %core_merge.1 = f32[16,136,128]{2,1,0:T(8,128)S(1)} custom-call(f32[16,136,128]{2,1,0:T(8,128)S(1)} %attend_own.1.a_ref, f32[16,136,128]{2,1,0:T(8,128)S(1)} %collective-permute-done.2.b_ref), custom_call_target="tpu_custom_call" | custom-call | bytes 4000000 | tf_op jit(solution)/shard_map/core_merge/pallas_call | solution.py:274
  49.5 0.1 convert_element_type.18
  49.6 21.2 %all_to_all.5 = f16[16,136,128]{2,1,0:T(8,128)(2,1)S(1)} all-to-all(f16[16,136,128]{2,1,0:T(8,128)(2,1)S(1)} %convert_element_type.18), channel_id=1, replica_groups=mesh['req'=32,'prefix'=16] {'prefix'}, dimensions={0} | all-to-all | bytes 1114112 | tf_op jit(solution)/shard_map/all_to_all | solution.py:275
  70.9 0.1 convert_element_type.19.z_ref
  70.9 1.1 %final.1 = bf16[2,2,8192]{2,1,0:T(2,128)(2,1)} custom-call(f32[16,136,128]{2,1,0:T(8,128)S(1)} %convert_element_type.19.z_ref), custom_call_target="tpu_custom_call" | custom-call | bytes 1000000 | tf_op jit(solution)/shard_map/final/pallas_call | solution.py:276
Async XLA Ops:
  0.0 33.7 %collective-permute-start = (bf16[2,128,1024]{2,1,0:T(8,128)(2,1)}, bf16[2,128,1024]{2,1,0:T(8,128)(2,1)S(1)}, u32[]{:S(2)}, u32[]{:S(2)}) collective-permute-start(bf16[2,128,1024]{2,1,0:T(8,128)(2,1)} %ok_ref.3), channel_id=1, source_target_pairs={{0,16},{16,0},{32,48},{48,32},{64,80},{80,64},{96,112},{112,96},{1... | collective-permute-start | bytes 1572872 | tf_op jit(solution)/shard_map/ppermute | solution.py:231
  3.9 29.7 %collective-permute-start.1 = (bf16[2,128,1024]{2,1,0:T(8,128)(2,1)}, bf16[2,128,1024]{2,1,0:T(8,128)(2,1)S(1)}, u32[]{:S(2)}, u32[]{:S(2)}) collective-permute-start(bf16[2,128,1024]{2,1,0:T(8,128)(2,1)} %ov_ref.3), channel_id=1, source_target_pairs={{0,16},{16,0},{32,48},{48,32},{64,80},{80,64},{96,112},{112,96},{1... | collective-permute-start | bytes 1572872 | tf_op jit(solution)/shard_map/ppermute | solution.py:232
  8.7 25.0 %copy-start.3 = (bf16[2,128,1024]{2,1,0:T(8,128)(2,1)S(1)}, bf16[2,128,1024]{2,1,0:T(8,128)(2,1)}, u32[]{:S(2)}) copy-start(bf16[2,128,1024]{2,1,0:T(8,128)(2,1)} %ov_ref.3) | copy-start | bytes 1572868
  8.7 25.0 %copy-start.4 = (bf16[128,1024]{1,0:T(8,128)(2,1)S(1)}, bf16[128,1024]{1,0:T(8,128)(2,1)}, u32[]{:S(2)}) copy-start(bf16[128,1024]{1,0:T(8,128)(2,1)} %get-tuple-element.10.nk_ref) | copy-start | bytes 786436
  8.8 25.0 %copy-start.5 = (bf16[128,1024]{1,0:T(8,128)(2,1)S(1)}, bf16[128,1024]{1,0:T(8,128)(2,1)}, u32[]{:S(2)}) copy-start(bf16[128,1024]{1,0:T(8,128)(2,1)} %get-tuple-element.11.nv_ref) | copy-start | bytes 786436
  33.4 1.1 %copy-start = (bf16[384,1024]{1,0:T(8,128)(2,1)S(1)}, bf16[384,1024]{1,0:T(8,128)(2,1)}, u32[]{:S(2)}) copy-start(bf16[384,1024]{1,0:T(8,128)(2,1)} %pk_ref.3) | copy-start | bytes 2359300
  33.4 1.4 %copy-start.1 = (bf16[384,1024]{1,0:T(8,128)(2,1)S(1)}, bf16[384,1024]{1,0:T(8,128)(2,1)}, u32[]{:S(2)}) copy-start(bf16[384,1024]{1,0:T(8,128)(2,1)} %pv_ref.3) | copy-start | bytes 2359300
  33.4 1.5 %copy-start.2 = (bf16[2,128,1024]{2,1,0:T(8,128)(2,1)S(1)}, bf16[2,128,1024]{2,1,0:T(8,128)(2,1)}, u32[]{:S(2)}) copy-start(bf16[2,128,1024]{2,1,0:T(8,128)(2,1)} %ok_ref.3) | copy-start | bytes 1572868
  33.4 1.5 %copy-start.6 = (s32[4,3]{1,0:T(4,128)S(1)}, s32[4,3]{1,0:T(4,128)}, u32[]{:S(2)}) copy-start(s32[4,3]{1,0:T(4,128)} %get-tuple-element.12.meta_ref) | copy-start | bytes 148
  40.8 8.0 %collective-permute-start.2 = (f32[16,136,128]{2,1,0:T(8,128)S(1)}, f32[16,136,128]{2,1,0:T(8,128)S(1)}, u32[]{:S(2)}, u32[]{:S(2)}) collective-permute-start(f32[16,136,128]{2,1,0:T(8,128)S(1)} %attend_other.1), channel_id=1, source_target_pairs={{0,1},{1,0},{2,3},{3,2},{4,5},{5,4},{6,7},{7,6},{8,9},{9,8},{10,11... | collective-permute-start | bytes 3342344 | tf_op jit(solution)/shard_map/ppermute | solution.py:272

commit v3 on v2

--- a/solution.py
+++ b/solution.py
@@ -80,8 +80,7 @@
 
 
 def attend_kernel(
-    flip, q_ref, pk_ref, pv_ref, ok_ref, ov_ref, xk_ref, xv_ref, nk_ref, nv_ref, meta_ref,
-    out_ref, m_s, t_s, a_s, l_s,
+    flip, q_ref, pk_ref, pv_ref, ok_ref, ov_ref, xk_ref, xv_ref, nk_ref, nv_ref, meta_ref, out_ref, m_s,
 ):
     pre = lax.axis_index("prefix")
     half = pre % 2
@@ -89,114 +88,117 @@
         half = 1 - half
     n_dev = q_ref.shape[0]
     rows = n_dev * 32
-    ones = jnp.ones((BLK, DH), bf16)
-    lane = lax.broadcasted_iota(jnp.int32, (32, BLK), 1)
-    row = lax.broadcasted_iota(jnp.int32, (32, BLK), 0)
-    row_req = row % 2
-    row_step = row // 2 % 2
-    new_live = (lane < 4) & (lane % 2 == row_req) & (lane // 2 <= row_step)
+    ones = jnp.ones((16, BLK), bf16)
+    key = lax.broadcasted_iota(jnp.int32, (BLK, DH), 0)
+    lane = lax.broadcasted_iota(jnp.int32, (BLK, DH), 1)
+    lane_dev, lane_req, lane_step = lane // 32, lane % 2, lane // 2 % 2
     n_blocks = pk_ref.shape[0] // BLK
+    masks = []
+    for n in range(4):
+        limit = jnp.where((lane_dev == meta_ref[n, 0] % 4) & (lane_req == meta_ref[n, 1]), meta_ref[n, 2], 0)
+        masks.append(key < limit)
+    masks.append((lane_dev == pre % 4) & (key < 4) & (key % 2 == lane_req) & (key // 2 <= lane_step))
     for i in range(HALF):
         kvh = half * HALF + i
         lanes = pl.ds(pl.multiple_of(kvh * DH, DH), DH)
         qrows = pl.ds(pl.multiple_of(kvh * 32, 32), 32)
         q = q_ref[:, qrows, :].reshape(rows, DH)
+        scores = lax.dot_general(pk_ref[:, lanes], q, NT, preferred_element_type=f32)
         peaks, outs = [], []
         for b in range(n_blocks):
             span = slice(b * BLK, (b + 1) * BLK)
-            s = lax.dot_general(q, pk_ref[span, lanes], NT, preferred_element_type=f32)
-            peak = jnp.max(s, axis=1, keepdims=True)
+            s = scores[span]
+            peak = jnp.max(s, axis=0, keepdims=True)
             w = jnp.exp2((s - peak) * EXPO).astype(bf16)
-            v = jnp.concatenate([pv_ref[span, lanes], ones], axis=1)
+            v = jnp.concatenate([pv_ref[span, lanes].T, ones], axis=0)
             peaks.append(peak)
-            outs.append(jnp.dot(w, v, preferred_element_type=f32))
+            outs.append(jnp.dot(v, w, preferred_element_type=f32)[0:136])
         top = functools.reduce(jnp.maximum, peaks)
         both = 0.0
         for peak, o in zip(peaks, outs):
             both = both + jnp.exp2((peak - top) * EXPO) * o
-        m_s[...] = jnp.broadcast_to(top, (rows, DH)).reshape(n_dev, 32, DH)
-        a_s[...] = both[:, :DH].reshape(n_dev, 32, DH)
-        t_s[...] = both[:, DH:].reshape(n_dev, 32, DH)
+        m_s[i : i + 1, :] = top
+        out_ref[i] = both
         extra = []
         for n in range(5):
             if n < 4:
-                dev = meta_ref[n, 0]
                 kr, vr = (ok_ref, ov_ref) if n < 2 else (xk_ref, xv_ref)
                 k, v = kr[n % 2, :, lanes], vr[n % 2, :, lanes]
-                live = (row_req == meta_ref[n, 1]) & (lane < meta_ref[n, 2])
+                quad = meta_ref[n, 0] // 4
             else:
-                dev = pre
                 k, v = nk_ref[:, lanes], nv_ref[:, lanes]
-                live = new_live
-            s = lax.dot_general(q_ref[dev, qrows, :], k, NT, preferred_element_type=f32)
-            s = jnp.where(live, s, NEG)
-            peak = jnp.max(s, axis=1, keepdims=True)
-            w = jnp.where(live, jnp.exp2((s - peak) * EXPO), 0.0).astype(bf16)
-            o = jnp.dot(w, jnp.concatenate([v, ones], axis=1), preferred_element_type=f32)
-            extra.append((dev, peak, o))
-        for dev, peak, o in extra:
-            old = m_s[dev]
+                quad = pre // 4
+            qn = q_ref[pl.ds(quad * 4, 4), qrows, :].reshape(DH, DH)
+            s = lax.dot_general(k, qn, NT, preferred_element_type=f32)
+            s = jnp.where(masks[n], s, NEG)
+            peak = jnp.max(s, axis=0, keepdims=True)
+            w = jnp.where(masks[n], jnp.exp2((s - peak) * EXPO), 0.0).astype(bf16)
+            o = jnp.dot(jnp.concatenate([v.T, ones], axis=0), w, preferred_element_type=f32)[0:136]
+            extra.append((pl.ds(pl.multiple_of(quad * DH, DH), DH), peak, o))
+        for at, peak, o in extra:
+            old = m_s[i : i + 1, at]
             new = jnp.maximum(old, peak)
-            fa = jnp.exp2((old - new) * EXPO)
-            fb = jnp.exp2((peak - new) * EXPO)
-            m_s[dev] = new
-            a_s[dev] = a_s[dev] * fa + o[:, :DH] * fb
-            t_s[dev] = t_s[dev] * fa + o[:, DH:] * fb
-        total = t_s[...]
-        out_ref[:, i * 32 : (i + 1) * 32, :] = a_s[...] / total
-        l_s[:, i * 32 : (i + 1) * 32, :] = m_s[...] * EXPO + jnp.log(total) * LOG2E
-    eye = lax.broadcasted_iota(jnp.int32, (DH, DH), 0) == lax.broadcasted_iota(jnp.int32, (DH, DH), 1)
-    for dev in range(n_dev):
-        line = jnp.sum(jnp.where(eye, l_s[dev], 0.0), axis=0, keepdims=True)
-        out_ref[dev, 128:136, :] = jnp.broadcast_to(line, (8, DH))
-
-
-def columns(lines):
-    pad = jnp.zeros((DH - lines.shape[0], DH), f32)
-    return jnp.concatenate([lines, pad], axis=0).T
+            m_s[i : i + 1, at] = new
+            out_ref[i, :, at] = (
+                out_ref[i, :, at] * jnp.exp2((old - new) * EXPO) + o * jnp.exp2((peak - new) * EXPO)
+            )
+        total = out_ref[i, 128:129, :]
+        out_ref[i, 0:128, :] = out_ref[i, 0:128, :] * (1.0 / total)
+        lse = m_s[i : i + 1, :] * EXPO + jnp.log(total) * LOG2E
+        out_ref[i, 128:136, :] = jnp.broadcast_to(lse, (8, rows))
 
 
 def core_merge_kernel(a_ref, b_ref, out_ref):
-    n_dev = a_ref.shape[0]
-    la = a_ref[:, 128:136, :][:, 0, :]
-    lb = b_ref[:, 128:136, :][:, 0, :]
-    top = jnp.maximum(la, lb)
-    wa = jnp.exp2(la - top)
-    wb = jnp.exp2(lb - top)
-    total = wa + wb
-    lse = top + jnp.log(total) * LOG2E
-    hi = lse.astype(bf16).astype(f32)
-    mid = (lse - hi).astype(bf16).astype(f32)
-    low = lse - hi - mid
-    ca = columns(wa * (LIFT / total))
-    cb = columns(wb * (LIFT / total))
-    for dev in range(n_dev):
-        out_ref[dev, 0:128, :] = (
-            a_ref[dev, 0:128, :] * ca[:, dev : dev + 1] + b_ref[dev, 0:128, :] * cb[:, dev : dev + 1]
-        )
-        out_ref[dev, 128:136, :] = jnp.concatenate(
-            [hi[dev : dev + 1], mid[dev : dev + 1], low[dev : dev + 1], jnp.zeros((5, DH), f32)], axis=0
-        )
-
-
-def final_kernel(z_ref, out_ref):
+    rows = a_ref.shape[2]
+    high, low = [], []
+    for i in range(HALF):
+        la = a_ref[i, 128:129, :]
+        lb = b_ref[i, 128:129, :]
+        top = jnp.maximum(la, lb)
+        wa = jnp.exp2(la - top)
+        wb = jnp.exp2(lb - top)
+        total = wa + wb
+        scale = LIFT / total
+        o = a_ref[i, 0:128, :] * (wa * scale) + b_ref[i, 0:128, :] * (wb * scale)
+        for quad in range(rows // DH):
+            out_ref[quad * 4 : quad * 4 + 4, i * 32 : (i + 1) * 32, :] = (
+                o[:, quad * DH : (quad + 1) * DH].T.reshape(4, 32, DH)
+            )
+        lse = top + jnp.log(total) * LOG2E
+        far = lse * 8193.0
+        head = far - (far - lse)
+        high.append(head)
+        low.append(lse - head)
+    parts = jnp.concatenate(high + low, axis=0)
+    for dev in range(rows // 32):
+        out_ref[dev, 128:136, :] = parts[:, dev // 4 * DH : (dev // 4 + 1) * DH]
+
+
+def final_kernel(z_ref, out_ref, w_s):
     n_dev = z_ref.shape[0]
+    pre = lax.axis_index("prefix")
+    mine = pl.ds(pl.multiple_of(pre % 4 * 32, 32), 32)
     for c in range(2):
-        lines = []
+        lses = []
         for src in range(c, n_dev, 2):
             parts = z_ref[src, 128:136, :]
-            lines.append(jnp.sum(parts, axis=0, keepdims=True))
-        lse = jnp.concatenate(lines, axis=0)
-        w = jnp.exp2(lse - jnp.max(lse, axis=0, keepdims=True))
-        w = columns(w / (LIFT * jnp.sum(w, axis=0, keepdims=True)))
-        o = 0.0
-        for y, src in enumerate(range(c, n_dev, 2)):
-            o = o + z_ref[src, 0:128, :] * w[:, y : y + 1]
-        for h in range(H // 2):
-            head = c * (H // 2) + h
-            for s in range(2):
-                r = h * 4 + s * 2
-                out_ref[s, :, head * DH : (head + 1) * DH] = o[r : r + 2, :].astype(bf16)
+            lses.append(parts[0:4] + parts[4:8])
+        top = functools.reduce(jnp.maximum, lses)
+        weights = [jnp.exp2(lse - top) for lse in lses]
+        scale = 1.0 / (LIFT * sum(weights))
+        lines = [w * scale for w in weights]
+        lines.append(jnp.zeros((DH - 2 * n_dev, DH), f32))
+        w_s[c] = jnp.concatenate(lines, axis=0).T
+        columns = w_s[c, mine, :]
+        for i in range(HALF):
+            o = 0.0
+            for y, src in enumerate(range(c, n_dev, 2)):
+                o = o + z_ref[src, i * 32 : (i + 1) * 32, :] * columns[:, y * 4 + i : y * 4 + i + 1]
+            for g in range(GROUP):
+                head = (c * HALF + i) * GROUP + g
+                for s in range(2):
+                    r = g * 4 + s * 2
+                    out_ref[s, :, head * DH : (head + 1) * DH] = o[r : r + 2, :].astype(bf16)
 
 
 def call(kernel, out_shape, ins, out_specs=VM, scratch=(), flops=0, moved=0, name=None, room=40):
@@ -249,21 +251,15 @@
     )(queries, new_keys, new_values, suffix_lengths.reshape(-1, 128), block_table.T)
     group = lax.all_gather(own.astype(jnp.float16), "prefix", axis=0)
     group = (group.astype(f32) * (1.0 / QLIFT)).astype(bf16)
-    partial = sds((n_pre, 136, DH), f32)
-    state = pltpu.VMEM((n_pre, 32, DH), f32)
+    rows = n_pre * 32
 
     def attend(flip):
         return call(
             functools.partial(attend_kernel, flip),
-            partial,
+            sds((HALF, 136, rows), f32),
             [VM] * 9 + [SM],
             VM,
-            [
-                state,
-                state,
-                state,
-                pltpu.VMEM((n_pre, 128, DH), f32),
-            ],
+            [pltpu.VMEM((HALF, rows), f32)],
             flops=800_000_000,
             moved=6_000_000,
             name="attend_other" if flip else "attend_own",
@@ -271,11 +267,19 @@
 
     theirs = lax.ppermute(attend(True), "prefix", core)
     mine = attend(False)
-    merged = call(core_merge_kernel, partial, [VM, VM], moved=4_000_000, name="core_merge")(mine, theirs)
+    merged = call(core_merge_kernel, sds((n_pre, 136, DH), f32), [VM, VM], moved=4_000_000, name="core_merge")(
+        mine, theirs
+    )
     spread = lax.all_to_all(merged.astype(jnp.float16), "prefix", 0, 0, tiled=True)
-    return call(final_kernel, sds((2, 2, H * DH), bf16), [VM], moved=1_000_000, name="final")(
-        spread.astype(f32)
-    )
+    return call(
+        final_kernel,
+        sds((2, 2, H * DH), bf16),
+        [VM],
+        VM,
+        [pltpu.VMEM((2, DH, DH), f32)],
+        moved=1_000_000,
+        name="final",
+    )(spread.astype(f32))
 
 
 def solution(mesh):

time: 72.4 us -> 68.7 us (0.949)
  Pallas kernels: 15.6 us -> 11.8 us
    pallas_call x4, Pallas kernels: 13.6 us -> 9.92 us  [the longest x2 8.37 us: attend(): call(functools.partial(attend_kernel, flip), sds((HALF, 136, rows), f32),...]
  transfers between devices with their start and end apart: 3 -> 3, of which waited for: 0 -> 0; matrix products, arithmetic and copies ran while one was open for 2% -> 2% of each run, Pallas kernels for 11% -> 9%
where the time goes in v3:
time: 68.7 us; the launch traced here: 68.4 us
  blocking collectives  45.9 us (67%)
  Pallas kernels  11.8 us (17%)
  starting transfers between devices  7.93 us (12%)
  other arithmetic  1.31 us (2%)
  local copies, waits for them, and re-layouts  1.23 us (2%)
    all_gather x1, blocking collectives, per_device(): group = lax.all_gather(own.astype(jnp.float16), 'prefix', axis=0)  24.7 us
    all_to_all x1, blocking collectives, per_device(): lax.all_to_all(merged.astype(jnp.float16), 'prefix', 0, 0, tiled=True)  21.2 us
    pallas_call x2, Pallas kernels, attend(): call(functools.partial(attend_kernel, flip), sds((HALF, 136, rows), f32),...  8.37 us
    ppermute x1, starting transfers between devices, per_device(): far_keys = lax.ppermute(pool_keys, 'req', swap)  3.94 us
    ppermute x1, starting transfers between devices, per_device(): theirs = lax.ppermute(attend(True), 'prefix', core)  2.07 us
    pallas_call x1, Pallas kernels, per_device(): call(prepare_kernel, (sds((4 * H, DH), f32), sds((BLK, KVH * DH), bf16),...  1.93 us
    ppermute x1, starting transfers between devices, per_device(): far_values = lax.ppermute(pool_values, 'req', swap)  1.92 us
  transfers between devices with their start and end apart: 3, of which 0 were waited for; matrix products, arithmetic and copies ran while one was open for 2% of the time, Pallas kernels for 9%

profile of v3, /device:TPU:1, one launch (start us, length us, event | category | flops | bytes accessed | tf_op | source)
XLA Modules:
  0.0 68.4 jit_solution(2453328166961540936)
XLA Ops:
  0.0 3.9 %collective-permute-start = (bf16[2,128,1024]{2,1,0:T(8,128)(2,1)}, bf16[2,128,1024]{2,1,0:T(8,128)(2,1)S(1)}, u32[]{:S(2)}, u32[]{:S(2)}) collective-permute-start(bf16[2,128,1024]{2,1,0:T(8,128)(2,1)} %ok_ref.3), channel_id=1, source_target_pairs={{0,16},{16,0},{32,48},{48,32},{64,80},{80,64},{96,112},{112,96},{1... | collective-permute-start | bytes 1572872 | tf_op jit(solution)/shard_map/ppermute | solution.py:233
  3.9 1.9 %collective-permute-start.1 = (bf16[2,128,1024]{2,1,0:T(8,128)(2,1)}, bf16[2,128,1024]{2,1,0:T(8,128)(2,1)S(1)}, u32[]{:S(2)}, u32[]{:S(2)}) collective-permute-start(bf16[2,128,1024]{2,1,0:T(8,128)(2,1)} %ov_ref.3), channel_id=1, source_target_pairs={{0,16},{16,0},{32,48},{48,32},{64,80},{80,64},{96,112},{112,96},{1... | collective-permute-start | bytes 1572872 | tf_op jit(solution)/shard_map/ppermute | solution.py:234
  5.9 1.9 %prepare.1 = (f32[256,128]{1,0:T(8,128)}, bf16[128,1024]{1,0:T(8,128)(2,1)}, bf16[128,1024]{1,0:T(8,128)(2,1)}, s32[4,3]{1,0:T(4,128)}) custom-call(bf16[2,2,8192]{2,1,0:T(2,128)(2,1)} %q_ref.1, bf16[2,2,1024]{2,1,0:T(2,128)(2,1)} %nk_ref.1, bf16[2,2,1024]{2,1,0:T(2,128)(2,1)} %nv_ref.1, s32[8,128]{1,0:T(8,128)} %bitcast.6, s32[16,1024]{1,0:T(8,128)} %bitcast.5), custom_call_target="tpu_custom_call" | custom-call | tf_op jit(solution)/shard_map/prepare/pallas_call | solution.py:236
  7.8 0.9 %convert_element_type.15 = f16[256,128]{1,0:T(8,128)(2,1)S(1)} convert(f32[256,128]{1,0:T(8,128)} %get-tuple-element.9) | non-fusion elementwise | flops 32768 | bytes 196608 | tf_op jit(solution)/shard_map/convert_element_type | solution.py:252
  8.7 0.0 copy-start.3
  8.7 0.0 copy-start.4
  8.8 0.0 copy-start.5
  8.8 24.7 %all-gather.2 = f16[4096,128]{1,0:T(8,128)(2,1)S(1)} all-gather(f16[256,128]{1,0:T(8,128)(2,1)S(1)} %convert_element_type.15), channel_id=2, replica_groups=mesh['req'=32,'prefix'=16] {'prefix'}, dimensions={0}, use_global_device_ids=true | all-gather | bytes 1114112 | tf_op jit(solution)/shard_map/all_gather | solution.py:252
  33.4 0.0 copy-start
  33.4 0.0 copy-start.1
  33.4 0.0 copy-start.2
  33.4 0.0 copy-start.6
  33.4 0.2 multiply_convert_fusion
  33.7 0.0 collective-permute-done.xk_ref
  33.7 0.0 collective-permute-done.1.xv_ref
  33.7 0.0 copy-done.3
  33.7 0.0 copy-done.4
  33.7 0.0 copy-done.5
  33.7 0.8 %copy-done = bf16[384,1024]{1,0:T(8,128)(2,1)S(1)} copy-done((bf16[384,1024]{1,0:T(8,128)(2,1)S(1)}, bf16[384,1024]{1,0:T(8,128)(2,1)}, u32[]{:S(2)}) %copy-start) | copy-done | bytes 786456
  34.6 0.2 copy-done.1
  34.8 0.1 copy-done.2
  34.9 0.0 copy-done.6
  34.9 4.2 %attend_other.1 = f32[4,136,512]{2,1,0:T(8,128)S(1)} custom-call(bf16[16,256,128]{2,1,0:T(8,128)(2,1)S(1)} %bitcast.3, bf16[384,1024]{1,0:T(8,128)(2,1)S(1)} %copy-done, bf16[384,1024]{1,0:T(8,128)(2,1)S(1)} %copy-done.1, bf16[2,128,1024]{2,1,0:T(8,128)(2,1)S(1)} %copy-done.2, bf16[2,128,1024]{2,1,0:T(8,128)(2,1)S(1)} %copy-done.3, ...), custom_call_target="tpu_custom_call" | custom-call | flops 800000000 | bytes 6000000 | tf_op jit(solution)/shard_map/attend_other/pallas_call | solution.py:257
  39.1 2.1 %collective-permute-start.2 = (f32[4,136,512]{2,1,0:T(8,128)S(1)}, f32[4,136,512]{2,1,0:T(8,128)S(1)}, u32[]{:S(2)}, u32[]{:S(2)}) collective-permute-start(f32[4,136,512]{2,1,0:T(8,128)S(1)} %attend_other.1), channel_id=1, source_target_pairs={{0,1},{1,0},{2,3},{3,2},{4,5},{5,4},{6,7},{7,6},{8,9},{9,8},{10,11... | collective-permute-start | bytes 3342344 | tf_op jit(solution)/shard_map/ppermute | solution.py:268
  41.2 4.2 %attend_own.1.a_ref = f32[4,136,512]{2,1,0:T(8,128)S(1)} custom-call(bf16[16,256,128]{2,1,0:T(8,128)(2,1)S(1)} %bitcast.4, bf16[384,1024]{1,0:T(8,128)(2,1)S(1)} %copy-done, bf16[384,1024]{1,0:T(8,128)(2,1)S(1)} %copy-done.1, bf16[2,128,1024]{2,1,0:T(8,128)(2,1)S(1)} %copy-done.2, bf16[2,128,1024]{2,1,0:T(8,128)(2,1)S(1)} %copy-done.3, ...), custom_call_target="tpu_custom_call" | custom-call | flops 800000000 | bytes 6000000 | tf_op jit(solution)/shard_map/attend_own/pallas_call | solution.py:257
  45.4 0.0 collective-permute-done.2.b_ref
  45.4 0.4 core_merge.1
  45.8 0.1 convert_element_type.18
  45.9 21.2 %all_to_all.5 = f16[16,136,128]{2,1,0:T(8,128)(2,1)S(1)} all-to-all(f16[16,136,128]{2,1,0:T(8,128)(2,1)S(1)} %convert_element_type.18), channel_id=1, replica_groups=mesh['req'=32,'prefix'=16] {'prefix'}, dimensions={0} | all-to-all | bytes 1114112 | tf_op jit(solution)/shard_map/all_to_all | solution.py:273
  67.1 0.1 convert_element_type.19.z_ref
  67.2 1.2 %final.1 = bf16[2,2,8192]{2,1,0:T(2,128)(2,1)} custom-call(f32[16,136,128]{2,1,0:T(8,128)S(1)} %convert_element_type.19.z_ref), custom_call_target="tpu_custom_call" | custom-call | bytes 1000000 | tf_op jit(solution)/shard_map/final/pallas_call | solution.py:274
Async XLA Ops:
  0.0 33.7 %collective-permute-start = (bf16[2,128,1024]{2,1,0:T(8,128)(2,1)}, bf16[2,128,1024]{2,1,0:T(8,128)(2,1)S(1)}, u32[]{:S(2)}, u32[]{:S(2)}) collective-permute-start(bf16[2,128,1024]{2,1,0:T(8,128)(2,1)} %ok_ref.3), channel_id=1, source_target_pairs={{0,16},{16,0},{32,48},{48,32},{64,80},{80,64},{96,112},{112,96},{1... | collective-permute-start | bytes 1572872 | tf_op jit(solution)/shard_map/ppermute | solution.py:233
  3.9 29.7 %collective-permute-start.1 = (bf16[2,128,1024]{2,1,0:T(8,128)(2,1)}, bf16[2,128,1024]{2,1,0:T(8,128)(2,1)S(1)}, u32[]{:S(2)}, u32[]{:S(2)}) collective-permute-start(bf16[2,128,1024]{2,1,0:T(8,128)(2,1)} %ov_ref.3), channel_id=1, source_target_pairs={{0,16},{16,0},{32,48},{48,32},{64,80},{80,64},{96,112},{112,96},{1... | collective-permute-start | bytes 1572872 | tf_op jit(solution)/shard_map/ppermute | solution.py:234
  8.7 25.0 %copy-start.3 = (bf16[2,128,1024]{2,1,0:T(8,128)(2,1)S(1)}, bf16[2,128,1024]{2,1,0:T(8,128)(2,1)}, u32[]{:S(2)}) copy-start(bf16[2,128,1024]{2,1,0:T(8,128)(2,1)} %ov_ref.3) | copy-start | bytes 1572868
  8.7 25.0 %copy-start.4 = (bf16[128,1024]{1,0:T(8,128)(2,1)S(1)}, bf16[128,1024]{1,0:T(8,128)(2,1)}, u32[]{:S(2)}) copy-start(bf16[128,1024]{1,0:T(8,128)(2,1)} %get-tuple-element.10.nk_ref) | copy-start | bytes 786436
  8.8 25.0 %copy-start.5 = (bf16[128,1024]{1,0:T(8,128)(2,1)S(1)}, bf16[128,1024]{1,0:T(8,128)(2,1)}, u32[]{:S(2)}) copy-start(bf16[128,1024]{1,0:T(8,128)(2,1)} %get-tuple-element.11.nv_ref) | copy-start | bytes 786436
  33.4 1.1 %copy-start = (bf16[384,1024]{1,0:T(8,128)(2,1)S(1)}, bf16[384,1024]{1,0:T(8,128)(2,1)}, u32[]{:S(2)}) copy-start(bf16[384,1024]{1,0:T(8,128)(2,1)} %pk_ref.3) | copy-start | bytes 2359300
  33.4 1.4 %copy-start.1 = (bf16[384,1024]{1,0:T(8,128)(2,1)S(1)}, bf16[384,1024]{1,0:T(8,128)(2,1)}, u32[]{:S(2)}) copy-start(bf16[384,1024]{1,0:T(8,128)(2,1)} %pv_ref.3) | copy-start | bytes 2359300
  33.4 1.5 %copy-start.2 = (bf16[2,128,1024]{2,1,0:T(8,128)(2,1)S(1)}, bf16[2,128,1024]{2,1,0:T(8,128)(2,1)}, u32[]{:S(2)}) copy-start(bf16[2,128,1024]{2,1,0:T(8,128)(2,1)} %ok_ref.3) | copy-start | bytes 1572868
  33.4 1.5 %copy-start.6 = (s32[4,3]{1,0:T(4,128)S(1)}, s32[4,3]{1,0:T(4,128)}, u32[]{:S(2)}) copy-start(s32[4,3]{1,0:T(4,128)} %get-tuple-element.12.meta_ref) | copy-start | bytes 148
  39.1 6.3 %collective-permute-start.2 = (f32[4,136,512]{2,1,0:T(8,128)S(1)}, f32[4,136,512]{2,1,0:T(8,128)S(1)}, u32[]{:S(2)}, u32[]{:S(2)}) collective-permute-start(f32[4,136,512]{2,1,0:T(8,128)S(1)} %attend_other.1), channel_id=1, source_target_pairs={{0,1},{1,0},{2,3},{3,2},{4,5},{5,4},{6,7},{7,6},{8,9},{9,8},{10,11... | collective-permute-start | bytes 3342344 | tf_op jit(solution)/shard_map/ppermute | solution.py:268

commit v4 on v3

--- a/solution.py
+++ b/solution.py
@@ -59,8 +59,7 @@
     qt_ref[...] = jnp.concatenate(pieces, axis=0)
     for src, dst in ((nk_s, nkp_ref), (nv_s, nvp_ref)):
         top = jnp.concatenate([src[0].astype(f32), src[1].astype(f32), jnp.zeros((12, KVH * DH), f32)], axis=0)
-        dst[...] = jnp.zeros(dst.shape, bf16)
-        dst[0:16, :] = top.astype(bf16)
+        dst[...] = top.astype(bf16)
     table = table_s[...]
     lane = lax.broadcasted_iota(jnp.int32, table.shape, 1) - first
     block = lax.broadcasted_iota(jnp.int32, table.shape, 0)
@@ -80,7 +79,7 @@
 
 
 def attend_kernel(
-    flip, q_ref, pk_ref, pv_ref, ok_ref, ov_ref, xk_ref, xv_ref, nk_ref, nv_ref, meta_ref, out_ref, m_s,
+    flip, q_ref, pk_ref, pv_ref, ok_ref, ov_ref, xk_ref, xv_ref, nk_ref, nv_ref, meta_ref, out_ref,
 ):
     pre = lax.axis_index("prefix")
     half = pre % 2
@@ -88,20 +87,53 @@
         half = 1 - half
     n_dev = q_ref.shape[0]
     rows = n_dev * 32
+    n_quads = n_dev // 4
+    n_blocks = pk_ref.shape[0] // BLK
     ones = jnp.ones((16, BLK), bf16)
+    first = half * HALF
+
+    def head_lanes(i):
+        return pl.ds(pl.multiple_of((first + i) * DH, DH), DH)
+
     key = lax.broadcasted_iota(jnp.int32, (BLK, DH), 0)
     lane = lax.broadcasted_iota(jnp.int32, (BLK, DH), 1)
-    lane_dev, lane_req, lane_step = lane // 32, lane % 2, lane // 2 % 2
-    n_blocks = pk_ref.shape[0] // BLK
-    masks = []
-    for n in range(4):
-        limit = jnp.where((lane_dev == meta_ref[n, 0] % 4) & (lane_req == meta_ref[n, 1]), meta_ref[n, 2], 0)
-        masks.append(key < limit)
-    masks.append((lane_dev == pre % 4) & (key < 4) & (key % 2 == lane_req) & (key // 2 <= lane_step))
+    lane_head, lane_req, lane_step = lane // 32, lane % 2, lane // 2 % 2
+    own_rows = pl.ds(pl.multiple_of(first * 32, DH), DH)
+    extra = []
+    for n in range(5):
+        if n < 4:
+            kr, vr = (ok_ref, ov_ref) if n < 2 else (xk_ref, xv_ref)
+            ks = [kr[n % 2, :, head_lanes(i)] for i in range(HALF)]
+            vs = [vr[n % 2, :, head_lanes(i)].T for i in range(HALF)]
+            dev = meta_ref[n, 0]
+            live = key < jnp.where(lane_req == meta_ref[n, 1], meta_ref[n, 2], 0)
+        else:
+            ks = [nk_ref[:, head_lanes(i)] for i in range(HALF)]
+            fill = jnp.zeros((BLK - HALF * 16, DH), bf16)
+            vs = [jnp.concatenate([nv_ref[:, head_lanes(i)] for i in range(HALF)] + [fill], axis=0).T]
+            dev = pre
+            live = ((key < 4) & (key % 2 == lane_req) & (key // 2 <= lane_step))[0:16]
+        count = ks[0].shape[0]
+        every = lax.dot_general(
+            jnp.concatenate(ks, axis=0), q_ref[dev, own_rows, :], NT, preferred_element_type=f32
+        )
+        s = every[0:count]
+        for i in range(1, HALF):
+            s = jnp.where(lane_head[0:count] == i, every[i * count : (i + 1) * count], s)
+        s = jnp.where(live, s, NEG)
+        peak = jnp.max(s, axis=0, keepdims=True)
+        w = jnp.where(live, jnp.exp2((s - peak) * EXPO), 0.0)
+        ws = [jnp.where(lane_head[0:count] == i, w, 0.0).astype(bf16) for i in range(HALF)]
+        if n == 4:
+            ws.append(fill)
+        v = jnp.concatenate([jnp.concatenate(vs, axis=1), jnp.concatenate([ones] * len(vs), axis=1)], axis=0)
+        o = jnp.dot(v, jnp.concatenate(ws, axis=0), preferred_element_type=f32)[0:136]
+        extra.append((dev, peak, o))
+
+    spot = lax.broadcasted_iota(jnp.int32, (1, rows), 1) // 32
     for i in range(HALF):
-        kvh = half * HALF + i
-        lanes = pl.ds(pl.multiple_of(kvh * DH, DH), DH)
-        qrows = pl.ds(pl.multiple_of(kvh * 32, 32), 32)
+        lanes = head_lanes(i)
+        qrows = pl.ds(pl.multiple_of((first + i) * 32, 32), 32)
         q = q_ref[:, qrows, :].reshape(rows, DH)
         scores = lax.dot_general(pk_ref[:, lanes], q, NT, preferred_element_type=f32)
         peaks, outs = [], []
@@ -113,38 +145,25 @@
             v = jnp.concatenate([pv_ref[span, lanes].T, ones], axis=0)
             peaks.append(peak)
             outs.append(jnp.dot(v, w, preferred_element_type=f32)[0:136])
-        top = functools.reduce(jnp.maximum, peaks)
+        wides = []
+        for dev, peak, o in extra:
+            turn = (dev + (4 - i)) % 4 * 32
+            moved = pltpu.roll(peak, turn, 1)
+            wides.append(jnp.where(spot == dev, jnp.concatenate([moved] * n_quads, axis=1), NEG))
+        top = functools.reduce(jnp.maximum, peaks + wides)
         both = 0.0
         for peak, o in zip(peaks, outs):
             both = both + jnp.exp2((peak - top) * EXPO) * o
-        m_s[i : i + 1, :] = top
         out_ref[i] = both
-        extra = []
-        for n in range(5):
-            if n < 4:
-                kr, vr = (ok_ref, ov_ref) if n < 2 else (xk_ref, xv_ref)
-                k, v = kr[n % 2, :, lanes], vr[n % 2, :, lanes]
-                quad = meta_ref[n, 0] // 4
-            else:
-                k, v = nk_ref[:, lanes], nv_ref[:, lanes]
-                quad = pre // 4
-            qn = q_ref[pl.ds(quad * 4, 4), qrows, :].reshape(DH, DH)
-            s = lax.dot_general(k, qn, NT, preferred_element_type=f32)
-            s = jnp.where(masks[n], s, NEG)
-            peak = jnp.max(s, axis=0, keepdims=True)
-            w = jnp.where(masks[n], jnp.exp2((s - peak) * EXPO), 0.0).astype(bf16)
-            o = jnp.dot(jnp.concatenate([v.T, ones], axis=0), w, preferred_element_type=f32)[0:136]
-            extra.append((pl.ds(pl.multiple_of(quad * DH, DH), DH), peak, o))
-        for at, peak, o in extra:
-            old = m_s[i : i + 1, at]
-            new = jnp.maximum(old, peak)
-            m_s[i : i + 1, at] = new
-            out_ref[i, :, at] = (
-                out_ref[i, :, at] * jnp.exp2((old - new) * EXPO) + o * jnp.exp2((peak - new) * EXPO)
-            )
+        for (dev, peak, o), wide in zip(extra, wides):
+            turn = (dev + (4 - i)) % 4 * 32
+            f = jnp.exp2((wide - top) * EXPO)
+            f = sum(f[:, quad * DH : (quad + 1) * DH] for quad in range(n_quads))
+            at = pl.ds(pl.multiple_of(dev // 4 * DH, DH), DH)
+            out_ref[i, :, at] = out_ref[i, :, at] + pltpu.roll(o, turn, 1) * f
         total = out_ref[i, 128:129, :]
         out_ref[i, 0:128, :] = out_ref[i, 0:128, :] * (1.0 / total)
-        lse = m_s[i : i + 1, :] * EXPO + jnp.log(total) * LOG2E
+        lse = top * EXPO + jnp.log(total) * LOG2E
         out_ref[i, 128:136, :] = jnp.broadcast_to(lse, (8, rows))
 
 
@@ -235,7 +254,7 @@
     sds = jax.ShapeDtypeStruct
     own, nk, nv, meta = call(
         prepare_kernel,
-        (sds((4 * H, DH), f32), sds((BLK, KVH * DH), bf16), sds((BLK, KVH * DH), bf16), sds((4, 3), jnp.int32)),
+        (sds((4 * H, DH), f32), sds((16, KVH * DH), bf16), sds((16, KVH * DH), bf16), sds((4, 3), jnp.int32)),
         [ANY] * 5,
         (VM, VM, VM, SM),
         [
@@ -258,8 +277,6 @@
             functools.partial(attend_kernel, flip),
             sds((HALF, 136, rows), f32),
             [VM] * 9 + [SM],
-            VM,
-            [pltpu.VMEM((HALF, rows), f32)],
             flops=800_000_000,
             moved=6_000_000,
             name="attend_other" if flip else "attend_own",

time: 68.7 us -> 66.4 us (0.967)
  Pallas kernels: 11.8 us -> 9.58 us
    pallas_call x2, Pallas kernels: 8.37 us -> 6.27 us  [attend(): call(functools.partial(attend_kernel, flip), sds((HALF, 136, rows), f32),...]
  transfers between devices with their start and end apart: 3 -> 3, of which waited for: 0 -> 0; matrix products, arithmetic and copies ran while one was open for 2% -> 2% of each run, Pallas kernels for 9% -> 7%
where the time goes in v4:
time: 66.4 us; the launch traced here: 66.1 us
  blocking collectives  45.9 us (69%)
  Pallas kernels  9.58 us (14%)
  starting transfers between devices  7.92 us (12%)
  other arithmetic  1.31 us (2%)
  local copies, waits for them, and re-layouts  1.23 us (2%)
    all_gather x1, blocking collectives, per_device(): group = lax.all_gather(own.astype(jnp.float16), 'prefix', axis=0)  24.7 us
    all_to_all x1, blocking collectives, per_device(): lax.all_to_all(merged.astype(jnp.float16), 'prefix', 0, 0, tiled=True)  21.2 us
    pallas_call x2, Pallas kernels, attend(): call(functools.partial(attend_kernel, flip), sds((HALF, 136, rows), f32),...  6.27 us
    ppermute x1, starting transfers between devices, per_device(): far_keys = lax.ppermute(pool_keys, 'req', swap)  3.94 us
    ppermute x1, starting transfers between devices, per_device(): theirs = lax.ppermute(attend(True), 'prefix', core)  2.06 us
    ppermute x1, starting transfers between devices, per_device(): far_values = lax.ppermute(pool_values, 'req', swap)  1.92 us
    pallas_call x1, Pallas kernels, per_device(): call(prepare_kernel, (sds((4 * H, DH), f32), sds((16, KVH * DH), bf16), s...  1.76 us
  transfers between devices with their start and end apart: 3, of which 0 were waited for; matrix products, arithmetic and copies ran while one was open for 2% of the time, Pallas kernels for 7%

profile of v4, /device:TPU:1, one launch (start us, length us, event | category | flops | bytes accessed | tf_op | source)
XLA Modules:
  0.0 66.1 jit_solution(6414699528850363076)
XLA Ops:
  0.0 3.9 %collective-permute-start = (bf16[2,128,1024]{2,1,0:T(8,128)(2,1)}, bf16[2,128,1024]{2,1,0:T(8,128)(2,1)S(1)}, u32[]{:S(2)}, u32[]{:S(2)}) collective-permute-start(bf16[2,128,1024]{2,1,0:T(8,128)(2,1)} %ok_ref.3), channel_id=1, source_target_pairs={{0,16},{16,0},{32,48},{48,32},{64,80},{80,64},{96,112},{112,96},{1... | collective-permute-start | bytes 1572872 | tf_op jit(solution)/shard_map/ppermute | solution.py:252
  3.9 1.9 %collective-permute-start.1 = (bf16[2,128,1024]{2,1,0:T(8,128)(2,1)}, bf16[2,128,1024]{2,1,0:T(8,128)(2,1)S(1)}, u32[]{:S(2)}, u32[]{:S(2)}) collective-permute-start(bf16[2,128,1024]{2,1,0:T(8,128)(2,1)} %ov_ref.3), channel_id=1, source_target_pairs={{0,16},{16,0},{32,48},{48,32},{64,80},{80,64},{96,112},{112,96},{1... | collective-permute-start | bytes 1572872 | tf_op jit(solution)/shard_map/ppermute | solution.py:253
  5.9 1.8 %prepare.1 = (f32[256,128]{1,0:T(8,128)}, bf16[16,1024]{1,0:T(8,128)(2,1)}, bf16[16,1024]{1,0:T(8,128)(2,1)}, s32[4,3]{1,0:T(4,128)}) custom-call(bf16[2,2,8192]{2,1,0:T(2,128)(2,1)} %q_ref.1, bf16[2,2,1024]{2,1,0:T(2,128)(2,1)} %nk_ref.1, bf16[2,2,1024]{2,1,0:T(2,128)(2,1)} %nv_ref.1, s32[8,128]{1,0:T(8,128)} %bitcast.6, s32[16,1024]{1,0:T(8,128)} %bitcast.5), custom_call_target="tpu_custom_call" | custom-call | tf_op jit(solution)/shard_map/prepare/pallas_call | solution.py:255
  7.6 0.9 %convert_element_type.15 = f16[256,128]{1,0:T(8,128)(2,1)S(1)} convert(f32[256,128]{1,0:T(8,128)} %get-tuple-element.9) | non-fusion elementwise | flops 32768 | bytes 196608 | tf_op jit(solution)/shard_map/convert_element_type | solution.py:271
  8.6 0.0 copy-start.3
  8.6 0.0 copy-start.4
  8.6 0.0 copy-start.5
  8.6 24.7 %all-gather.2 = f16[4096,128]{1,0:T(8,128)(2,1)S(1)} all-gather(f16[256,128]{1,0:T(8,128)(2,1)S(1)} %convert_element_type.15), channel_id=2, replica_groups=mesh['req'=32,'prefix'=16] {'prefix'}, dimensions={0}, use_global_device_ids=true | all-gather | bytes 1114112 | tf_op jit(solution)/shard_map/all_gather | solution.py:271
  33.3 0.0 copy-start
  33.3 0.0 copy-start.1
  33.3 0.0 copy-start.2
  33.3 0.0 copy-start.6
  33.3 0.2 multiply_convert_fusion
  33.5 0.0 collective-permute-done.xk_ref
  33.5 0.0 collective-permute-done.1.xv_ref
  33.5 0.0 copy-done.3
  33.5 0.0 copy-done.4
  33.6 0.0 copy-done.5
  33.6 0.8 %copy-done = bf16[384,1024]{1,0:T(8,128)(2,1)S(1)} copy-done((bf16[384,1024]{1,0:T(8,128)(2,1)S(1)}, bf16[384,1024]{1,0:T(8,128)(2,1)}, u32[]{:S(2)}) %copy-start) | copy-done | bytes 786456
  34.4 0.2 copy-done.1
  34.6 0.1 copy-done.2
  34.8 0.0 copy-done.6
  34.8 3.1 %attend_other.1 = f32[4,136,512]{2,1,0:T(8,128)S(1)} custom-call(bf16[16,256,128]{2,1,0:T(8,128)(2,1)S(1)} %bitcast.3, bf16[384,1024]{1,0:T(8,128)(2,1)S(1)} %copy-done, bf16[384,1024]{1,0:T(8,128)(2,1)S(1)} %copy-done.1, bf16[2,128,1024]{2,1,0:T(8,128)(2,1)S(1)} %copy-done.2, bf16[2,128,1024]{2,1,0:T(8,128)(2,1)S(1)} %copy-done.3, ...), custom_call_target="tpu_custom_call" | custom-call | flops 800000000 | bytes 6000000 | tf_op jit(solution)/shard_map/attend_other/pallas_call | solution.py:276
  37.9 2.1 %collective-permute-start.2 = (f32[4,136,512]{2,1,0:T(8,128)S(1)}, f32[4,136,512]{2,1,0:T(8,128)S(1)}, u32[]{:S(2)}, u32[]{:S(2)}) collective-permute-start(f32[4,136,512]{2,1,0:T(8,128)S(1)} %attend_other.1), channel_id=1, source_target_pairs={{0,1},{1,0},{2,3},{3,2},{4,5},{5,4},{6,7},{7,6},{8,9},{9,8},{10,11... | collective-permute-start | bytes 3342344 | tf_op jit(solution)/shard_map/ppermute | solution.py:285
  40.0 3.1 %attend_own.1.a_ref = f32[4,136,512]{2,1,0:T(8,128)S(1)} custom-call(bf16[16,256,128]{2,1,0:T(8,128)(2,1)S(1)} %bitcast.4, bf16[384,1024]{1,0:T(8,128)(2,1)S(1)} %copy-done, bf16[384,1024]{1,0:T(8,128)(2,1)S(1)} %copy-done.1, bf16[2,128,1024]{2,1,0:T(8,128)(2,1)S(1)} %copy-done.2, bf16[2,128,1024]{2,1,0:T(8,128)(2,1)S(1)} %copy-done.3, ...), custom_call_target="tpu_custom_call" | custom-call | flops 800000000 | bytes 6000000 | tf_op jit(solution)/shard_map/attend_own/pallas_call | solution.py:276
  43.1 0.0 collective-permute-done.2.b_ref
  43.1 0.4 core_merge.1
  43.5 0.1 convert_element_type.18
  43.6 21.2 %all_to_all.5 = f16[16,136,128]{2,1,0:T(8,128)(2,1)S(1)} all-to-all(f16[16,136,128]{2,1,0:T(8,128)(2,1)S(1)} %convert_element_type.18), channel_id=1, replica_groups=mesh['req'=32,'prefix'=16] {'prefix'}, dimensions={0} | all-to-all | bytes 1114112 | tf_op jit(solution)/shard_map/all_to_all | solution.py:290
  64.8 0.1 convert_element_type.19.z_ref
  64.9 1.2 %final.1 = bf16[2,2,8192]{2,1,0:T(2,128)(2,1)} custom-call(f32[16,136,128]{2,1,0:T(8,128)S(1)} %convert_element_type.19.z_ref), custom_call_target="tpu_custom_call" | custom-call | bytes 1000000 | tf_op jit(solution)/shard_map/final/pallas_call | solution.py:291
Async XLA Ops:
  0.0 33.5 %collective-permute-start = (bf16[2,128,1024]{2,1,0:T(8,128)(2,1)}, bf16[2,128,1024]{2,1,0:T(8,128)(2,1)S(1)}, u32[]{:S(2)}, u32[]{:S(2)}) collective-permute-start(bf16[2,128,1024]{2,1,0:T(8,128)(2,1)} %ok_ref.3), channel_id=1, source_target_pairs={{0,16},{16,0},{32,48},{48,32},{64,80},{80,64},{96,112},{112,96},{1... | collective-permute-start | bytes 1572872 | tf_op jit(solution)/shard_map/ppermute | solution.py:252
  3.9 29.6 %collective-permute-start.1 = (bf16[2,128,1024]{2,1,0:T(8,128)(2,1)}, bf16[2,128,1024]{2,1,0:T(8,128)(2,1)S(1)}, u32[]{:S(2)}, u32[]{:S(2)}) collective-permute-start(bf16[2,128,1024]{2,1,0:T(8,128)(2,1)} %ov_ref.3), channel_id=1, source_target_pairs={{0,16},{16,0},{32,48},{48,32},{64,80},{80,64},{96,112},{112,96},{1... | collective-permute-start | bytes 1572872 | tf_op jit(solution)/shard_map/ppermute | solution.py:253
  8.6 25.0 %copy-start.3 = (bf16[2,128,1024]{2,1,0:T(8,128)(2,1)S(1)}, bf16[2,128,1024]{2,1,0:T(8,128)(2,1)}, u32[]{:S(2)}) copy-start(bf16[2,128,1024]{2,1,0:T(8,128)(2,1)} %ov_ref.3) | copy-start | bytes 1572868
  8.6 25.0 %copy-start.4 = (bf16[16,1024]{1,0:T(8,128)(2,1)S(1)}, bf16[16,1024]{1,0:T(8,128)(2,1)}, u32[]{:S(2)}) copy-start(bf16[16,1024]{1,0:T(8,128)(2,1)} %get-tuple-element.10.nk_ref) | copy-start | bytes 98308
  8.6 25.0 %copy-start.5 = (bf16[16,1024]{1,0:T(8,128)(2,1)S(1)}, bf16[16,1024]{1,0:T(8,128)(2,1)}, u32[]{:S(2)}) copy-start(bf16[16,1024]{1,0:T(8,128)(2,1)} %get-tuple-element.11.nv_ref) | copy-start | bytes 98308
  33.3 1.1 %copy-start = (bf16[384,1024]{1,0:T(8,128)(2,1)S(1)}, bf16[384,1024]{1,0:T(8,128)(2,1)}, u32[]{:S(2)}) copy-start(bf16[384,1024]{1,0:T(8,128)(2,1)} %pk_ref.3) | copy-start | bytes 2359300
  33.3 1.4 %copy-start.1 = (bf16[384,1024]{1,0:T(8,128)(2,1)S(1)}, bf16[384,1024]{1,0:T(8,128)(2,1)}, u32[]{:S(2)}) copy-start(bf16[384,1024]{1,0:T(8,128)(2,1)} %pv_ref.3) | copy-start | bytes 2359300
  33.3 1.5 %copy-start.2 = (bf16[2,128,1024]{2,1,0:T(8,128)(2,1)S(1)}, bf16[2,128,1024]{2,1,0:T(8,128)(2,1)}, u32[]{:S(2)}) copy-start(bf16[2,128,1024]{2,1,0:T(8,128)(2,1)} %ok_ref.3) | copy-start | bytes 1572868
  33.3 1.5 %copy-start.6 = (s32[4,3]{1,0:T(4,128)S(1)}, s32[4,3]{1,0:T(4,128)}, u32[]{:S(2)}) copy-start(s32[4,3]{1,0:T(4,128)} %get-tuple-element.12.meta_ref) | copy-start | bytes 148
  37.9 5.2 %collective-permute-start.2 = (f32[4,136,512]{2,1,0:T(8,128)S(1)}, f32[4,136,512]{2,1,0:T(8,128)S(1)}, u32[]{:S(2)}, u32[]{:S(2)}) collective-permute-start(f32[4,136,512]{2,1,0:T(8,128)S(1)} %attend_other.1), channel_id=1, source_target_pairs={{0,1},{1,0},{2,3},{3,2},{4,5},{5,4},{6,7},{7,6},{8,9},{9,8},{10,11... | collective-permute-start | bytes 3342344 | tf_op jit(solution)/shard_map/ppermute | solution.py:285

commit v5 on v4

--- a/solution.py
+++ b/solution.py
@@ -25,13 +25,9 @@
 NT = (((1,), (1,)), ((), ()))
 VM = pl.BlockSpec(memory_space=pltpu.VMEM)
 SM = pl.BlockSpec(memory_space=pltpu.SMEM)
-ANY = pl.BlockSpec(memory_space=pl.ANY)
-
-
-def prepare_kernel(
-    q_ref, nk_ref, nv_ref, len_ref, table_ref, qt_ref, nkp_ref, nvp_ref, meta_ref,
-    q_s, nk_s, nv_s, len_s, table_s, sems,
-):
+
+
+def find_owners(len_ref, table_ref, meta_ref):
     req = lax.axis_index("req")
     pre = lax.axis_index("prefix")
     n_pre = lax.axis_size("prefix")
@@ -41,50 +37,35 @@
     side = req % 2
     line = pair // per_line
     first = (pair % per_line) * pair_rows
-    lanes = pl.ds(pl.multiple_of(line * 128, 128), 128)
-    sources = (len_ref, table_ref.at[:, lanes], q_ref, nk_ref, nv_ref)
-    copies = [
-        pltpu.make_async_copy(src, dst, sems.at[i])
-        for i, (src, dst) in enumerate(zip(sources, (len_s, table_s, q_s, nk_s, nv_s)))
-    ]
-    for copy in copies:
-        copy.start()
-    for copy in copies:
-        copy.wait()
-    pieces = []
-    steps = [q_s[s].astype(f32) * QLIFT for s in range(2)]
-    for head in range(H):
-        for s in range(2):
-            pieces.append(steps[s][:, head * DH : (head + 1) * DH])
-    qt_ref[...] = jnp.concatenate(pieces, axis=0)
-    for src, dst in ((nk_s, nkp_ref), (nv_s, nvp_ref)):
-        top = jnp.concatenate([src[0].astype(f32), src[1].astype(f32), jnp.zeros((12, KVH * DH), f32)], axis=0)
-        dst[...] = top.astype(bf16)
-    table = table_s[...]
+    table = table_ref[:, pl.ds(pl.multiple_of(line * 128, 128), 128)]
     lane = lax.broadcasted_iota(jnp.int32, table.shape, 1) - first
     block = lax.broadcasted_iota(jnp.int32, table.shape, 0)
-    left = jnp.broadcast_to(len_s[pl.ds(line, 1), :], table.shape) - block * BLK
+    left = jnp.broadcast_to(len_ref[pl.ds(line, 1), :], table.shape) - block * BLK
     usable = (left > 0) & (lane >= 0) & (lane < pair_rows)
     for n in range(4):
         holder = side if n < 2 else 1 - side
         slot = (holder * n_pre + pre) * 2 + n % 2
         hit = (table == slot) & usable
-        owner = jnp.sum(jnp.where(hit, lane, 0)) - side * (pair_rows // 2)
-        live = jnp.sum(jnp.where(hit, jnp.minimum(left, BLK), 0))
+        found = jnp.sum(jnp.where(hit, lane * 256 + jnp.minimum(left, BLK), 0))
+        owner = found // 256 - side * (pair_rows // 2)
         mine = (owner >= 0) & (owner < pair_rows // 2)
         owner = jnp.where(mine, owner, 0)
         meta_ref[n, 0] = owner // 2
         meta_ref[n, 1] = owner % 2
-        meta_ref[n, 2] = jnp.where(mine, live, 0)
+        meta_ref[n, 2] = jnp.where(mine, found % 256, 0)
 
 
 def attend_kernel(
-    flip, q_ref, pk_ref, pv_ref, ok_ref, ov_ref, xk_ref, xv_ref, nk_ref, nv_ref, meta_ref, out_ref,
+    flip, q_ref, pk_ref, pv_ref, ok_ref, ov_ref, xk_ref, xv_ref, nk_ref, nv_ref, *refs
 ):
     pre = lax.axis_index("prefix")
     half = pre % 2
     if flip:
         half = 1 - half
+        len_ref, table_ref, out_ref, meta_ref = refs
+        find_owners(len_ref, table_ref, meta_ref)
+    else:
+        meta_ref, out_ref = refs
     n_dev = q_ref.shape[0]
     rows = n_dev * 32
     n_quads = n_dev // 4
@@ -94,6 +75,10 @@
 
     def head_lanes(i):
         return pl.ds(pl.multiple_of((first + i) * DH, DH), DH)
+
+    def tokens(ref, i):
+        pair = [ref[s, :, head_lanes(i)].astype(f32) for s in range(2)]
+        return jnp.concatenate(pair + [jnp.zeros((12, DH), f32)], axis=0).astype(bf16)
 
     key = lax.broadcasted_iota(jnp.int32, (BLK, DH), 0)
     lane = lax.broadcasted_iota(jnp.int32, (BLK, DH), 1)
@@ -108,9 +93,9 @@
             dev = meta_ref[n, 0]
             live = key < jnp.where(lane_req == meta_ref[n, 1], meta_ref[n, 2], 0)
         else:
-            ks = [nk_ref[:, head_lanes(i)] for i in range(HALF)]
+            ks = [tokens(nk_ref, i) for i in range(HALF)]
             fill = jnp.zeros((BLK - HALF * 16, DH), bf16)
-            vs = [jnp.concatenate([nv_ref[:, head_lanes(i)] for i in range(HALF)] + [fill], axis=0).T]
+            vs = [jnp.concatenate([tokens(nv_ref, i) for i in range(HALF)] + [fill], axis=0).T]
             dev = pre
             live = ((key < 4) & (key % 2 == lane_req) & (key // 2 <= lane_step))[0:16]
         count = ks[0].shape[0]
@@ -161,22 +146,19 @@
             f = sum(f[:, quad * DH : (quad + 1) * DH] for quad in range(n_quads))
             at = pl.ds(pl.multiple_of(dev // 4 * DH, DH), DH)
             out_ref[i, :, at] = out_ref[i, :, at] + pltpu.roll(o, turn, 1) * f
-        total = out_ref[i, 128:129, :]
-        out_ref[i, 0:128, :] = out_ref[i, 0:128, :] * (1.0 / total)
-        lse = top * EXPO + jnp.log(total) * LOG2E
-        out_ref[i, 128:136, :] = jnp.broadcast_to(lse, (8, rows))
+        out_ref[i, 132:136, :] = jnp.broadcast_to(top * EXPO, (4, rows))
 
 
 def core_merge_kernel(a_ref, b_ref, out_ref):
     rows = a_ref.shape[2]
     high, low = [], []
     for i in range(HALF):
-        la = a_ref[i, 128:129, :]
-        lb = b_ref[i, 128:129, :]
-        top = jnp.maximum(la, lb)
-        wa = jnp.exp2(la - top)
-        wb = jnp.exp2(lb - top)
-        total = wa + wb
+        pa = a_ref[i, 132:133, :]
+        pb = b_ref[i, 132:133, :]
+        top = jnp.maximum(pa, pb)
+        wa = jnp.exp2(pa - top)
+        wb = jnp.exp2(pb - top)
+        total = a_ref[i, 128:129, :] * wa + b_ref[i, 128:129, :] * wb
         scale = LIFT / total
         o = a_ref[i, 0:128, :] * (wa * scale) + b_ref[i, 0:128, :] * (wb * scale)
         for quad in range(rows // DH):
@@ -220,14 +202,14 @@
                     out_ref[s, :, head * DH : (head + 1) * DH] = o[r : r + 2, :].astype(bf16)
 
 
-def call(kernel, out_shape, ins, out_specs=VM, scratch=(), flops=0, moved=0, name=None, room=40):
+def call(kernel, out_shape, ins, out_specs=VM, scratch=(), flops=0, moved=0, name=None):
     return pl.pallas_call(
         kernel,
         out_shape=out_shape,
         in_specs=ins,
         out_specs=out_specs,
         scratch_shapes=list(scratch),
-        compiler_params=pltpu.CompilerParams(vmem_limit_bytes=room * 1024 * 1024),
+        compiler_params=pltpu.CompilerParams(vmem_limit_bytes=40 * 1024 * 1024),
         cost_estimate=pl.CostEstimate(flops=flops, bytes_accessed=moved, transcendentals=0),
         name=name,
     )
@@ -246,44 +228,34 @@
 ):
     n_req = lax.axis_size("req")
     n_pre = lax.axis_size("prefix")
-    pair_rows = 4 * n_pre
     swap = [(i, i ^ 1) for i in range(n_req)]
     core = [(i, i ^ 1) for i in range(n_pre)]
     far_keys = lax.ppermute(pool_keys, "req", swap)
     far_values = lax.ppermute(pool_values, "req", swap)
     sds = jax.ShapeDtypeStruct
-    own, nk, nv, meta = call(
-        prepare_kernel,
-        (sds((4 * H, DH), f32), sds((16, KVH * DH), bf16), sds((16, KVH * DH), bf16), sds((4, 3), jnp.int32)),
-        [ANY] * 5,
-        (VM, VM, VM, SM),
-        [
-            pltpu.VMEM(queries.shape, bf16),
-            pltpu.VMEM(new_keys.shape, bf16),
-            pltpu.VMEM(new_values.shape, bf16),
-            pltpu.VMEM((suffix_lengths.size // 128, 128), jnp.int32),
-            pltpu.VMEM((block_table.shape[1], 128), jnp.int32),
-            pltpu.SemaphoreType.DMA((5,)),
-        ],
-        name="prepare",
-        room=62,
-    )(queries, new_keys, new_values, suffix_lengths.reshape(-1, 128), block_table.T)
-    group = lax.all_gather(own.astype(jnp.float16), "prefix", axis=0)
+    own = (queries.astype(f32) * QLIFT).astype(jnp.float16)
+    own = own.reshape(4, H, DH).transpose(1, 0, 2).reshape(4 * H, DH)
+    group = lax.all_gather(own, "prefix", axis=0)
     group = (group.astype(f32) * (1.0 / QLIFT)).astype(bf16)
     rows = n_pre * 32
 
-    def attend(flip):
-        return call(
-            functools.partial(attend_kernel, flip),
-            sds((HALF, 136, rows), f32),
-            [VM] * 9 + [SM],
-            flops=800_000_000,
-            moved=6_000_000,
-            name="attend_other" if flip else "attend_own",
-        )(group, prefix_keys, prefix_values, pool_keys, pool_values, far_keys, far_values, nk, nv, meta)
-
-    theirs = lax.ppermute(attend(True), "prefix", core)
-    mine = attend(False)
+    common = (
+        group, prefix_keys, prefix_values, pool_keys, pool_values, far_keys, far_values, new_keys, new_values
+    )
+    part = sds((HALF, 136, rows), f32)
+    cost = dict(flops=800_000_000, moved=6_000_000)
+    other, meta = call(
+        functools.partial(attend_kernel, True),
+        (part, sds((4, 3), jnp.int32)),
+        [VM] * 11,
+        (VM, SM),
+        name="attend_other",
+        **cost,
+    )(*common, suffix_lengths.reshape(-1, 128), block_table.T)
+    theirs = lax.ppermute(other, "prefix", core)
+    mine = call(
+        functools.partial(attend_kernel, False), part, [VM] * 9 + [SM], name="attend_own", **cost
+    )(*common, meta)
     merged = call(core_merge_kernel, sds((n_pre, 136, DH), f32), [VM, VM], moved=4_000_000, name="core_merge")(
         mine, theirs
     )

time: 66.4 us -> 64.1 us (0.965)
  Pallas kernels: 9.58 us -> 7.14 us
    pallas_call x3 -> x2, Pallas kernels: 8.03 us -> 5.57 us  [the longest x1 2.99 us: per_device(): call(functools.partial(attend_kernel, False), part, [VM] * 9 + [SM], name...]
  transfers between devices with their start and end apart: 3 -> 3, of which waited for: 0 -> 0; matrix products, arithmetic and copies ran while one was open for 2% -> 2% of each run, Pallas kernels for 7% -> 5%
where the time goes in v5:
time: 64.1 us; the launch traced here: 63.8 us
  blocking collectives  45.9 us (72%)
  starting transfers between devices  7.93 us (12%)
  Pallas kernels  7.14 us (11%)
  other arithmetic  1.34 us (2%)
  local copies, waits for them, and re-layouts  1.31 us (2%)
    all_gather x1, blocking collectives, per_device(): group = lax.all_gather(own, 'prefix', axis=0)  24.7 us
    all_to_all x1, blocking collectives, per_device(): lax.all_to_all(merged.astype(jnp.float16), 'prefix', 0, 0, tiled=True)  21.2 us
    ppermute x1, starting transfers between devices, per_device(): far_keys = lax.ppermute(pool_keys, 'req', swap)  3.94 us
    pallas_call x1, Pallas kernels, per_device(): call(functools.partial(attend_kernel, False), part, [VM] * 9 + [SM], name...  2.99 us
    pallas_call x1, Pallas kernels, per_device(): call(functools.partial(attend_kernel, True), (part, sds((4, 3), jnp.int32...  2.58 us
    ppermute x1, starting transfers between devices, per_device(): theirs = lax.ppermute(other, 'prefix', core)  2.07 us
    ppermute x1, starting transfers between devices, per_device(): far_values = lax.ppermute(pool_values, 'req', swap)  1.92 us
  transfers between devices with their start and end apart: 3, of which 0 were waited for; matrix products, arithmetic and copies ran while one was open for 2% of the time, Pallas kernels for 5%

profile of v5, /device:TPU:1, one launch (start us, length us, event | category | flops | bytes accessed | tf_op | source)
XLA Modules:
  0.0 63.8 jit_solution(7692729669356192328)
XLA Ops:
  0.0 3.9 %collective-permute-start = (bf16[2,128,1024]{2,1,0:T(8,128)(2,1)}, bf16[2,128,1024]{2,1,0:T(8,128)(2,1)S(1)}, u32[]{:S(2)}, u32[]{:S(2)}) collective-permute-start(bf16[2,128,1024]{2,1,0:T(8,128)(2,1)} %ok_ref.3), channel_id=1, source_target_pairs={{0,16},{16,0},{32,48},{48,32},{64,80},{80,64},{96,112},{112,96},{1... | collective-permute-start | bytes 1572872 | tf_op jit(solution)/shard_map/ppermute | solution.py:233
  3.9 1.9 %collective-permute-start.1 = (bf16[2,128,1024]{2,1,0:T(8,128)(2,1)}, bf16[2,128,1024]{2,1,0:T(8,128)(2,1)S(1)}, u32[]{:S(2)}, u32[]{:S(2)}) collective-permute-start(bf16[2,128,1024]{2,1,0:T(8,128)(2,1)} %ov_ref.3), channel_id=1, source_target_pairs={{0,16},{16,0},{32,48},{48,32},{64,80},{80,64},{96,112},{112,96},{1... | collective-permute-start | bytes 1572872 | tf_op jit(solution)/shard_map/ppermute | solution.py:234
  5.9 0.9 %multiply_convert_fusion.1 = f16[2,2,8192]{2,1,0:T(2,128)(2,1)S(1)} fusion(bf16[2,2,8192]{2,1,0:T(2,128)(2,1)} %param.9), kind=kLoop, calls=%fused_computation.1 | loop fusion | flops 98304 | bytes 131072 | tf_op jit(solution)/shard_map/convert_element_type | solution.py:236
  6.8 0.1 reshape.6
  6.9 0.1 copy.11
  6.9 0.0 copy-start.3
  6.9 0.0 copy-start.4
  7.0 0.0 copy-start.5
  7.0 0.0 copy-start.6
  7.0 0.0 copy-start.7
  7.0 24.7 %all-gather.1 = f16[16,256,128]{2,1,0:T(8,128)(2,1)S(1)} all-gather(f16[1,256,128]{2,1,0:T(8,128)(2,1)S(1)} %bitcast.7), channel_id=1, replica_groups=mesh['req'=32,'prefix'=16] {'prefix'}, dimensions={0}, use_global_device_ids=true | all-gather | bytes 1114112 | tf_op jit(solution)/shard_map/all_gather | solution.py:238
  31.7 0.0 copy-start
  31.7 0.0 copy-start.1
  31.7 0.0 copy-start.2
  31.7 0.3 multiply_convert_fusion.q_ref
  31.9 0.0 collective-permute-done.xk_ref
  32.0 0.0 collective-permute-done.1.xv_ref
  32.0 0.0 copy-done.3
  32.0 0.0 copy-done.4
  32.0 0.0 copy-done.5
  32.0 0.0 copy-done.6
  32.0 0.0 copy-done.7
  32.0 0.8 %copy-done = bf16[384,1024]{1,0:T(8,128)(2,1)S(1)} copy-done((bf16[384,1024]{1,0:T(8,128)(2,1)S(1)}, bf16[384,1024]{1,0:T(8,128)(2,1)}, u32[]{:S(2)}) %copy-start) | copy-done | bytes 786456
  32.8 0.2 copy-done.1
  33.0 0.1 copy-done.2
  33.2 2.6 %attend_other.1 = (f32[4,136,512]{2,1,0:T(8,128)S(1)}, s32[4,3]{1,0:T(4,128)S(1)}) custom-call(bf16[16,256,128]{2,1,0:T(8,128)(2,1)S(1)} %multiply_convert_fusion.q_ref, bf16[384,1024]{1,0:T(8,128)(2,1)S(1)} %copy-done, bf16[384,1024]{1,0:T(8,128)(2,1)S(1)} %copy-done.1, bf16[2,128,1024]{2,1,0:T(8,128)(2,1)S(1)} %copy-done.2, ...), custom_call_target="tpu_custom_call" | custom-call | flops 800000000 | bytes 6000000 | tf_op jit(solution)/shard_map/attend_other/pallas_call | solution.py:247
  35.8 2.1 %collective-permute-start.2 = (f32[4,136,512]{2,1,0:T(8,128)S(1)}, f32[4,136,512]{2,1,0:T(8,128)S(1)}, u32[]{:S(2)}, u32[]{:S(2)}) collective-permute-start(f32[4,136,512]{2,1,0:T(8,128)S(1)} %get-tuple-element.8), channel_id=1, source_target_pairs={{0,1},{1,0},{2,3},{3,2},{4,5},{5,4},{6,7},{7,6},{8,9},{9,8},{10,11... | collective-permute-start | bytes 3342344 | tf_op jit(solution)/shard_map/ppermute | solution.py:255
  37.8 3.0 %attend_own.1.a_ref = f32[4,136,512]{2,1,0:T(8,128)S(1)} custom-call(bf16[16,256,128]{2,1,0:T(8,128)(2,1)S(1)} %multiply_convert_fusion.q_ref, bf16[384,1024]{1,0:T(8,128)(2,1)S(1)} %copy-done, bf16[384,1024]{1,0:T(8,128)(2,1)S(1)} %copy-done.1, bf16[2,128,1024]{2,1,0:T(8,128)(2,1)S(1)} %copy-done.2, bf16[2,128,1024]{2,1,0:T(8,128)(2,1)S(1)} %copy-done.3, ...), custom_call_target="tpu_custom_call" | custom-call | flops 800000000 | bytes 6000000 | tf_op jit(solution)/shard_map/attend_own/pallas_call | solution.py:256
  40.8 0.0 collective-permute-done.2.b_ref
  40.8 0.4 core_merge.1
  41.2 0.1 convert_element_type.22
  41.3 21.2 %all_to_all.5 = f16[16,136,128]{2,1,0:T(8,128)(2,1)S(1)} all-to-all(f16[16,136,128]{2,1,0:T(8,128)(2,1)S(1)} %convert_element_type.22), channel_id=1, replica_groups=mesh['req'=32,'prefix'=16] {'prefix'}, dimensions={0} | all-to-all | bytes 1114112 | tf_op jit(solution)/shard_map/all_to_all | solution.py:262
  62.5 0.1 convert_element_type.23.z_ref
  62.6 1.2 %final.1 = bf16[2,2,8192]{2,1,0:T(2,128)(2,1)} custom-call(f32[16,136,128]{2,1,0:T(8,128)S(1)} %convert_element_type.23.z_ref), custom_call_target="tpu_custom_call" | custom-call | bytes 1000000 | tf_op jit(solution)/shard_map/final/pallas_call | solution.py:263
Async XLA Ops:
  0.0 31.9 %collective-permute-start = (bf16[2,128,1024]{2,1,0:T(8,128)(2,1)}, bf16[2,128,1024]{2,1,0:T(8,128)(2,1)S(1)}, u32[]{:S(2)}, u32[]{:S(2)}) collective-permute-start(bf16[2,128,1024]{2,1,0:T(8,128)(2,1)} %ok_ref.3), channel_id=1, source_target_pairs={{0,16},{16,0},{32,48},{48,32},{64,80},{80,64},{96,112},{112,96},{1... | collective-permute-start | bytes 1572872 | tf_op jit(solution)/shard_map/ppermute | solution.py:233
  3.9 28.0 %collective-permute-start.1 = (bf16[2,128,1024]{2,1,0:T(8,128)(2,1)}, bf16[2,128,1024]{2,1,0:T(8,128)(2,1)S(1)}, u32[]{:S(2)}, u32[]{:S(2)}) collective-permute-start(bf16[2,128,1024]{2,1,0:T(8,128)(2,1)} %ov_ref.3), channel_id=1, source_target_pairs={{0,16},{16,0},{32,48},{48,32},{64,80},{80,64},{96,112},{112,96},{1... | collective-permute-start | bytes 1572872 | tf_op jit(solution)/shard_map/ppermute | solution.py:234
  6.9 25.0 %copy-start.3 = (bf16[2,128,1024]{2,1,0:T(8,128)(2,1)S(1)}, bf16[2,128,1024]{2,1,0:T(8,128)(2,1)}, u32[]{:S(2)}) copy-start(bf16[2,128,1024]{2,1,0:T(8,128)(2,1)} %ov_ref.3) | copy-start | bytes 1572868
  6.9 25.0 %copy-start.4 = (s32[1024,16]{0,1:T(8,128)S(1)}, s32[1024,16]{0,1:T(8,128)}, u32[]{:S(2)}) copy-start(s32[1024,16]{0,1:T(8,128)} %param.16) | copy-start | bytes 196612
  7.0 25.0 %copy-start.5 = (bf16[2,2,1024]{2,1,0:T(2,128)(2,1)S(1)}, bf16[2,2,1024]{2,1,0:T(2,128)(2,1)}, u32[]{:S(2)}) copy-start(bf16[2,2,1024]{2,1,0:T(2,128)(2,1)} %nk_ref.3) | copy-start | bytes 24580
  7.0 25.0 %copy-start.6 = (bf16[2,2,1024]{2,1,0:T(2,128)(2,1)S(1)}, bf16[2,2,1024]{2,1,0:T(2,128)(2,1)}, u32[]{:S(2)}) copy-start(bf16[2,2,1024]{2,1,0:T(2,128)(2,1)} %nv_ref.3) | copy-start | bytes 24580
  7.0 25.0 %copy-start.7 = (s32[1024]{0:T(1024)S(1)}, s32[1024]{0:T(1024)}, u32[]{:S(2)}) copy-start(s32[1024]{0:T(1024)} %param.17) | copy-start | bytes 12292
  31.7 1.1 %copy-start = (bf16[384,1024]{1,0:T(8,128)(2,1)S(1)}, bf16[384,1024]{1,0:T(8,128)(2,1)}, u32[]{:S(2)}) copy-start(bf16[384,1024]{1,0:T(8,128)(2,1)} %pk_ref.3) | copy-start | bytes 2359300
  31.7 1.4 %copy-start.1 = (bf16[384,1024]{1,0:T(8,128)(2,1)S(1)}, bf16[384,1024]{1,0:T(8,128)(2,1)}, u32[]{:S(2)}) copy-start(bf16[384,1024]{1,0:T(8,128)(2,1)} %pv_ref.3) | copy-start | bytes 2359300
  31.7 1.5 %copy-start.2 = (bf16[2,128,1024]{2,1,0:T(8,128)(2,1)S(1)}, bf16[2,128,1024]{2,1,0:T(8,128)(2,1)}, u32[]{:S(2)}) copy-start(bf16[2,128,1024]{2,1,0:T(8,128)(2,1)} %ok_ref.3) | copy-start | bytes 1572868
  35.8 5.1 %collective-permute-start.2 = (f32[4,136,512]{2,1,0:T(8,128)S(1)}, f32[4,136,512]{2,1,0:T(8,128)S(1)}, u32[]{:S(2)}, u32[]{:S(2)}) collective-permute-start(f32[4,136,512]{2,1,0:T(8,128)S(1)} %get-tuple-element.8), channel_id=1, source_target_pairs={{0,1},{1,0},{2,3},{3,2},{4,5},{5,4},{6,7},{7,6},{8,9},{9,8},{10,11... | collective-permute-start | bytes 3342344 | tf_op jit(solution)/shard_map/ppermute | solution.py:255

commit v6 on v5

--- a/solution.py
+++ b/solution.py
@@ -80,11 +80,31 @@
         pair = [ref[s, :, head_lanes(i)].astype(f32) for s in range(2)]
         return jnp.concatenate(pair + [jnp.zeros((12, DH), f32)], axis=0).astype(bf16)
 
+    def products(i):
+        q = q_ref[:, pl.ds(pl.multiple_of((first + i) * 32, 32), 32), :].reshape(rows, DH)
+        return lax.dot_general(pk_ref[:, head_lanes(i)], q, NT, preferred_element_type=f32)
+
+    def weigh(scores):
+        peaks, ws = [], []
+        for b in range(n_blocks):
+            s = scores[b * BLK : (b + 1) * BLK]
+            peak = jnp.max(s, axis=0, keepdims=True)
+            ws.append(jnp.exp2((s - peak) * EXPO).astype(bf16))
+            peaks.append(peak)
+        return peaks, ws
+
+    def collect(i, ws):
+        outs = []
+        for b in range(n_blocks):
+            v = jnp.concatenate([pv_ref[b * BLK : (b + 1) * BLK, head_lanes(i)].T, ones], axis=0)
+            outs.append(jnp.dot(v, ws[b], preferred_element_type=f32)[0:136])
+        return outs
+
     key = lax.broadcasted_iota(jnp.int32, (BLK, DH), 0)
     lane = lax.broadcasted_iota(jnp.int32, (BLK, DH), 1)
     lane_head, lane_req, lane_step = lane // 32, lane % 2, lane // 2 % 2
     own_rows = pl.ds(pl.multiple_of(first * 32, DH), DH)
-    extra = []
+    stage = []
     for n in range(5):
         if n < 4:
             kr, vr = (ok_ref, ov_ref) if n < 2 else (xk_ref, xv_ref)
@@ -102,6 +122,10 @@
         every = lax.dot_general(
             jnp.concatenate(ks, axis=0), q_ref[dev, own_rows, :], NT, preferred_element_type=f32
         )
+        stage.append((n, vs, dev, live, count, every))
+    scores = [products(i) for i in range(HALF)]
+    weighed = []
+    for n, vs, dev, live, count, every in stage:
         s = every[0:count]
         for i in range(1, HALF):
             s = jnp.where(lane_head[0:count] == i, every[i * count : (i + 1) * count], s)
@@ -112,24 +136,19 @@
         if n == 4:
             ws.append(fill)
         v = jnp.concatenate([jnp.concatenate(vs, axis=1), jnp.concatenate([ones] * len(vs), axis=1)], axis=0)
+        weighed.append((dev, peak, v, ws))
+    extra = []
+    for dev, peak, v, ws in weighed:
         o = jnp.dot(v, jnp.concatenate(ws, axis=0), preferred_element_type=f32)[0:136]
         extra.append((dev, peak, o))
 
     spot = lax.broadcasted_iota(jnp.int32, (1, rows), 1) // 32
+    ready = weigh(scores[0])
     for i in range(HALF):
-        lanes = head_lanes(i)
-        qrows = pl.ds(pl.multiple_of((first + i) * 32, 32), 32)
-        q = q_ref[:, qrows, :].reshape(rows, DH)
-        scores = lax.dot_general(pk_ref[:, lanes], q, NT, preferred_element_type=f32)
-        peaks, outs = [], []
-        for b in range(n_blocks):
-            span = slice(b * BLK, (b + 1) * BLK)
-            s = scores[span]
-            peak = jnp.max(s, axis=0, keepdims=True)
-            w = jnp.exp2((s - peak) * EXPO).astype(bf16)
-            v = jnp.concatenate([pv_ref[span, lanes].T, ones], axis=0)
-            peaks.append(peak)
-            outs.append(jnp.dot(v, w, preferred_element_type=f32)[0:136])
+        peaks, ws = ready
+        outs = collect(i, ws)
+        if i + 1 < HALF:
+            ready = weigh(scores[i + 1])
         wides = []
         for dev, peak, o in extra:
             turn = (dev + (4 - i)) % 4 * 32

time: 64.1 us -> 63.2 us (0.986)
  Pallas kernels: 7.14 us -> 6.2 us
  transfers between devices with their start and end apart: 3 -> 3, of which waited for: 0 -> 1; matrix products, arithmetic and copies ran while one was open for 2% -> 2% of each run, Pallas kernels for 5% -> 4%
where the time goes in v6:
time: 63.2 us; the launch traced here: 62.9 us
  blocking collectives  45.8 us (72%)
  starting transfers between devices  7.92 us (13%)
  Pallas kernels  6.2 us (10%)
  other arithmetic  1.34 us (2%)
  local copies, waits for them, and re-layouts  1.31 us (2%)
    all_gather x1, blocking collectives, per_device(): group = lax.all_gather(own, 'prefix', axis=0)  24.7 us
    all_to_all x1, blocking collectives, per_device(): lax.all_to_all(merged.astype(jnp.float16), 'prefix', 0, 0, tiled=True)  21.1 us
    ppermute x1, starting transfers between devices, per_device(): far_keys = lax.ppermute(pool_keys, 'req', swap)  3.94 us
    pallas_call x1, Pallas kernels, per_device(): call(functools.partial(attend_kernel, False), part, [VM] * 9 + [SM], name...  2.43 us
    pallas_call x1, Pallas kernels, per_device(): call(functools.partial(attend_kernel, True), (part, sds((4, 3), jnp.int32...  2.19 us
    ppermute x1, starting transfers between devices, per_device(): theirs = lax.ppermute(other, 'prefix', core)  2.06 us
    ppermute x1, starting transfers between devices, per_device(): far_values = lax.ppermute(pool_values, 'req', swap)  1.92 us
  transfers between devices with their start and end apart: 3, of which 1 were waited for; matrix products, arithmetic and copies ran while one was open for 2% of the time, Pallas kernels for 4%

profile of v6, /device:TPU:1, one launch (start us, length us, event | category | flops | bytes accessed | tf_op | source)
XLA Modules:
  0.0 62.9 jit_solution(16555896980264724789)
XLA Ops:
  0.0 3.9 %collective-permute-start = (bf16[2,128,1024]{2,1,0:T(8,128)(2,1)}, bf16[2,128,1024]{2,1,0:T(8,128)(2,1)S(1)}, u32[]{:S(2)}, u32[]{:S(2)}) collective-permute-start(bf16[2,128,1024]{2,1,0:T(8,128)(2,1)} %ok_ref.3), channel_id=1, source_target_pairs={{0,16},{16,0},{32,48},{48,32},{64,80},{80,64},{96,112},{112,96},{1... | collective-permute-start | bytes 1572872 | tf_op jit(solution)/shard_map/ppermute | solution.py:252
  3.9 1.9 %collective-permute-start.1 = (bf16[2,128,1024]{2,1,0:T(8,128)(2,1)}, bf16[2,128,1024]{2,1,0:T(8,128)(2,1)S(1)}, u32[]{:S(2)}, u32[]{:S(2)}) collective-permute-start(bf16[2,128,1024]{2,1,0:T(8,128)(2,1)} %ov_ref.3), channel_id=1, source_target_pairs={{0,16},{16,0},{32,48},{48,32},{64,80},{80,64},{96,112},{112,96},{1... | collective-permute-start | bytes 1572872 | tf_op jit(solution)/shard_map/ppermute | solution.py:253
  5.9 0.9 %multiply_convert_fusion.1 = f16[2,2,8192]{2,1,0:T(2,128)(2,1)S(1)} fusion(bf16[2,2,8192]{2,1,0:T(2,128)(2,1)} %param.9), kind=kLoop, calls=%fused_computation.1 | loop fusion | flops 98304 | bytes 131072 | tf_op jit(solution)/shard_map/convert_element_type | solution.py:255
  6.8 0.1 reshape.6
  6.9 0.1 copy.11
  6.9 0.0 copy-start.3
  6.9 0.0 copy-start.4
  7.0 0.0 copy-start.5
  7.0 0.0 copy-start.6
  7.0 0.0 copy-start.7
  7.0 24.7 %all-gather.1 = f16[16,256,128]{2,1,0:T(8,128)(2,1)S(1)} all-gather(f16[1,256,128]{2,1,0:T(8,128)(2,1)S(1)} %bitcast.7), channel_id=1, replica_groups=mesh['req'=32,'prefix'=16] {'prefix'}, dimensions={0}, use_global_device_ids=true | all-gather | bytes 1114112 | tf_op jit(solution)/shard_map/all_gather | solution.py:257
  31.7 0.0 copy-start
  31.7 0.0 copy-start.1
  31.7 0.0 copy-start.2
  31.7 0.3 multiply_convert_fusion.q_ref
  31.9 0.0 collective-permute-done.xk_ref
  32.0 0.0 collective-permute-done.1.xv_ref
  32.0 0.0 copy-done.3
  32.0 0.0 copy-done.4
  32.0 0.0 copy-done.5
  32.0 0.0 copy-done.6
  32.0 0.0 copy-done.7
  32.0 0.8 %copy-done = bf16[384,1024]{1,0:T(8,128)(2,1)S(1)} copy-done((bf16[384,1024]{1,0:T(8,128)(2,1)S(1)}, bf16[384,1024]{1,0:T(8,128)(2,1)}, u32[]{:S(2)}) %copy-start) | copy-done | bytes 786456
  32.8 0.2 copy-done.1
  33.0 0.1 copy-done.2
  33.2 2.2 %attend_other.1 = (f32[4,136,512]{2,1,0:T(8,128)S(1)}, s32[4,3]{1,0:T(4,128)S(1)}) custom-call(bf16[16,256,128]{2,1,0:T(8,128)(2,1)S(1)} %multiply_convert_fusion.q_ref, bf16[384,1024]{1,0:T(8,128)(2,1)S(1)} %copy-done, bf16[384,1024]{1,0:T(8,128)(2,1)S(1)} %copy-done.1, bf16[2,128,1024]{2,1,0:T(8,128)(2,1)S(1)} %copy-done.2, ...), custom_call_target="tpu_custom_call" | custom-call | flops 800000000 | bytes 6000000 | tf_op jit(solution)/shard_map/attend_other/pallas_call | solution.py:266
  35.4 2.1 %collective-permute-start.2 = (f32[4,136,512]{2,1,0:T(8,128)S(1)}, f32[4,136,512]{2,1,0:T(8,128)S(1)}, u32[]{:S(2)}, u32[]{:S(2)}) collective-permute-start(f32[4,136,512]{2,1,0:T(8,128)S(1)} %get-tuple-element.8), channel_id=1, source_target_pairs={{0,1},{1,0},{2,3},{3,2},{4,5},{5,4},{6,7},{7,6},{8,9},{9,8},{10,11... | collective-permute-start | bytes 3342344 | tf_op jit(solution)/shard_map/ppermute | solution.py:274
  37.4 2.4 %attend_own.1.a_ref = f32[4,136,512]{2,1,0:T(8,128)S(1)} custom-call(bf16[16,256,128]{2,1,0:T(8,128)(2,1)S(1)} %multiply_convert_fusion.q_ref, bf16[384,1024]{1,0:T(8,128)(2,1)S(1)} %copy-done, bf16[384,1024]{1,0:T(8,128)(2,1)S(1)} %copy-done.1, bf16[2,128,1024]{2,1,0:T(8,128)(2,1)S(1)} %copy-done.2, bf16[2,128,1024]{2,1,0:T(8,128)(2,1)S(1)} %copy-done.3, ...), custom_call_target="tpu_custom_call" | custom-call | flops 800000000 | bytes 6000000 | tf_op jit(solution)/shard_map/attend_own/pallas_call | solution.py:275
  39.9 0.1 collective-permute-done.2.b_ref
  40.0 0.4 core_merge.1
  40.4 0.1 convert_element_type.22
  40.5 21.1 %all_to_all.5 = f16[16,136,128]{2,1,0:T(8,128)(2,1)S(1)} all-to-all(f16[16,136,128]{2,1,0:T(8,128)(2,1)S(1)} %convert_element_type.22), channel_id=1, replica_groups=mesh['req'=32,'prefix'=16] {'prefix'}, dimensions={0} | all-to-all | bytes 1114112 | tf_op jit(solution)/shard_map/all_to_all | solution.py:281
  61.6 0.1 convert_element_type.23.z_ref
  61.7 1.2 %final.1 = bf16[2,2,8192]{2,1,0:T(2,128)(2,1)} custom-call(f32[16,136,128]{2,1,0:T(8,128)S(1)} %convert_element_type.23.z_ref), custom_call_target="tpu_custom_call" | custom-call | bytes 1000000 | tf_op jit(solution)/shard_map/final/pallas_call | solution.py:282
Async XLA Ops:
  0.0 31.9 %collective-permute-start = (bf16[2,128,1024]{2,1,0:T(8,128)(2,1)}, bf16[2,128,1024]{2,1,0:T(8,128)(2,1)S(1)}, u32[]{:S(2)}, u32[]{:S(2)}) collective-permute-start(bf16[2,128,1024]{2,1,0:T(8,128)(2,1)} %ok_ref.3), channel_id=1, source_target_pairs={{0,16},{16,0},{32,48},{48,32},{64,80},{80,64},{96,112},{112,96},{1... | collective-permute-start | bytes 1572872 | tf_op jit(solution)/shard_map/ppermute | solution.py:252
  3.9 28.0 %collective-permute-start.1 = (bf16[2,128,1024]{2,1,0:T(8,128)(2,1)}, bf16[2,128,1024]{2,1,0:T(8,128)(2,1)S(1)}, u32[]{:S(2)}, u32[]{:S(2)}) collective-permute-start(bf16[2,128,1024]{2,1,0:T(8,128)(2,1)} %ov_ref.3), channel_id=1, source_target_pairs={{0,16},{16,0},{32,48},{48,32},{64,80},{80,64},{96,112},{112,96},{1... | collective-permute-start | bytes 1572872 | tf_op jit(solution)/shard_map/ppermute | solution.py:253
  6.9 25.0 %copy-start.3 = (bf16[2,128,1024]{2,1,0:T(8,128)(2,1)S(1)}, bf16[2,128,1024]{2,1,0:T(8,128)(2,1)}, u32[]{:S(2)}) copy-start(bf16[2,128,1024]{2,1,0:T(8,128)(2,1)} %ov_ref.3) | copy-start | bytes 1572868
  6.9 25.0 %copy-start.4 = (s32[1024,16]{0,1:T(8,128)S(1)}, s32[1024,16]{0,1:T(8,128)}, u32[]{:S(2)}) copy-start(s32[1024,16]{0,1:T(8,128)} %param.16) | copy-start | bytes 196612
  7.0 25.0 %copy-start.5 = (bf16[2,2,1024]{2,1,0:T(2,128)(2,1)S(1)}, bf16[2,2,1024]{2,1,0:T(2,128)(2,1)}, u32[]{:S(2)}) copy-start(bf16[2,2,1024]{2,1,0:T(2,128)(2,1)} %nk_ref.3) | copy-start | bytes 24580
  7.0 25.0 %copy-start.6 = (bf16[2,2,1024]{2,1,0:T(2,128)(2,1)S(1)}, bf16[2,2,1024]{2,1,0:T(2,128)(2,1)}, u32[]{:S(2)}) copy-start(bf16[2,2,1024]{2,1,0:T(2,128)(2,1)} %nv_ref.3) | copy-start | bytes 24580
  7.0 25.0 %copy-start.7 = (s32[1024]{0:T(1024)S(1)}, s32[1024]{0:T(1024)}, u32[]{:S(2)}) copy-start(s32[1024]{0:T(1024)} %param.17) | copy-start | bytes 12292
  31.7 1.1 %copy-start = (bf16[384,1024]{1,0:T(8,128)(2,1)S(1)}, bf16[384,1024]{1,0:T(8,128)(2,1)}, u32[]{:S(2)}) copy-start(bf16[384,1024]{1,0:T(8,128)(2,1)} %pk_ref.3) | copy-start | bytes 2359300
  31.7 1.4 %copy-start.1 = (bf16[384,1024]{1,0:T(8,128)(2,1)S(1)}, bf16[384,1024]{1,0:T(8,128)(2,1)}, u32[]{:S(2)}) copy-start(bf16[384,1024]{1,0:T(8,128)(2,1)} %pv_ref.3) | copy-start | bytes 2359300
  31.7 1.5 %copy-start.2 = (bf16[2,128,1024]{2,1,0:T(8,128)(2,1)S(1)}, bf16[2,128,1024]{2,1,0:T(8,128)(2,1)}, u32[]{:S(2)}) copy-start(bf16[2,128,1024]{2,1,0:T(8,128)(2,1)} %ok_ref.3) | copy-start | bytes 1572868
  35.4 4.6 %collective-permute-start.2 = (f32[4,136,512]{2,1,0:T(8,128)S(1)}, f32[4,136,512]{2,1,0:T(8,128)S(1)}, u32[]{:S(2)}, u32[]{:S(2)}) collective-permute-start(f32[4,136,512]{2,1,0:T(8,128)S(1)} %get-tuple-element.8), channel_id=1, source_target_pairs={{0,1},{1,0},{2,3},{3,2},{4,5},{5,4},{6,7},{7,6},{8,9},{9,8},{10,11... | collective-permute-start | bytes 3342344 | tf_op jit(solution)/shard_map/ppermute | solution.py:274

commit v7 on v6

--- a/solution.py
+++ b/solution.py
@@ -24,7 +24,6 @@
 f32 = jnp.float32
 NT = (((1,), (1,)), ((), ()))
 VM = pl.BlockSpec(memory_space=pltpu.VMEM)
-SM = pl.BlockSpec(memory_space=pltpu.SMEM)
 
 
 def find_owners(len_ref, table_ref, meta_ref):
@@ -56,16 +55,14 @@
 
 
 def attend_kernel(
-    flip, q_ref, pk_ref, pv_ref, ok_ref, ov_ref, xk_ref, xv_ref, nk_ref, nv_ref, *refs
+    flip, q_ref, pk_ref, pv_ref, ok_ref, ov_ref, xk_ref, xv_ref, nk_ref, nv_ref, len_ref, table_ref,
+    out_ref, meta_ref,
 ):
     pre = lax.axis_index("prefix")
     half = pre % 2
     if flip:
         half = 1 - half
-        len_ref, table_ref, out_ref, meta_ref = refs
-        find_owners(len_ref, table_ref, meta_ref)
-    else:
-        meta_ref, out_ref = refs
+    find_owners(len_ref, table_ref, meta_ref)
     n_dev = q_ref.shape[0]
     rows = n_dev * 32
     n_quads = n_dev // 4
@@ -258,23 +255,24 @@
     group = (group.astype(f32) * (1.0 / QLIFT)).astype(bf16)
     rows = n_pre * 32
 
-    common = (
-        group, prefix_keys, prefix_values, pool_keys, pool_values, far_keys, far_values, new_keys, new_values
-    )
-    part = sds((HALF, 136, rows), f32)
-    cost = dict(flops=800_000_000, moved=6_000_000)
-    other, meta = call(
-        functools.partial(attend_kernel, True),
-        (part, sds((4, 3), jnp.int32)),
-        [VM] * 11,
-        (VM, SM),
-        name="attend_other",
-        **cost,
-    )(*common, suffix_lengths.reshape(-1, 128), block_table.T)
-    theirs = lax.ppermute(other, "prefix", core)
-    mine = call(
-        functools.partial(attend_kernel, False), part, [VM] * 9 + [SM], name="attend_own", **cost
-    )(*common, meta)
+
+    def attend(flip):
+        return call(
+            functools.partial(attend_kernel, flip),
+            sds((HALF, 136, rows), f32),
+            [VM] * 11,
+            VM,
+            [pltpu.SMEM((4, 3), jnp.int32)],
+            flops=800_000_000,
+            moved=6_000_000,
+            name="attend_other" if flip else "attend_own",
+        )(
+            group, prefix_keys, prefix_values, pool_keys, pool_values, far_keys, far_values,
+            new_keys, new_values, suffix_lengths.reshape(-1, 128), block_table.T,
+        )
+
+    theirs = lax.ppermute(attend(True), "prefix", core)
+    mine = attend(False)
     merged = call(core_merge_kernel, sds((n_pre, 136, DH), f32), [VM, VM], moved=4_000_000, name="core_merge")(
         mine, theirs
     )

time: 63.2 us -> 62.9 us (level)
  transfers between devices with their start and end apart: 3 -> 3, of which waited for: 1 -> 1; matrix products, arithmetic and copies ran while one was open for 2% -> 2% of each run, Pallas kernels for 4% -> 3%
where the time goes in v7:
time: 62.9 us; the launch traced here: 62.6 us
  blocking collectives  45.7 us (73%)
  starting transfers between devices  7.93 us (13%)
  Pallas kernels  5.57 us (9%)
  other arithmetic  1.34 us (2%)
  local copies, waits for them, and re-layouts  1.31 us (2%)
    all_gather x1, blocking collectives, per_device(): group = lax.all_gather(own, 'prefix', axis=0)  24.7 us
    all_to_all x1, blocking collectives, per_device(): lax.all_to_all(merged.astype(jnp.float16), 'prefix', 0, 0, tiled=True)  21 us
    pallas_call x2, Pallas kernels, attend(): call(functools.partial(attend_kernel, flip), sds((HALF, 136, rows), f32),...  4.02 us
    ppermute x1, starting transfers between devices, per_device(): far_keys = lax.ppermute(pool_keys, 'req', swap)  3.94 us
    ppermute x1, starting transfers between devices, per_device(): theirs = lax.ppermute(attend(True), 'prefix', core)  2.07 us
    ppermute x1, starting transfers between devices, per_device(): far_values = lax.ppermute(pool_values, 'req', swap)  1.92 us
  transfers between devices with their start and end apart: 3, of which 1 were waited for; matrix products, arithmetic and copies ran while one was open for 2% of the time, Pallas kernels for 3%

profile of v7, /device:TPU:1, one launch (start us, length us, event | category | flops | bytes accessed | tf_op | source)
XLA Modules:
  0.0 62.6 jit_solution(1423812980824467369)
XLA Ops:
  0.0 3.9 %collective-permute-start = (bf16[2,128,1024]{2,1,0:T(8,128)(2,1)}, bf16[2,128,1024]{2,1,0:T(8,128)(2,1)S(1)}, u32[]{:S(2)}, u32[]{:S(2)}) collective-permute-start(bf16[2,128,1024]{2,1,0:T(8,128)(2,1)} %ok_ref.3), channel_id=1, source_target_pairs={{0,16},{16,0},{32,48},{48,32},{64,80},{80,64},{96,112},{112,96},{1... | collective-permute-start | bytes 1572872 | tf_op jit(solution)/shard_map/ppermute | solution.py:249
  3.9 1.9 %collective-permute-start.1 = (bf16[2,128,1024]{2,1,0:T(8,128)(2,1)}, bf16[2,128,1024]{2,1,0:T(8,128)(2,1)S(1)}, u32[]{:S(2)}, u32[]{:S(2)}) collective-permute-start(bf16[2,128,1024]{2,1,0:T(8,128)(2,1)} %ov_ref.3), channel_id=1, source_target_pairs={{0,16},{16,0},{32,48},{48,32},{64,80},{80,64},{96,112},{112,96},{1... | collective-permute-start | bytes 1572872 | tf_op jit(solution)/shard_map/ppermute | solution.py:250
  5.9 0.9 %multiply_convert_fusion.1 = f16[2,2,8192]{2,1,0:T(2,128)(2,1)S(1)} fusion(bf16[2,2,8192]{2,1,0:T(2,128)(2,1)} %param.9), kind=kLoop, calls=%fused_computation.1 | loop fusion | flops 98304 | bytes 131072 | tf_op jit(solution)/shard_map/convert_element_type | solution.py:252
  6.8 0.1 reshape.7
  6.9 0.1 copy.11
  6.9 0.0 copy-start.3
  6.9 0.0 copy-start.4
  7.0 0.0 copy-start.5
  7.0 0.0 copy-start.6
  7.0 0.0 copy-start.7
  7.0 24.7 %all-gather.1 = f16[16,256,128]{2,1,0:T(8,128)(2,1)S(1)} all-gather(f16[1,256,128]{2,1,0:T(8,128)(2,1)S(1)} %bitcast.9), channel_id=1, replica_groups=mesh['req'=32,'prefix'=16] {'prefix'}, dimensions={0}, use_global_device_ids=true | all-gather | bytes 1114112 | tf_op jit(solution)/shard_map/all_gather | solution.py:254
  31.7 0.0 copy-start
  31.7 0.0 copy-start.1
  31.7 0.0 copy-start.2
  31.7 0.3 multiply_convert_fusion.q_ref
  31.9 0.0 collective-permute-done.xk_ref
  32.0 0.0 collective-permute-done.1.xv_ref
  32.0 0.0 copy-done.3
  32.0 0.0 copy-done.4
  32.0 0.0 copy-done.5
  32.0 0.0 copy-done.6
  32.0 0.0 copy-done.7
  32.0 0.8 %copy-done = bf16[384,1024]{1,0:T(8,128)(2,1)S(1)} copy-done((bf16[384,1024]{1,0:T(8,128)(2,1)S(1)}, bf16[384,1024]{1,0:T(8,128)(2,1)}, u32[]{:S(2)}) %copy-start) | copy-done | bytes 786456
  32.8 0.2 copy-done.1
  33.0 0.1 copy-done.2
  33.2 2.0 %attend_other.1 = f32[4,136,512]{2,1,0:T(8,128)S(1)} custom-call(bf16[16,256,128]{2,1,0:T(8,128)(2,1)S(1)} %multiply_convert_fusion.q_ref, bf16[384,1024]{1,0:T(8,128)(2,1)S(1)} %copy-done, bf16[384,1024]{1,0:T(8,128)(2,1)S(1)} %copy-done.1, bf16[2,128,1024]{2,1,0:T(8,128)(2,1)S(1)} %copy-done.2, bf16[2,128,1024]{2,1,0:T(8,128)(2,1)S(1)} %copy-done.3, ...), custom_call_target="tpu_custom_call" | custom-call | flops 800000000 | bytes 6000000 | tf_op jit(solution)/shard_map/attend_other/pallas_call | solution.py:260
  35.2 2.1 %collective-permute-start.2 = (f32[4,136,512]{2,1,0:T(8,128)S(1)}, f32[4,136,512]{2,1,0:T(8,128)S(1)}, u32[]{:S(2)}, u32[]{:S(2)}) collective-permute-start(f32[4,136,512]{2,1,0:T(8,128)S(1)} %attend_other.1), channel_id=1, source_target_pairs={{0,1},{1,0},{2,3},{3,2},{4,5},{5,4},{6,7},{7,6},{8,9},{9,8},{10,11... | collective-permute-start | bytes 3342344 | tf_op jit(solution)/shard_map/ppermute | solution.py:274
  37.2 2.0 %attend_own.1.a_ref = f32[4,136,512]{2,1,0:T(8,128)S(1)} custom-call(bf16[16,256,128]{2,1,0:T(8,128)(2,1)S(1)} %multiply_convert_fusion.q_ref, bf16[384,1024]{1,0:T(8,128)(2,1)S(1)} %copy-done, bf16[384,1024]{1,0:T(8,128)(2,1)S(1)} %copy-done.1, bf16[2,128,1024]{2,1,0:T(8,128)(2,1)S(1)} %copy-done.2, bf16[2,128,1024]{2,1,0:T(8,128)(2,1)S(1)} %copy-done.3, ...), custom_call_target="tpu_custom_call" | custom-call | flops 800000000 | bytes 6000000 | tf_op jit(solution)/shard_map/attend_own/pallas_call | solution.py:260
  39.3 0.5 collective-permute-done.2.b_ref
  39.8 0.4 core_merge.1
  40.2 0.1 convert_element_type.22
  40.3 21.0 %all_to_all.5 = f16[16,136,128]{2,1,0:T(8,128)(2,1)S(1)} all-to-all(f16[16,136,128]{2,1,0:T(8,128)(2,1)S(1)} %convert_element_type.22), channel_id=1, replica_groups=mesh['req'=32,'prefix'=16] {'prefix'}, dimensions={0} | all-to-all | bytes 1114112 | tf_op jit(solution)/shard_map/all_to_all | solution.py:279
  61.3 0.1 convert_element_type.23.z_ref
  61.4 1.2 %final.1 = bf16[2,2,8192]{2,1,0:T(2,128)(2,1)} custom-call(f32[16,136,128]{2,1,0:T(8,128)S(1)} %convert_element_type.23.z_ref), custom_call_target="tpu_custom_call" | custom-call | bytes 1000000 | tf_op jit(solution)/shard_map/final/pallas_call | solution.py:280
Async XLA Ops:
  0.0 31.9 %collective-permute-start = (bf16[2,128,1024]{2,1,0:T(8,128)(2,1)}, bf16[2,128,1024]{2,1,0:T(8,128)(2,1)S(1)}, u32[]{:S(2)}, u32[]{:S(2)}) collective-permute-start(bf16[2,128,1024]{2,1,0:T(8,128)(2,1)} %ok_ref.3), channel_id=1, source_target_pairs={{0,16},{16,0},{32,48},{48,32},{64,80},{80,64},{96,112},{112,96},{1... | collective-permute-start | bytes 1572872 | tf_op jit(solution)/shard_map/ppermute | solution.py:249
  3.9 28.0 %collective-permute-start.1 = (bf16[2,128,1024]{2,1,0:T(8,128)(2,1)}, bf16[2,128,1024]{2,1,0:T(8,128)(2,1)S(1)}, u32[]{:S(2)}, u32[]{:S(2)}) collective-permute-start(bf16[2,128,1024]{2,1,0:T(8,128)(2,1)} %ov_ref.3), channel_id=1, source_target_pairs={{0,16},{16,0},{32,48},{48,32},{64,80},{80,64},{96,112},{112,96},{1... | collective-permute-start | bytes 1572872 | tf_op jit(solution)/shard_map/ppermute | solution.py:250
  6.9 25.0 %copy-start.3 = (bf16[2,128,1024]{2,1,0:T(8,128)(2,1)S(1)}, bf16[2,128,1024]{2,1,0:T(8,128)(2,1)}, u32[]{:S(2)}) copy-start(bf16[2,128,1024]{2,1,0:T(8,128)(2,1)} %ov_ref.3) | copy-start | bytes 1572868
  6.9 25.0 %copy-start.4 = (s32[1024,16]{0,1:T(8,128)S(1)}, s32[1024,16]{0,1:T(8,128)}, u32[]{:S(2)}) copy-start(s32[1024,16]{0,1:T(8,128)} %param.16) | copy-start | bytes 196612
  7.0 25.0 %copy-start.5 = (bf16[2,2,1024]{2,1,0:T(2,128)(2,1)S(1)}, bf16[2,2,1024]{2,1,0:T(2,128)(2,1)}, u32[]{:S(2)}) copy-start(bf16[2,2,1024]{2,1,0:T(2,128)(2,1)} %nk_ref.3) | copy-start | bytes 24580
  7.0 25.0 %copy-start.6 = (bf16[2,2,1024]{2,1,0:T(2,128)(2,1)S(1)}, bf16[2,2,1024]{2,1,0:T(2,128)(2,1)}, u32[]{:S(2)}) copy-start(bf16[2,2,1024]{2,1,0:T(2,128)(2,1)} %nv_ref.3) | copy-start | bytes 24580
  7.0 25.0 %copy-start.7 = (s32[1024]{0:T(1024)S(1)}, s32[1024]{0:T(1024)}, u32[]{:S(2)}) copy-start(s32[1024]{0:T(1024)} %param.17) | copy-start | bytes 12292
  31.7 1.1 %copy-start = (bf16[384,1024]{1,0:T(8,128)(2,1)S(1)}, bf16[384,1024]{1,0:T(8,128)(2,1)}, u32[]{:S(2)}) copy-start(bf16[384,1024]{1,0:T(8,128)(2,1)} %pk_ref.3) | copy-start | bytes 2359300
  31.7 1.4 %copy-start.1 = (bf16[384,1024]{1,0:T(8,128)(2,1)S(1)}, bf16[384,1024]{1,0:T(8,128)(2,1)}, u32[]{:S(2)}) copy-start(bf16[384,1024]{1,0:T(8,128)(2,1)} %pv_ref.3) | copy-start | bytes 2359300
  31.7 1.5 %copy-start.2 = (bf16[2,128,1024]{2,1,0:T(8,128)(2,1)S(1)}, bf16[2,128,1024]{2,1,0:T(8,128)(2,1)}, u32[]{:S(2)}) copy-start(bf16[2,128,1024]{2,1,0:T(8,128)(2,1)} %ok_ref.3) | copy-start | bytes 1572868
  35.2 4.6 %collective-permute-start.2 = (f32[4,136,512]{2,1,0:T(8,128)S(1)}, f32[4,136,512]{2,1,0:T(8,128)S(1)}, u32[]{:S(2)}, u32[]{:S(2)}) collective-permute-start(f32[4,136,512]{2,1,0:T(8,128)S(1)} %attend_other.1), channel_id=1, source_target_pairs={{0,1},{1,0},{2,3},{3,2},{4,5},{5,4},{6,7},{7,6},{8,9},{9,8},{10,11... | collective-permute-start | bytes 3342344 | tf_op jit(solution)/shard_map/ppermute | solution.py:274

commit v8 on v7

--- a/solution.py
+++ b/solution.py
@@ -55,7 +55,7 @@
 
 
 def attend_kernel(
-    flip, q_ref, pk_ref, pv_ref, ok_ref, ov_ref, xk_ref, xv_ref, nk_ref, nv_ref, len_ref, table_ref,
+    flip, q_ref, pk_ref, pv_ref, own_ref, far_ref, nk_ref, nv_ref, len_ref, table_ref,
     out_ref, meta_ref,
 ):
     pre = lax.axis_index("prefix")
@@ -104,9 +104,9 @@
     stage = []
     for n in range(5):
         if n < 4:
-            kr, vr = (ok_ref, ov_ref) if n < 2 else (xk_ref, xv_ref)
-            ks = [kr[n % 2, :, head_lanes(i)] for i in range(HALF)]
-            vs = [vr[n % 2, :, head_lanes(i)].T for i in range(HALF)]
+            pool = own_ref if n < 2 else far_ref
+            ks = [pool[0, n % 2, :, head_lanes(i)] for i in range(HALF)]
+            vs = [pool[1, n % 2, :, head_lanes(i)].T for i in range(HALF)]
             dev = meta_ref[n, 0]
             live = key < jnp.where(lane_req == meta_ref[n, 1], meta_ref[n, 2], 0)
         else:
@@ -246,8 +246,8 @@
     n_pre = lax.axis_size("prefix")
     swap = [(i, i ^ 1) for i in range(n_req)]
     core = [(i, i ^ 1) for i in range(n_pre)]
-    far_keys = lax.ppermute(pool_keys, "req", swap)
-    far_values = lax.ppermute(pool_values, "req", swap)
+    pool = jnp.stack([pool_keys, pool_values])
+    far = lax.ppermute(pool, "req", swap)
     sds = jax.ShapeDtypeStruct
     own = (queries.astype(f32) * QLIFT).astype(jnp.float16)
     own = own.reshape(4, H, DH).transpose(1, 0, 2).reshape(4 * H, DH)
@@ -260,15 +260,15 @@
         return call(
             functools.partial(attend_kernel, flip),
             sds((HALF, 136, rows), f32),
-            [VM] * 11,
+            [VM] * 9,
             VM,
             [pltpu.SMEM((4, 3), jnp.int32)],
             flops=800_000_000,
             moved=6_000_000,
             name="attend_other" if flip else "attend_own",
         )(
-            group, prefix_keys, prefix_values, pool_keys, pool_values, far_keys, far_values,
-            new_keys, new_values, suffix_lengths.reshape(-1, 128), block_table.T,
+            group, prefix_keys, prefix_values, pool, far, new_keys, new_values,
+            suffix_lengths.reshape(-1, 128), block_table.T,
         )
 
     theirs = lax.ppermute(attend(True), "prefix", core)

time: 62.9 us -> 63.6 us (1.011)
  blocking collectives: 45.7 us -> 48.1 us
  starting transfers between devices: 7.93 us -> 6.01 us
    all_to_all x1, blocking collectives: 21 us -> 25.5 us  [per_device(): lax.all_to_all(merged.astype(jnp.float16), 'prefix', 0, 0, tiled=True)]
    all_gather x1, blocking collectives: 24.7 us -> 22.5 us  [per_device(): group = lax.all_gather(own, 'prefix', axis=0)]
    ppermute x2 -> x1, starting transfers between devices: 5.86 us -> 3.95 us  [per_device(): far = lax.ppermute(pool, 'req', swap)]
    another operation x0 -> x1, other arithmetic: none -> 1.33 us  [per_device(): pool = jnp.stack([pool_keys, pool_values])]
    convert_element_type x1, other arithmetic: 0.91 us -> 0.07 us  [per_device(): own = (queries.astype(f32) * QLIFT).astype(jnp.float16)]
  transfers between devices with their start and end apart: 3 -> 2, of which waited for: 1 -> 1; matrix products, arithmetic and copies ran while one was open for 2% -> 1% of each run, Pallas kernels for 3% -> 3%
where the time goes in v8:
time: 63.6 us; the launch traced here: 63.4 us
  blocking collectives  48.1 us (76%)
  starting transfers between devices  6.01 us (9%)
  Pallas kernels  5.63 us (9%)
  other arithmetic  1.83 us (3%)
  local copies, waits for them, and re-layouts  1.19 us (2%)
    all_to_all x1, blocking collectives, per_device(): lax.all_to_all(merged.astype(jnp.float16), 'prefix', 0, 0, tiled=True)  25.5 us
    all_gather x1, blocking collectives, per_device(): group = lax.all_gather(own, 'prefix', axis=0)  22.5 us
    pallas_call x2, Pallas kernels, attend(): call(functools.partial(attend_kernel, flip), sds((HALF, 136, rows), f32),...  4.07 us
    ppermute x1, starting transfers between devices, per_device(): far = lax.ppermute(pool, 'req', swap)  3.95 us
    ppermute x1, starting transfers between devices, per_device(): theirs = lax.ppermute(attend(True), 'prefix', core)  2.07 us
    another operation x1, other arithmetic, per_device(): pool = jnp.stack([pool_keys, pool_values])  1.33 us
  transfers between devices with their start and end apart: 2, of which 1 were waited for; matrix products, arithmetic and copies ran while one was open for 1% of the time, Pallas kernels for 3%

profile of v8, /device:TPU:1, one launch (start us, length us, event | category | flops | bytes accessed | tf_op | source)
XLA Modules:
  0.0 63.4 jit_solution(1786501122440091332)
XLA Ops:
  0.0 0.0 copy-start.6
  0.0 1.3 %pad_maximum_fusion.own_ref = bf16[2,2,128,1024]{3,2,1,0:T(8,128)(2,1)S(1)} fusion(bf16[1,2,128,1024]{3,2,1,0:T(8,128)(2,1)} %bitcast.11, bf16[1,2,128,1024]{3,2,1,0:T(8,128)(2,1)} %bitcast.12), kind=kLoop, calls=%fused_computation.1 | loop fusion | flops 524288 | bytes 2097152 | tf_op jit(solution)/shard_map/stack | solution.py:249
  1.3 3.9 %collective-permute-start = (bf16[2,2,128,1024]{3,2,1,0:T(8,128)(2,1)S(1)}, bf16[2,2,128,1024]{3,2,1,0:T(8,128)(2,1)S(1)}, u32[]{:S(2)}, u32[]{:S(2)}) collective-permute-start(bf16[2,2,128,1024]{3,2,1,0:T(8,128)(2,1)S(1)} %pad_maximum_fusion.own_ref), channel_id=1, source_target_pairs={{0,16},{16,0},{32,48},{48,32},{64,80},{80,64},{96,112},{112,96},{1... | collective-permute-start | bytes 3145736 | tf_op jit(solution)/shard_map/ppermute | solution.py:250
  5.3 0.0 copy-done.6
  5.3 0.1 multiply_convert_fusion.1
  5.4 0.1 reshape.7
  5.5 0.1 copy.11
  5.5 22.5 %all-gather.1 = f16[16,256,128]{2,1,0:T(8,128)(2,1)S(1)} all-gather(f16[1,256,128]{2,1,0:T(8,128)(2,1)S(1)} %bitcast.13), channel_id=1, replica_groups=mesh['req'=32,'prefix'=16] {'prefix'}, dimensions={0}, use_global_device_ids=true | all-gather | bytes 1114112 | tf_op jit(solution)/shard_map/all_gather | solution.py:254
  28.0 0.0 copy-start
  28.0 0.0 copy-start.1
  28.1 0.0 copy-start.2
  28.1 0.0 copy-start.3
  28.1 0.0 copy-start.4
  28.1 0.0 copy-start.5
  28.1 0.3 multiply_convert_fusion.q_ref
  28.4 0.0 collective-permute-done.far_ref
  28.4 0.8 %copy-done = bf16[384,1024]{1,0:T(8,128)(2,1)S(1)} copy-done((bf16[384,1024]{1,0:T(8,128)(2,1)S(1)}, bf16[384,1024]{1,0:T(8,128)(2,1)}, u32[]{:S(2)}) %copy-start) | copy-done | bytes 786456
  29.2 0.2 copy-done.1
  29.4 0.0 copy-done.2
  29.4 0.0 copy-done.3
  29.4 0.0 copy-done.4
  29.4 0.0 copy-done.5
  29.4 2.0 %attend_other.1 = f32[4,136,512]{2,1,0:T(8,128)S(1)} custom-call(bf16[16,256,128]{2,1,0:T(8,128)(2,1)S(1)} %multiply_convert_fusion.q_ref, bf16[384,1024]{1,0:T(8,128)(2,1)S(1)} %copy-done, bf16[384,1024]{1,0:T(8,128)(2,1)S(1)} %copy-done.1, bf16[2,2,128,1024]{3,2,1,0:T(8,128)(2,1)S(1)} %pad_maximum_fusion.own_ref, ...), custom_call_target="tpu_custom_call" | custom-call | flops 800000000 | bytes 6000000 | tf_op jit(solution)/shard_map/attend_other/pallas_call | solution.py:260
  31.5 2.1 %collective-permute-start.1 = (f32[4,136,512]{2,1,0:T(8,128)S(1)}, f32[4,136,512]{2,1,0:T(8,128)S(1)}, u32[]{:S(2)}, u32[]{:S(2)}) collective-permute-start(f32[4,136,512]{2,1,0:T(8,128)S(1)} %attend_other.1), channel_id=1, source_target_pairs={{0,1},{1,0},{2,3},{3,2},{4,5},{5,4},{6,7},{7,6},{8,9},{9,8},{10,11... | collective-permute-start | bytes 3342344 | tf_op jit(solution)/shard_map/ppermute | solution.py:274
  33.5 2.0 %attend_own.1.a_ref = f32[4,136,512]{2,1,0:T(8,128)S(1)} custom-call(bf16[16,256,128]{2,1,0:T(8,128)(2,1)S(1)} %multiply_convert_fusion.q_ref, bf16[384,1024]{1,0:T(8,128)(2,1)S(1)} %copy-done, bf16[384,1024]{1,0:T(8,128)(2,1)S(1)} %copy-done.1, bf16[2,2,128,1024]{3,2,1,0:T(8,128)(2,1)S(1)} %pad_maximum_fusion.own_ref, ...), custom_call_target="tpu_custom_call" | custom-call | flops 800000000 | bytes 6000000 | tf_op jit(solution)/shard_map/attend_own/pallas_call | solution.py:260
  35.6 0.5 collective-permute-done.1.b_ref
  36.1 0.4 core_merge.1
  36.5 0.1 convert_element_type.22
  36.6 25.5 %all_to_all.5 = f16[16,136,128]{2,1,0:T(8,128)(2,1)S(1)} all-to-all(f16[16,136,128]{2,1,0:T(8,128)(2,1)S(1)} %convert_element_type.22), channel_id=1, replica_groups=mesh['req'=32,'prefix'=16] {'prefix'}, dimensions={0} | all-to-all | bytes 1114112 | tf_op jit(solution)/shard_map/all_to_all | solution.py:279
  62.1 0.1 convert_element_type.23.z_ref
  62.2 1.2 %final.1 = bf16[2,2,8192]{2,1,0:T(2,128)(2,1)} custom-call(f32[16,136,128]{2,1,0:T(8,128)S(1)} %convert_element_type.23.z_ref), custom_call_target="tpu_custom_call" | custom-call | bytes 1000000 | tf_op jit(solution)/shard_map/final/pallas_call | solution.py:280
Async XLA Ops:
  0.0 5.3 %copy-start.6 = (bf16[2,2,8192]{2,1,0:T(2,128)(2,1)S(1)}, bf16[2,2,8192]{2,1,0:T(2,128)(2,1)}, u32[]{:S(2)}) copy-start(bf16[2,2,8192]{2,1,0:T(2,128)(2,1)} %param.9) | copy-start | bytes 196612
  1.3 27.0 %collective-permute-start = (bf16[2,2,128,1024]{3,2,1,0:T(8,128)(2,1)S(1)}, bf16[2,2,128,1024]{3,2,1,0:T(8,128)(2,1)S(1)}, u32[]{:S(2)}, u32[]{:S(2)}) collective-permute-start(bf16[2,2,128,1024]{3,2,1,0:T(8,128)(2,1)S(1)} %pad_maximum_fusion.own_ref), channel_id=1, source_target_pairs={{0,16},{16,0},{32,48},{48,32},{64,80},{80,64},{96,112},{112,96},{1... | collective-permute-start | bytes 3145736 | tf_op jit(solution)/shard_map/ppermute | solution.py:250
  28.0 1.1 %copy-start = (bf16[384,1024]{1,0:T(8,128)(2,1)S(1)}, bf16[384,1024]{1,0:T(8,128)(2,1)}, u32[]{:S(2)}) copy-start(bf16[384,1024]{1,0:T(8,128)(2,1)} %pk_ref.3) | copy-start | bytes 2359300
  28.0 1.4 %copy-start.1 = (bf16[384,1024]{1,0:T(8,128)(2,1)S(1)}, bf16[384,1024]{1,0:T(8,128)(2,1)}, u32[]{:S(2)}) copy-start(bf16[384,1024]{1,0:T(8,128)(2,1)} %pv_ref.3) | copy-start | bytes 2359300
  28.1 1.4 %copy-start.2 = (s32[1024,16]{0,1:T(8,128)S(1)}, s32[1024,16]{0,1:T(8,128)}, u32[]{:S(2)}) copy-start(s32[1024,16]{0,1:T(8,128)} %param.16) | copy-start | bytes 196612
  28.1 1.4 %copy-start.3 = (bf16[2,2,1024]{2,1,0:T(2,128)(2,1)S(1)}, bf16[2,2,1024]{2,1,0:T(2,128)(2,1)}, u32[]{:S(2)}) copy-start(bf16[2,2,1024]{2,1,0:T(2,128)(2,1)} %nk_ref.3) | copy-start | bytes 24580
  28.1 1.4 %copy-start.4 = (bf16[2,2,1024]{2,1,0:T(2,128)(2,1)S(1)}, bf16[2,2,1024]{2,1,0:T(2,128)(2,1)}, u32[]{:S(2)}) copy-start(bf16[2,2,1024]{2,1,0:T(2,128)(2,1)} %nv_ref.3) | copy-start | bytes 24580
  28.1 1.4 %copy-start.5 = (s32[1024]{0:T(1024)S(1)}, s32[1024]{0:T(1024)}, u32[]{:S(2)}) copy-start(s32[1024]{0:T(1024)} %param.17) | copy-start | bytes 12292
  31.5 4.6 %collective-permute-start.1 = (f32[4,136,512]{2,1,0:T(8,128)S(1)}, f32[4,136,512]{2,1,0:T(8,128)S(1)}, u32[]{:S(2)}, u32[]{:S(2)}) collective-permute-start(f32[4,136,512]{2,1,0:T(8,128)S(1)} %attend_other.1), channel_id=1, source_target_pairs={{0,1},{1,0},{2,3},{3,2},{4,5},{5,4},{6,7},{7,6},{8,9},{9,8},{10,11... | collective-permute-start | bytes 3342344 | tf_op jit(solution)/shard_map/ppermute | solution.py:274

commit v9 on v8

--- a/solution.py
+++ b/solution.py
@@ -26,9 +26,8 @@
 VM = pl.BlockSpec(memory_space=pltpu.VMEM)
 
 
-def find_owners(len_ref, table_ref, meta_ref):
+def find_owners(homes, len_ref, table_ref, meta_ref):
     req = lax.axis_index("req")
-    pre = lax.axis_index("prefix")
     n_pre = lax.axis_size("prefix")
     pair_rows = 4 * n_pre
     per_line = 128 // pair_rows
@@ -41,8 +40,9 @@
     block = lax.broadcasted_iota(jnp.int32, table.shape, 0)
     left = jnp.broadcast_to(len_ref[pl.ds(line, 1), :], table.shape) - block * BLK
     usable = (left > 0) & (lane >= 0) & (lane < pair_rows)
-    for n in range(4):
-        holder = side if n < 2 else 1 - side
+    for n in range(2 * len(homes)):
+        near, pre = homes[n // 2]
+        holder = side if near else 1 - side
         slot = (holder * n_pre + pre) * 2 + n % 2
         hit = (table == slot) & usable
         found = jnp.sum(jnp.where(hit, lane * 256 + jnp.minimum(left, BLK), 0))
@@ -55,14 +55,16 @@
 
 
 def attend_kernel(
-    flip, q_ref, pk_ref, pv_ref, own_ref, far_ref, nk_ref, nv_ref, len_ref, table_ref,
-    out_ref, meta_ref,
+    flip, q_ref, pk_ref, pv_ref, nk_ref, nv_ref, len_ref, table_ref, *refs
 ):
     pre = lax.axis_index("prefix")
     half = pre % 2
     if flip:
         half = 1 - half
-    find_owners(len_ref, table_ref, meta_ref)
+    *pools, out_ref, meta_ref = refs
+    homes = [(True, pre), (False, pre), (False, pre + 1 - 2 * (pre % 2))][0 : len(pools)]
+    find_owners(homes, len_ref, table_ref, meta_ref)
+    n_slots = 2 * len(pools)
     n_dev = q_ref.shape[0]
     rows = n_dev * 32
     n_quads = n_dev // 4
@@ -102,11 +104,11 @@
     lane_head, lane_req, lane_step = lane // 32, lane % 2, lane // 2 % 2
     own_rows = pl.ds(pl.multiple_of(first * 32, DH), DH)
     stage = []
-    for n in range(5):
-        if n < 4:
-            pool = own_ref if n < 2 else far_ref
-            ks = [pool[0, n % 2, :, head_lanes(i)] for i in range(HALF)]
-            vs = [pool[1, n % 2, :, head_lanes(i)].T for i in range(HALF)]
+    for n in range(n_slots + 1):
+        if n < n_slots:
+            pool = pools[n // 2]
+            ks = [pool[0, n % 2, :, i * DH : (i + 1) * DH] for i in range(HALF)]
+            vs = [pool[1, n % 2, :, i * DH : (i + 1) * DH].T for i in range(HALF)]
             dev = meta_ref[n, 0]
             live = key < jnp.where(lane_req == meta_ref[n, 1], meta_ref[n, 2], 0)
         else:
@@ -130,7 +132,7 @@
         peak = jnp.max(s, axis=0, keepdims=True)
         w = jnp.where(live, jnp.exp2((s - peak) * EXPO), 0.0)
         ws = [jnp.where(lane_head[0:count] == i, w, 0.0).astype(bf16) for i in range(HALF)]
-        if n == 4:
+        if n == n_slots:
             ws.append(fill)
         v = jnp.concatenate([jnp.concatenate(vs, axis=1), jnp.concatenate([ones] * len(vs), axis=1)], axis=0)
         weighed.append((dev, peak, v, ws))
@@ -246,8 +248,15 @@
     n_pre = lax.axis_size("prefix")
     swap = [(i, i ^ 1) for i in range(n_req)]
     core = [(i, i ^ 1) for i in range(n_pre)]
+    across = [(i, (i ^ 1) ^ n_pre) for i in range(n_req * n_pre)]
     pool = jnp.stack([pool_keys, pool_values])
-    far = lax.ppermute(pool, "req", swap)
+    wide = HALF * DH
+    side = lax.axis_index("prefix") % 2
+    pool_same = lax.dynamic_slice_in_dim(pool, side * wide, wide, 3)
+    pool_cross = lax.dynamic_slice_in_dim(pool, (1 - side) * wide, wide, 3)
+    pool_same, pool_cross, queries = lax.optimization_barrier((pool_same, pool_cross, queries))
+    far_same = lax.ppermute(pool_same, "req", swap)
+    far_cross = lax.ppermute(pool_cross, ("req", "prefix"), across)
     sds = jax.ShapeDtypeStruct
     own = (queries.astype(f32) * QLIFT).astype(jnp.float16)
     own = own.reshape(4, H, DH).transpose(1, 0, 2).reshape(4 * H, DH)
@@ -256,23 +265,24 @@
     rows = n_pre * 32
 
 
-    def attend(flip):
+    def attend(flip, pools):
         return call(
             functools.partial(attend_kernel, flip),
             sds((HALF, 136, rows), f32),
-            [VM] * 9,
+            [VM] * (7 + len(pools)),
             VM,
-            [pltpu.SMEM((4, 3), jnp.int32)],
+            [pltpu.SMEM((2 * len(pools), 3), jnp.int32)],
             flops=800_000_000,
             moved=6_000_000,
             name="attend_other" if flip else "attend_own",
         )(
-            group, prefix_keys, prefix_values, pool, far, new_keys, new_values,
-            suffix_lengths.reshape(-1, 128), block_table.T,
+            group, prefix_keys, prefix_values, new_keys, new_values,
+            suffix_lengths.reshape(-1, 128), block_table.T, *pools,
         )
 
-    theirs = lax.ppermute(attend(True), "prefix", core)
-    mine = attend(False)
+    other, far_same, far_cross = lax.optimization_barrier((attend(True, [pool_cross]), far_same, far_cross))
+    theirs = lax.ppermute(other, "prefix", core)
+    mine = attend(False, [pool_same, far_same, far_cross])
     merged = call(core_merge_kernel, sds((n_pre, 136, DH), f32), [VM, VM], moved=4_000_000, name="core_merge")(
         mine, theirs
     )

time: 63.6 us -> 62 us (0.975)
  blocking collectives: 48.1 us -> 38.4 us
  starting transfers between devices: 6.01 us -> 14.4 us
    ppermute x2 -> x3, starting transfers between devices: 6.01 us -> 14.4 us  [the longest x1 8.38 us: per_device(): far_cross = lax.ppermute(pool_cross, ('req', 'prefix'), across)]
    all_gather x1, blocking collectives: 22.5 us -> 17.4 us  [per_device(): group = lax.all_gather(own, 'prefix', axis=0)]
    all_to_all x1, blocking collectives: 25.5 us -> 21 us  [per_device(): lax.all_to_all(merged.astype(jnp.float16), 'prefix', 0, 0, tiled=True)]
  transfers between devices with their start and end apart: 2 -> 3, of which waited for: 1 -> 1; matrix products, arithmetic and copies ran while one was open for 1% -> 1% of each run, Pallas kernels for 3% -> 7%
where the time goes in v9:
time: 62 us; the launch traced here: 61.8 us
  blocking collectives  38.4 us (62%)
  starting transfers between devices  14.4 us (23%)
  Pallas kernels  5.58 us (9%)
  other arithmetic  1.82 us (3%)
  local copies, waits for them, and re-layouts  1.2 us (2%)
    all_to_all x1, blocking collectives, per_device(): lax.all_to_all(merged.astype(jnp.float16), 'prefix', 0, 0, tiled=True)  21 us
    all_gather x1, blocking collectives, per_device(): group = lax.all_gather(own, 'prefix', axis=0)  17.4 us
    ppermute x1, starting transfers between devices, per_device(): far_cross = lax.ppermute(pool_cross, ('req', 'prefix'), across)  8.38 us
    pallas_call x2, Pallas kernels, attend(): call(functools.partial(attend_kernel, flip), sds((HALF, 136, rows), f32),...  4.03 us
    ppermute x1, starting transfers between devices, per_device(): far_same = lax.ppermute(pool_same, 'req', swap)  3.95 us
    ppermute x1, starting transfers between devices, per_device(): theirs = lax.ppermute(other, 'prefix', core)  2.06 us
    another operation x1, other arithmetic, per_device(): pool = jnp.stack([pool_keys, pool_values])  1.32 us
  transfers between devices with their start and end apart: 3, of which 1 were waited for; matrix products, arithmetic and copies ran while one was open for 1% of the time, Pallas kernels for 7%

profile of v9, /device:TPU:1, one launch (start us, length us, event | category | flops | bytes accessed | tf_op | source)
XLA Modules:
  0.0 61.8 jit_solution(8272835676311376030)
XLA Ops:
  0.0 0.0 copy-start.6
  0.0 1.3 %fusion = (bf16[2,2,128,512]{3,2,1,0:T(8,128)(2,1)S(1)}, bf16[2,2,128,512]{3,2,1,0:T(8,128)(2,1)S(1)}) fusion(s32[]{:T(128)S(6)} %select_n.15, bf16[1,2,128,1024]{3,2,1,0:T(8,128)(2,1)} %bitcast.11, bf16[1,2,128,1024]{3,2,1,0:T(8,128)(2,1)} %bitcast.12, s32[]{:T(128)S(6)} %select_n.14), kind=kLoop, calls=%fused_computation.5 | loop fusion | flops 2097152 | bytes 2097160 | tf_op jit(solution)/shard_map/stack | solution.py:252
  1.3 3.9 %collective-permute-start = (bf16[2,2,128,512]{3,2,1,0:T(8,128)(2,1)S(1)}, bf16[2,2,128,512]{3,2,1,0:T(8,128)(2,1)S(1)}, u32[]{:S(2)}, u32[]{:S(2)}) collective-permute-start(bf16[2,2,128,512]{3,2,1,0:T(8,128)(2,1)S(1)} %get-tuple-element.12.refs_0_), channel_id=1, source_target_pairs={{0,16},{16,0},{32,48},{48,32},{64,80},{80,64},{96,112},{112,96},{1... | collective-permute-start | bytes 1572872 | tf_op jit(solution)/shard_map/ppermute | solution.py:258
  5.3 8.4 %collective-permute-start.1 = (bf16[2,2,128,512]{3,2,1,0:T(8,128)(2,1)S(1)}, bf16[2,2,128,512]{3,2,1,0:T(8,128)(2,1)S(1)}, u32[]{:S(2)}, u32[]{:S(2)}) collective-permute-start(bf16[2,2,128,512]{3,2,1,0:T(8,128)(2,1)S(1)} %get-tuple-element.13.refs_0_), channel_id=1, source_target_pairs={{0,17},{1,16},{2,19},{3,18},{4,21},{5,20},{6,23},{7,22},{8,25},{9,... | collective-permute-start | bytes 1572872 | tf_op jit(solution)/shard_map/ppermute | solution.py:259
  13.7 0.0 copy-done.6
  13.7 0.1 multiply_convert_fusion.1
  13.8 0.1 reshape.7
  13.8 0.1 copy.11
  13.9 17.4 %all-gather.1 = f16[16,256,128]{2,1,0:T(8,128)(2,1)S(1)} all-gather(f16[1,256,128]{2,1,0:T(8,128)(2,1)S(1)} %bitcast.13), channel_id=1, replica_groups=mesh['req'=32,'prefix'=16] {'prefix'}, dimensions={0}, use_global_device_ids=true | all-gather | bytes 1114112 | tf_op jit(solution)/shard_map/all_gather | solution.py:263
  31.3 0.0 copy-start
  31.3 0.0 copy-start.1
  31.3 0.0 copy-start.2
  31.3 0.0 copy-start.3
  31.3 0.0 copy-start.4
  31.3 0.0 copy-start.5
  31.3 0.3 multiply_convert_fusion.q_ref
  31.6 0.8 %copy-done = bf16[384,1024]{1,0:T(8,128)(2,1)S(1)} copy-done((bf16[384,1024]{1,0:T(8,128)(2,1)S(1)}, bf16[384,1024]{1,0:T(8,128)(2,1)}, u32[]{:S(2)}) %copy-start) | copy-done | bytes 786456
  32.4 0.2 copy-done.1
  32.7 0.0 copy-done.2
  32.7 0.0 copy-done.3
  32.7 0.0 copy-done.4
  32.7 0.0 copy-done.5
  32.7 1.7 %attend_other.1 = f32[4,136,512]{2,1,0:T(8,128)S(1)} custom-call(bf16[16,256,128]{2,1,0:T(8,128)(2,1)S(1)} %multiply_convert_fusion.q_ref, bf16[384,1024]{1,0:T(8,128)(2,1)S(1)} %copy-done, bf16[384,1024]{1,0:T(8,128)(2,1)S(1)} %copy-done.1, bf16[2,2,1024]{2,1,0:T(2,128)(2,1)S(1)} %copy-done.3, bf16[2,2,1024]{2,1,0:T(2,128)(2,1)S(1)} %copy-done.4, ...), custom_call_target="tpu_custom_call" | custom-call | flops 800000000 | bytes 6000000 | tf_op jit(solution)/shard_map/attend_other/pallas_call | solution.py:269
  34.4 0.0 collective-permute-done.refs_1_
  34.4 0.0 collective-permute-done.1.refs_2_
  34.4 2.1 %collective-permute-start.2 = (f32[4,136,512]{2,1,0:T(8,128)S(1)}, f32[4,136,512]{2,1,0:T(8,128)S(1)}, u32[]{:S(2)}, u32[]{:S(2)}) collective-permute-start(f32[4,136,512]{2,1,0:T(8,128)S(1)} %attend_other.1), channel_id=1, source_target_pairs={{0,1},{1,0},{2,3},{3,2},{4,5},{5,4},{6,7},{7,6},{8,9},{9,8},{10,11... | collective-permute-start | bytes 3342344 | tf_op jit(solution)/shard_map/ppermute | solution.py:284
  36.5 2.4 %attend_own.1.a_ref = f32[4,136,512]{2,1,0:T(8,128)S(1)} custom-call(bf16[16,256,128]{2,1,0:T(8,128)(2,1)S(1)} %multiply_convert_fusion.q_ref, bf16[384,1024]{1,0:T(8,128)(2,1)S(1)} %copy-done, bf16[384,1024]{1,0:T(8,128)(2,1)S(1)} %copy-done.1, bf16[2,2,1024]{2,1,0:T(2,128)(2,1)S(1)} %copy-done.3, bf16[2,2,1024]{2,1,0:T(2,128)(2,1)S(1)} %copy-done.4, ...), custom_call_target="tpu_custom_call" | custom-call | flops 800000000 | bytes 6000000 | tf_op jit(solution)/shard_map/attend_own/pallas_call | solution.py:269
  38.8 0.2 collective-permute-done.2.b_ref
  39.0 0.4 core_merge.1
  39.4 0.1 convert_element_type.22
  39.5 21.0 %all_to_all.5 = f16[16,136,128]{2,1,0:T(8,128)(2,1)S(1)} all-to-all(f16[16,136,128]{2,1,0:T(8,128)(2,1)S(1)} %convert_element_type.22), channel_id=1, replica_groups=mesh['req'=32,'prefix'=16] {'prefix'}, dimensions={0} | all-to-all | bytes 1114112 | tf_op jit(solution)/shard_map/all_to_all | solution.py:289
  60.5 0.1 convert_element_type.23.z_ref
  60.6 1.2 %final.1 = bf16[2,2,8192]{2,1,0:T(2,128)(2,1)} custom-call(f32[16,136,128]{2,1,0:T(8,128)S(1)} %convert_element_type.23.z_ref), custom_call_target="tpu_custom_call" | custom-call | bytes 1000000 | tf_op jit(solution)/shard_map/final/pallas_call | solution.py:290
Async XLA Ops:
  0.0 13.7 %copy-start.6 = (bf16[2,2,8192]{2,1,0:T(2,128)(2,1)S(1)}, bf16[2,2,8192]{2,1,0:T(2,128)(2,1)}, u32[]{:S(2)}) copy-start(bf16[2,2,8192]{2,1,0:T(2,128)(2,1)} %param.9) | copy-start | bytes 196612
  1.3 33.0 %collective-permute-start = (bf16[2,2,128,512]{3,2,1,0:T(8,128)(2,1)S(1)}, bf16[2,2,128,512]{3,2,1,0:T(8,128)(2,1)S(1)}, u32[]{:S(2)}, u32[]{:S(2)}) collective-permute-start(bf16[2,2,128,512]{3,2,1,0:T(8,128)(2,1)S(1)} %get-tuple-element.12.refs_0_), channel_id=1, source_target_pairs={{0,16},{16,0},{32,48},{48,32},{64,80},{80,64},{96,112},{112,96},{1... | collective-permute-start | bytes 1572872 | tf_op jit(solution)/shard_map/ppermute | solution.py:258
  5.3 29.1 %collective-permute-start.1 = (bf16[2,2,128,512]{3,2,1,0:T(8,128)(2,1)S(1)}, bf16[2,2,128,512]{3,2,1,0:T(8,128)(2,1)S(1)}, u32[]{:S(2)}, u32[]{:S(2)}) collective-permute-start(bf16[2,2,128,512]{3,2,1,0:T(8,128)(2,1)S(1)} %get-tuple-element.13.refs_0_), channel_id=1, source_target_pairs={{0,17},{1,16},{2,19},{3,18},{4,21},{5,20},{6,23},{7,22},{8,25},{9,... | collective-permute-start | bytes 1572872 | tf_op jit(solution)/shard_map/ppermute | solution.py:259
  31.3 1.1 %copy-start = (bf16[384,1024]{1,0:T(8,128)(2,1)S(1)}, bf16[384,1024]{1,0:T(8,128)(2,1)}, u32[]{:S(2)}) copy-start(bf16[384,1024]{1,0:T(8,128)(2,1)} %pk_ref.3) | copy-start | bytes 2359300
  31.3 1.4 %copy-start.1 = (bf16[384,1024]{1,0:T(8,128)(2,1)S(1)}, bf16[384,1024]{1,0:T(8,128)(2,1)}, u32[]{:S(2)}) copy-start(bf16[384,1024]{1,0:T(8,128)(2,1)} %pv_ref.3) | copy-start | bytes 2359300
  31.3 1.4 %copy-start.2 = (s32[1024,16]{0,1:T(8,128)S(1)}, s32[1024,16]{0,1:T(8,128)}, u32[]{:S(2)}) copy-start(s32[1024,16]{0,1:T(8,128)} %param.16) | copy-start | bytes 196612
  31.3 1.4 %copy-start.3 = (bf16[2,2,1024]{2,1,0:T(2,128)(2,1)S(1)}, bf16[2,2,1024]{2,1,0:T(2,128)(2,1)}, u32[]{:S(2)}) copy-start(bf16[2,2,1024]{2,1,0:T(2,128)(2,1)} %nk_ref.3) | copy-start | bytes 24580
  31.3 1.4 %copy-start.4 = (bf16[2,2,1024]{2,1,0:T(2,128)(2,1)S(1)}, bf16[2,2,1024]{2,1,0:T(2,128)(2,1)}, u32[]{:S(2)}) copy-start(bf16[2,2,1024]{2,1,0:T(2,128)(2,1)} %nv_ref.3) | copy-start | bytes 24580
  31.3 1.4 %copy-start.5 = (s32[1024]{0:T(1024)S(1)}, s32[1024]{0:T(1024)}, u32[]{:S(2)}) copy-start(s32[1024]{0:T(1024)} %param.17) | copy-start | bytes 12292
  34.4 4.6 %collective-permute-start.2 = (f32[4,136,512]{2,1,0:T(8,128)S(1)}, f32[4,136,512]{2,1,0:T(8,128)S(1)}, u32[]{:S(2)}, u32[]{:S(2)}) collective-permute-start(f32[4,136,512]{2,1,0:T(8,128)S(1)} %attend_other.1), channel_id=1, source_target_pairs={{0,1},{1,0},{2,3},{3,2},{4,5},{5,4},{6,7},{7,6},{8,9},{9,8},{10,11... | collective-permute-start | bytes 3342344 | tf_op jit(solution)/shard_map/ppermute | solution.py:284

commit v10 on v9

--- a/solution.py
+++ b/solution.py
@@ -193,10 +193,11 @@
         out_ref[dev, 128:136, :] = parts[:, dev // 4 * DH : (dev // 4 + 1) * DH]
 
 
-def final_kernel(z_ref, out_ref, w_s):
+def final_kernel(z_ref, out_ref, w_s, o_s, sems):
     n_dev = z_ref.shape[0]
     pre = lax.axis_index("prefix")
     mine = pl.ds(pl.multiple_of(pre % 4 * 32, 32), 32)
+    copies = []
     for c in range(2):
         lses = []
         for src in range(c, n_dev, 2):
@@ -214,10 +215,15 @@
             for y, src in enumerate(range(c, n_dev, 2)):
                 o = o + z_ref[src, i * 32 : (i + 1) * 32, :] * columns[:, y * 4 + i : y * 4 + i + 1]
             for g in range(GROUP):
-                head = (c * HALF + i) * GROUP + g
+                head = i * GROUP + g
                 for s in range(2):
                     r = g * 4 + s * 2
-                    out_ref[s, :, head * DH : (head + 1) * DH] = o[r : r + 2, :].astype(bf16)
+                    o_s[c, s, :, head * DH : (head + 1) * DH] = o[r : r + 2, :].astype(bf16)
+        wide = o_s.shape[3]
+        copies.append(pltpu.make_async_copy(o_s.at[c], out_ref.at[:, :, c * wide : (c + 1) * wide], sems.at[c]))
+        copies[c].start()
+    for copy in copies:
+        copy.wait()
 
 
 def call(kernel, out_shape, ins, out_specs=VM, scratch=(), flops=0, moved=0, name=None):
@@ -291,8 +297,12 @@
         final_kernel,
         sds((2, 2, H * DH), bf16),
         [VM],
-        VM,
-        [pltpu.VMEM((2, DH, DH), f32)],
+        pl.BlockSpec(memory_space=pl.ANY),
+        [
+            pltpu.VMEM((2, DH, DH), f32),
+            pltpu.VMEM((2, 2, 2, H * DH // 2), bf16),
+            pltpu.SemaphoreType.DMA((2,)),
+        ],
         moved=1_000_000,
         name="final",
     )(spread.astype(f32))

time: 62 us -> 62.1 us (level)
  transfers between devices with their start and end apart: 3 -> 3, of which waited for: 1 -> 1; matrix products, arithmetic and copies ran while one was open for 1% -> 1% of each run, Pallas kernels for 7% -> 6%
where the time goes in v10:
time: 62.1 us; the launch traced here: 61.8 us
  blocking collectives  38.5 us (62%)
  starting transfers between devices  14.4 us (23%)
  Pallas kernels  5.57 us (9%)
  other arithmetic  1.82 us (3%)
  local copies, waits for them, and re-layouts  1.2 us (2%)
    all_to_all x1, blocking collectives, per_device(): lax.all_to_all(merged.astype(jnp.float16), 'prefix', 0, 0, tiled=True)  21 us
    all_gather x1, blocking collectives, per_device(): group = lax.all_gather(own, 'prefix', axis=0)  17.4 us
    ppermute x1, starting transfers between devices, per_device(): far_cross = lax.ppermute(pool_cross, ('req', 'prefix'), across)  8.38 us
    pallas_call x2, Pallas kernels, attend(): call(functools.partial(attend_kernel, flip), sds((HALF, 136, rows), f32),...  4.02 us
    ppermute x1, starting transfers between devices, per_device(): far_same = lax.ppermute(pool_same, 'req', swap)  3.95 us
    ppermute x1, starting transfers between devices, per_device(): theirs = lax.ppermute(other, 'prefix', core)  2.07 us
    another operation x1, other arithmetic, per_device(): pool = jnp.stack([pool_keys, pool_values])  1.32 us
  transfers between devices with their start and end apart: 3, of which 1 were waited for; matrix products, arithmetic and copies ran while one was open for 1% of the time, Pallas kernels for 6%

profile of v10, /device:TPU:1, one launch (start us, length us, event | category | flops | bytes accessed | tf_op | source)
XLA Modules:
  0.0 61.8 jit_solution(7699511014480278330)
XLA Ops:
  0.0 0.0 copy-start.6
  0.0 1.3 %fusion = (bf16[2,2,128,512]{3,2,1,0:T(8,128)(2,1)S(1)}, bf16[2,2,128,512]{3,2,1,0:T(8,128)(2,1)S(1)}) fusion(s32[]{:T(128)S(6)} %select_n.15, bf16[1,2,128,1024]{3,2,1,0:T(8,128)(2,1)} %bitcast.11, bf16[1,2,128,1024]{3,2,1,0:T(8,128)(2,1)} %bitcast.12, s32[]{:T(128)S(6)} %select_n.14), kind=kLoop, calls=%fused_computation.5 | loop fusion | flops 2097152 | bytes 2097160 | tf_op jit(solution)/shard_map/stack | solution.py:258
  1.3 3.9 %collective-permute-start = (bf16[2,2,128,512]{3,2,1,0:T(8,128)(2,1)S(1)}, bf16[2,2,128,512]{3,2,1,0:T(8,128)(2,1)S(1)}, u32[]{:S(2)}, u32[]{:S(2)}) collective-permute-start(bf16[2,2,128,512]{3,2,1,0:T(8,128)(2,1)S(1)} %get-tuple-element.12.refs_0_), channel_id=1, source_target_pairs={{0,16},{16,0},{32,48},{48,32},{64,80},{80,64},{96,112},{112,96},{1... | collective-permute-start | bytes 1572872 | tf_op jit(solution)/shard_map/ppermute | solution.py:264
  5.3 8.4 %collective-permute-start.1 = (bf16[2,2,128,512]{3,2,1,0:T(8,128)(2,1)S(1)}, bf16[2,2,128,512]{3,2,1,0:T(8,128)(2,1)S(1)}, u32[]{:S(2)}, u32[]{:S(2)}) collective-permute-start(bf16[2,2,128,512]{3,2,1,0:T(8,128)(2,1)S(1)} %get-tuple-element.13.refs_0_), channel_id=1, source_target_pairs={{0,17},{1,16},{2,19},{3,18},{4,21},{5,20},{6,23},{7,22},{8,25},{9,... | collective-permute-start | bytes 1572872 | tf_op jit(solution)/shard_map/ppermute | solution.py:265
  13.7 0.0 copy-done.6
  13.7 0.1 multiply_convert_fusion.1
  13.8 0.1 reshape.7
  13.8 0.1 copy.11
  13.9 17.4 %all-gather.1 = f16[16,256,128]{2,1,0:T(8,128)(2,1)S(1)} all-gather(f16[1,256,128]{2,1,0:T(8,128)(2,1)S(1)} %bitcast.13), channel_id=1, replica_groups=mesh['req'=32,'prefix'=16] {'prefix'}, dimensions={0}, use_global_device_ids=true | all-gather | bytes 1114112 | tf_op jit(solution)/shard_map/all_gather | solution.py:269
  31.3 0.0 copy-start
  31.3 0.0 copy-start.1
  31.3 0.0 copy-start.2
  31.3 0.0 copy-start.3
  31.3 0.0 copy-start.4
  31.3 0.0 copy-start.5
  31.3 0.3 multiply_convert_fusion.q_ref
  31.6 0.8 %copy-done = bf16[384,1024]{1,0:T(8,128)(2,1)S(1)} copy-done((bf16[384,1024]{1,0:T(8,128)(2,1)S(1)}, bf16[384,1024]{1,0:T(8,128)(2,1)}, u32[]{:S(2)}) %copy-start) | copy-done | bytes 786456
  32.4 0.2 copy-done.1
  32.7 0.0 copy-done.2
  32.7 0.0 copy-done.3
  32.7 0.0 copy-done.4
  32.7 0.0 copy-done.5
  32.7 1.7 %attend_other.1 = f32[4,136,512]{2,1,0:T(8,128)S(1)} custom-call(bf16[16,256,128]{2,1,0:T(8,128)(2,1)S(1)} %multiply_convert_fusion.q_ref, bf16[384,1024]{1,0:T(8,128)(2,1)S(1)} %copy-done, bf16[384,1024]{1,0:T(8,128)(2,1)S(1)} %copy-done.1, bf16[2,2,1024]{2,1,0:T(2,128)(2,1)S(1)} %copy-done.3, bf16[2,2,1024]{2,1,0:T(2,128)(2,1)S(1)} %copy-done.4, ...), custom_call_target="tpu_custom_call" | custom-call | flops 800000000 | bytes 6000000 | tf_op jit(solution)/shard_map/attend_other/pallas_call | solution.py:275
  34.4 0.0 collective-permute-done.refs_1_
  34.4 0.0 collective-permute-done.1.refs_2_
  34.4 2.1 %collective-permute-start.2 = (f32[4,136,512]{2,1,0:T(8,128)S(1)}, f32[4,136,512]{2,1,0:T(8,128)S(1)}, u32[]{:S(2)}, u32[]{:S(2)}) collective-permute-start(f32[4,136,512]{2,1,0:T(8,128)S(1)} %attend_other.1), channel_id=1, source_target_pairs={{0,1},{1,0},{2,3},{3,2},{4,5},{5,4},{6,7},{7,6},{8,9},{9,8},{10,11... | collective-permute-start | bytes 3342344 | tf_op jit(solution)/shard_map/ppermute | solution.py:290
  36.5 2.3 %attend_own.1.a_ref = f32[4,136,512]{2,1,0:T(8,128)S(1)} custom-call(bf16[16,256,128]{2,1,0:T(8,128)(2,1)S(1)} %multiply_convert_fusion.q_ref, bf16[384,1024]{1,0:T(8,128)(2,1)S(1)} %copy-done, bf16[384,1024]{1,0:T(8,128)(2,1)S(1)} %copy-done.1, bf16[2,2,1024]{2,1,0:T(2,128)(2,1)S(1)} %copy-done.3, bf16[2,2,1024]{2,1,0:T(2,128)(2,1)S(1)} %copy-done.4, ...), custom_call_target="tpu_custom_call" | custom-call | flops 800000000 | bytes 6000000 | tf_op jit(solution)/shard_map/attend_own/pallas_call | solution.py:275
  38.8 0.2 collective-permute-done.2.b_ref
  39.0 0.4 core_merge.1
  39.4 0.1 convert_element_type.22
  39.5 21.0 %all_to_all.5 = f16[16,136,128]{2,1,0:T(8,128)(2,1)S(1)} all-to-all(f16[16,136,128]{2,1,0:T(8,128)(2,1)S(1)} %convert_element_type.22), channel_id=1, replica_groups=mesh['req'=32,'prefix'=16] {'prefix'}, dimensions={0} | all-to-all | bytes 1114112 | tf_op jit(solution)/shard_map/all_to_all | solution.py:295
  60.5 0.1 convert_element_type.23.z_ref
  60.6 1.2 %final.1 = bf16[2,2,8192]{2,1,0:T(2,128)(2,1)} custom-call(f32[16,136,128]{2,1,0:T(8,128)S(1)} %convert_element_type.23.z_ref), custom_call_target="tpu_custom_call" | custom-call | bytes 1000000 | tf_op jit(solution)/shard_map/final/pallas_call | solution.py:296
Async XLA Ops:
  0.0 13.7 %copy-start.6 = (bf16[2,2,8192]{2,1,0:T(2,128)(2,1)S(1)}, bf16[2,2,8192]{2,1,0:T(2,128)(2,1)}, u32[]{:S(2)}) copy-start(bf16[2,2,8192]{2,1,0:T(2,128)(2,1)} %param.9) | copy-start | bytes 196612
  1.3 33.0 %collective-permute-start = (bf16[2,2,128,512]{3,2,1,0:T(8,128)(2,1)S(1)}, bf16[2,2,128,512]{3,2,1,0:T(8,128)(2,1)S(1)}, u32[]{:S(2)}, u32[]{:S(2)}) collective-permute-start(bf16[2,2,128,512]{3,2,1,0:T(8,128)(2,1)S(1)} %get-tuple-element.12.refs_0_), channel_id=1, source_target_pairs={{0,16},{16,0},{32,48},{48,32},{64,80},{80,64},{96,112},{112,96},{1... | collective-permute-start | bytes 1572872 | tf_op jit(solution)/shard_map/ppermute | solution.py:264
  5.3 29.1 %collective-permute-start.1 = (bf16[2,2,128,512]{3,2,1,0:T(8,128)(2,1)S(1)}, bf16[2,2,128,512]{3,2,1,0:T(8,128)(2,1)S(1)}, u32[]{:S(2)}, u32[]{:S(2)}) collective-permute-start(bf16[2,2,128,512]{3,2,1,0:T(8,128)(2,1)S(1)} %get-tuple-element.13.refs_0_), channel_id=1, source_target_pairs={{0,17},{1,16},{2,19},{3,18},{4,21},{5,20},{6,23},{7,22},{8,25},{9,... | collective-permute-start | bytes 1572872 | tf_op jit(solution)/shard_map/ppermute | solution.py:265
  31.3 1.1 %copy-start = (bf16[384,1024]{1,0:T(8,128)(2,1)S(1)}, bf16[384,1024]{1,0:T(8,128)(2,1)}, u32[]{:S(2)}) copy-start(bf16[384,1024]{1,0:T(8,128)(2,1)} %pk_ref.3) | copy-start | bytes 2359300
  31.3 1.4 %copy-start.1 = (bf16[384,1024]{1,0:T(8,128)(2,1)S(1)}, bf16[384,1024]{1,0:T(8,128)(2,1)}, u32[]{:S(2)}) copy-start(bf16[384,1024]{1,0:T(8,128)(2,1)} %pv_ref.3) | copy-start | bytes 2359300
  31.3 1.4 %copy-start.2 = (s32[1024,16]{0,1:T(8,128)S(1)}, s32[1024,16]{0,1:T(8,128)}, u32[]{:S(2)}) copy-start(s32[1024,16]{0,1:T(8,128)} %param.16) | copy-start | bytes 196612
  31.3 1.4 %copy-start.3 = (bf16[2,2,1024]{2,1,0:T(2,128)(2,1)S(1)}, bf16[2,2,1024]{2,1,0:T(2,128)(2,1)}, u32[]{:S(2)}) copy-start(bf16[2,2,1024]{2,1,0:T(2,128)(2,1)} %nk_ref.3) | copy-start | bytes 24580
  31.3 1.4 %copy-start.4 = (bf16[2,2,1024]{2,1,0:T(2,128)(2,1)S(1)}, bf16[2,2,1024]{2,1,0:T(2,128)(2,1)}, u32[]{:S(2)}) copy-start(bf16[2,2,1024]{2,1,0:T(2,128)(2,1)} %nv_ref.3) | copy-start | bytes 24580
  31.3 1.4 %copy-start.5 = (s32[1024]{0:T(1024)S(1)}, s32[1024]{0:T(1024)}, u32[]{:S(2)}) copy-start(s32[1024]{0:T(1024)} %param.17) | copy-start | bytes 12292
  34.4 4.6 %collective-permute-start.2 = (f32[4,136,512]{2,1,0:T(8,128)S(1)}, f32[4,136,512]{2,1,0:T(8,128)S(1)}, u32[]{:S(2)}, u32[]{:S(2)}) collective-permute-start(f32[4,136,512]{2,1,0:T(8,128)S(1)} %attend_other.1), channel_id=1, source_target_pairs={{0,1},{1,0},{2,3},{3,2},{4,5},{5,4},{6,7},{7,6},{8,9},{9,8},{10,11... | collective-permute-start | bytes 3342344 | tf_op jit(solution)/shard_map/ppermute | solution.py:290
